TPU v7x, 128 devices: a whole 4x4x4 slice. The times are simulated.
128 devices in a mesh: gy: 8 (over z, core), gz: 16 (over y, x).
Axes of the slice: x: 4, y: 4, z: 4, core: 2. Of those that a mesh axis runs over, the one named last changes fastest.
Arguments:
- populations: float32 [19, 4, 256, 2048], P(None, None, 'gy', 'gz'), may hold values from 0.5 to 1.5
- solid_mask: int32 [4, 256, 2048], P(None, 'gy', 'gz'), may hold values from 0 to 1, as said below
- centers: int32 [3, 512], P(None, ('gy', 'gz')), may hold values from 0 to 2047, as said below
- tile_lists: int32 [2048, 4], P(('gy', 'gz')), may hold values from -15 to 126, as said below
- sphere_state: float32 [8, 512], P(None, ('gy', 'gz')), may hold values from -0.2 to 2.5, as said below
- destination: int32 [512], P(('gy', 'gz')), may hold values from 0 to 511, as said below
- relax_rates: float32 [19], replicated, may hold values from 0.6 to 1.9
Outputs:
- populations_next: float32 [19, 4, 256, 2048], P(None, None, 'gy', 'gz')
- forces: float32 [6, 512], P(None, ('gy', 'gz'))
- state_next: float32 [8, 512], P(None, ('gy', 'gz'))
Inputs may be any that keep to these rules, and one draw needn't show every extreme that they name: `solid_mask`: 1 marks a solid cell, 0 a fluid one; every cell within distance 6 of a sphere's center (wrapping in y and z) is solid. `centers`: row 0 is x, rows 1 and 2 are global y and z. Sphere g belongs to device g // 4 (devices numbered with gz fastest), whose 32 rows and 128 columns contain its y and z; x lies from 0 to 3. Of one device's spheres at most 2 have local y below 7, at most 2 have local y at least 25, and likewise in z with 128; each of these four counts is exactly 2 on some device. `tile_lists`: A device's 8 * 2 rows form 8 blocks of 2 rows, one for each offset (dy, dz) in the order (-1,-1), (-1,0), (-1,1), (0,-1), (0,1), (1,-1), (1,0), (1,1), offsets wrapping. Block (dy, dz) names, in rising slot order, exactly those spheres of the device at that offset whose local y is below 7 if dy = 1 or at least 25 if dy = -1, and likewise in z for dz; columns: the sphere's slot on its device, the tile's first row and column in this device's local coordinates (center minus 16 / 2 plus dy * 32 and dz * 128), the center's x. Unused rows are -1, 0, 0, 0 and come last in a block. `sphere_state`: rows 0 to 2 a sphere's velocity and rows 3 to 5 its angular velocity, each from -0.2 to 0.2; row 6 the fluid density over the sphere's density, from 0.125 to 0.67; row 7 the reciprocal of the sphere's gyration factor k (moment of inertia k m * 6^2), from 1.5 to 2.5. `destination`: A permutation of the sphere slots; each sphere's new slot lies on its own device or on one of the 8 devices whose gy and gz indices differ by -1, 0 or 1, with wrap.
All inputs are finite; a program needn't handle non-finite values.
Results may differ from a plain program's by a relative error of at most 0.0003.
Values sent between devices are 32-bit elements; how exact they have to be, the bound alone decides.
No kernel may reach another device: no remote copies, remote signals or barrier semaphores. Data moves between devices by JAX's collectives and lax.ppermute only.
A program may use at most 128 MiB of HBM per device.

v0:
```python
import math

import jax
import jax.numpy as jnp
import numpy as np
from jax import lax
from jax.experimental import pallas as pl
from jax.experimental.pallas import tpu as pltpu
from jax.sharding import PartitionSpec as P

TILE = 16
RADIUS = 6
PLANES = 4
ROWS = 32
COLS = 128
SLOTS = 4
GROUPS = PLANES * ROWS // 8

VELOCITIES = (
    (0, 0, 0),
    (1, 0, 0),
    (-1, 0, 0),
    (0, 1, 0),
    (0, -1, 0),
    (0, 0, 1),
    (0, 0, -1),
    (1, 1, 0),
    (-1, -1, 0),
    (1, -1, 0),
    (-1, 1, 0),
    (1, 0, 1),
    (-1, 0, -1),
    (1, 0, -1),
    (-1, 0, 1),
    (0, 1, 1),
    (0, -1, -1),
    (0, 1, -1),
    (0, -1, 1),
)
OPPOSITE = (0, 2, 1, 4, 3, 6, 5, 8, 7, 10, 9, 12, 11, 14, 13, 16, 15, 18, 17)
EXPONENTS = (
    (0, 0, 0),
    (1, 0, 0),
    (0, 1, 0),
    (0, 0, 1),
    (2, 0, 0),
    (0, 2, 0),
    (0, 0, 2),
    (1, 1, 0),
    (1, 0, 1),
    (0, 1, 1),
    (1, 2, 0),
    (1, 0, 2),
    (2, 1, 0),
    (0, 1, 2),
    (2, 0, 1),
    (0, 2, 1),
    (2, 2, 0),
    (2, 0, 2),
    (0, 2, 2),
)
DIRECTIONS = ((-1, -1), (-1, 0), (-1, 1), (0, -1), (0, 1), (1, -1), (1, 0), (1, 1))

Z_UP = (5, 11, 14, 15, 18)
Z_DOWN = (6, 12, 13, 16, 17)
Y_UP = (3, 7, 10, 15, 17)
Y_DOWN = (4, 8, 9, 16, 18)
CLASS_MEMBER = (0, 1, 3, 5, 7, 11, 15)
EVEN_MOMENTS = (0, 4, 5, 6, 16, 17, 18)
ODD_MOMENTS = ((1, 10, 11), (2, 12, 13), (3, 14, 15))
ODD_CLASSES = ((1, 4, 5), (2, 4, 6), (3, 5, 6))
CROSS_MOMENTS = (7, 8, 9)
STATE_LANE = 64
DEST_LANE = 96
EDGE_ROWS = 24


def moment_basis():
    velocity = np.array(VELOCITIES, dtype=np.float64)
    moment_rows = []
    for a, b, e in EXPONENTS:
        vector = velocity[:, 0] ** a * velocity[:, 1] ** b * velocity[:, 2] ** e
        for earlier in moment_rows:
            vector = vector - np.dot(earlier, vector) * earlier
        moment_rows.append(vector / np.sqrt(np.dot(vector, vector)))
    return np.array(moment_rows)


BASIS = moment_basis()


def store_coefficients(rates, coef):
    splat = [jnp.full((8, COLS), rates[k], jnp.float32) for k in range(19)]
    at = 0
    for a in range(7):
        for b in range(a, 7):
            total = None
            for k in EVEN_MOMENTS:
                c = float(BASIS[k, CLASS_MEMBER[a]] * BASIS[k, CLASS_MEMBER[b]])
                if abs(c) > 1e-12:
                    total = c * splat[k] if total is None else total + c * splat[k]
            coef[at] = total
            at += 1
    for axis in range(3):
        for a in range(3):
            for b in range(a, 3):
                total = None
                for k in ODD_MOMENTS[axis]:
                    c = float(
                        BASIS[k, CLASS_MEMBER[ODD_CLASSES[axis][a]]]
                        * BASIS[k, CLASS_MEMBER[ODD_CLASSES[axis][b]]]
                    )
                    if abs(c) > 1e-12:
                        total = c * splat[k] if total is None else total + c * splat[k]
                coef[at] = total
                at += 1
    for axis in range(3):
        c = float(BASIS[CROSS_MOMENTS[axis], CLASS_MEMBER[4 + axis]] ** 2)
        coef[at] = c * splat[CROSS_MOMENTS[axis]]
        at += 1


N_COEF = 28 + 18 + 3


def collide(f, coef):
    even_at = {}
    at = 0
    for a in range(7):
        for b in range(a, 7):
            even_at[a, b] = even_at[b, a] = at
            at += 1
    odd_at = []
    for _ in range(3):
        table = {}
        for a in range(3):
            for b in range(a, 3):
                table[a, b] = table[b, a] = at
                at += 1
        odd_at.append(table)
    cross_at = at

    def split(i):
        ab, amb = f[i] + f[i + 1], f[i] - f[i + 1]
        cd, cmd = f[i + 2] + f[i + 3], f[i + 2] - f[i + 3]
        return ab + cd, ab - cd, amb + cmd, amb - cmd

    s_xy, q_xy, xy_x, xy_y = split(7)
    s_xz, q_xz, xz_x, xz_z = split(11)
    s_yz, q_yz, yz_y, yz_z = split(15)
    s_x, s_y, s_z = f[1] + f[2], f[3] + f[4], f[5] + f[6]
    d_x, d_y, d_z = f[1] - f[2], f[3] - f[4], f[5] - f[6]
    rho = ((f[0] + s_x) + (s_y + s_z)) + ((s_xy + s_xz) + s_yz)
    j_x = d_x + (xy_x + xz_x)
    j_y = d_y + (xy_y + yz_y)
    j_z = d_z + (xz_z + yz_z)
    inverse = 1.0 / rho
    u_x, u_y, u_z = j_x * inverse, j_y * inverse, j_z * inverse
    e_x, e_y, e_z = j_x * u_x, j_y * u_y, j_z * u_z
    base = (rho - 1.5 * ((e_x + e_y) + e_z)) * (1.0 / 9.0)
    h_x, h_y, h_z = 0.5 * e_x, 0.5 * e_y, 0.5 * e_z
    even = (
        f[0] - 3.0 * base,
        s_x - (base + h_x),
        s_y - (base + h_y),
        s_z - (base + h_z),
        s_xy - (base + (h_x + h_y)),
        s_xz - (base + (h_x + h_z)),
        s_yz - (base + (h_y + h_z)),
    )
    third = 1.0 / 3.0
    t_x, t_y, t_z = third * j_x, third * j_y, third * j_z
    odd = (
        (d_x - t_x, xy_x - t_x, xz_x - t_x),
        (d_y - t_y, xy_y - t_y, yz_y - t_y),
        (d_z - t_z, xz_z - t_z, yz_z - t_z),
    )
    cross = (
        (q_xy - j_x * u_y) * coef[cross_at],
        (q_xz - j_x * u_z) * coef[cross_at + 1],
        (q_yz - j_y * u_z) * coef[cross_at + 2],
    )

    def apply(vector, table, n):
        out = []
        for a in range(n):
            terms = [coef[table[a, b]] * vector[b] for b in range(n)]
            while len(terms) > 1:
                terms = [
                    terms[i] + terms[i + 1] if i + 1 < len(terms) else terms[i]
                    for i in range(0, len(terms), 2)
                ]
            out.append(terms[0])
        return out

    ev = apply(even, even_at, 7)
    ox, oy, oz = (apply(odd[axis], odd_at[axis], 3) for axis in range(3))
    new = [f[0] - ev[0]]
    for axis, o in enumerate((ox, oy, oz)):
        i = 1 + 2 * axis
        new += [f[i] - (ev[1 + axis] + o[0]), f[i + 1] - (ev[1 + axis] - o[0])]
    for axis, (a, b) in enumerate(((ox[1], oy[1]), (ox[2], oz[1]), (oy[2], oz[2]))):
        i = 7 + 4 * axis
        plus, minus = ev[4 + axis] + cross[axis], ev[4 + axis] - cross[axis]
        both, differ = a + b, a - b
        new += [
            f[i] - (plus + both),
            f[i + 1] - (plus - both),
            f[i + 2] - (minus + differ),
            f[i + 3] - (minus - differ),
        ]
    return new


def sphere_partial(coll, center_x, center_y, center_z, row_f, lane_f):
    first = jnp.maximum(lax.shift_right_arithmetic(center_y - (RADIUS + 1), 3), 0)
    last = jnp.minimum(lax.shift_right_arithmetic(center_y + (RADIUS + 1), 3), ROWS // 8 - 1)
    x_f = center_x.astype(jnp.float32)
    r_z = lane_f - center_z.astype(jnp.float32)
    z_sq = r_z * r_z
    zero = jnp.zeros((8, COLS), jnp.float32)

    def row_tile(tile, carry):
        f_x, f_y, f_z, t_x, t_y, t_z = carry
        r_y = row_f + (tile * 8 - center_y).astype(jnp.float32)
        yz_sq = r_y * r_y + z_sq
        p_x, p_y, p_z, x_py, x_pz = zero, zero, zero, zero, zero
        y_plus_z, y_minus_z = r_y + r_z, r_y - r_z
        for t in range(PLANES):
            r_x = t - x_f
            dist = yz_sq + r_x * r_x
            outside = dist > float(RADIUS * RADIUS)
            half = jnp.where(outside, (RADIUS * RADIUS - 1.0) * 0.5 - 0.5 * dist, -1e9)
            half_2 = half - 0.5

            def linked(i, along, limit):
                up, down = VELOCITIES[i][0], VELOCITIES[i + 1][0]
                total = None
                if 0 <= t + up < PLANES:
                    total = jnp.where(along <= limit, coll[i, t * 4 + tile], 0.0)
                if 0 <= t + down < PLANES:
                    back = jnp.where(-along <= limit, coll[i + 1, t * 4 + tile], 0.0)
                    total = -back if total is None else total - back
                return total

            l_x = linked(1, r_x, half)
            l_y = linked(3, r_y, half)
            l_z = linked(5, r_z, half)
            l_xy = linked(7, r_y + r_x, half_2)
            l_xmy = linked(9, r_x - r_y, half_2)
            l_xz = linked(11, r_z + r_x, half_2)
            l_xmz = linked(13, r_x - r_z, half_2)
            l_yz = linked(15, y_plus_z, half_2)
            l_ymz = linked(17, y_minus_z, half_2)
            m_x = l_x + ((l_xy + l_xmy) + (l_xz + l_xmz))
            m_y = l_y + ((l_xy - l_xmy) + (l_yz + l_ymz))
            m_z = l_z + ((l_xz - l_xmz) + (l_yz - l_ymz))
            p_x, p_y, p_z = p_x + m_x, p_y + m_y, p_z + m_z
            x_py, x_pz = x_py + r_x * m_y, x_pz + r_x * m_z
        return (
            f_x + p_x,
            f_y + p_y,
            f_z + p_z,
            t_x + (r_y * p_z - r_z * p_y),
            t_y + (r_z * p_x - x_pz),
            t_z + (x_py - r_y * p_x),
        )

    sums = lax.fori_loop(first, last + 1, row_tile, (zero,) * 6)
    packed = zero
    for j in range(6):
        packed = jnp.where(row_f == float(j), jnp.sum(sums[j], axis=0, keepdims=True), packed)
    return packed


def collide_kernel(
    pops,
    mask,
    state,
    centers,
    lists,
    destination,
    rates,
    held,
    up_z,
    down_z,
    info,
    up_y,
    down_y,
    coll,
    coef,
    turn,
    partial,
):
    lane = lax.broadcasted_iota(jnp.int32, (8, COLS), 1)
    lane_f = lane.astype(jnp.float32)
    row_f = lax.broadcasted_iota(jnp.int32, (8, COLS), 0).astype(jnp.float32)
    store_coefficients(rates, coef)

    def group(g, _):
        f = [pops[i, g] for i in range(19)]
        solid = mask[g] > 0
        flag = solid.astype(jnp.float32)
        new = collide(f, coef)
        edge = jnp.zeros((8, COLS), jnp.float32)
        for i in range(19):
            coll[i, g] = new[i]
            held[i, g] = jnp.where(solid, f[i], new[i])
        for k, values in enumerate([new[i] for i in Z_UP] + [flag]):
            edge = jnp.where(lane == k, pltpu.roll(values, k + 1, 1), edge)
        for k, values in enumerate([new[i] for i in Z_DOWN] + [flag]):
            edge = jnp.where(lane == 8 + k, pltpu.roll(values, 8 + k, 1), edge)
        turn[pl.ds(pl.multiple_of(g * 8, 8), 8), :] = edge
        return 0

    lax.fori_loop(0, GROUPS, group, 0)

    turned = turn[...].T
    up_z[0:8, :] = turned[0:8, :]
    down_z[0:8, :] = turned[8:16, :]
    for t in range(PLANES):
        for d in range(5):
            up_y[d * 4 + t : d * 4 + t + 1, :] = coll[Y_UP[d], t * 4 + 3, 7:8, :]
            down_y[d * 4 + t : d * 4 + t + 1, :] = coll[Y_DOWN[d], t * 4, 0:1, :]
        up_y[20 + t : 21 + t, :] = mask[t * 4 + 3, 7:8, :].astype(jnp.float32)
        down_y[20 + t : 21 + t, :] = mask[t * 4, 0:1, :].astype(jnp.float32)

    def own(s, _):
        partial[s] = sphere_partial(
            coll, centers[0, s], centers[1, s] & (ROWS - 1), centers[2, s] & (COLS - 1), row_f, lane_f
        )
        return 0

    lax.fori_loop(0, SLOTS, own, 0)

    def listed(r, _):
        partial[SLOTS + r] = jnp.zeros((8, COLS), jnp.float32)

        @pl.when(lists[r, 0] >= 0)
        def _():
            partial[SLOTS + r] = sphere_partial(
                coll, lists[r, 3], lists[r, 1] + TILE // 2, lists[r, 2] + TILE // 2, row_f, lane_f
            )

        return 0

    lax.fori_loop(0, 16, listed, 0)

    tile = jnp.zeros((8, COLS), jnp.float32)
    for s in range(SLOTS):
        total = 2.0 * jnp.sum(partial[s], axis=1, keepdims=True)
        tile = jnp.where(lane == 4 * SLOTS + s, total, tile)
        tile = jnp.where(lane == STATE_LANE + s, state[:, s : s + 1], tile)
        tile = jnp.where(lane == DEST_LANE + s, destination[s].astype(jnp.float32), tile)
    for r in range(16):
        offset = DIRECTIONS[r // 2]
        block = (offset[0] + 1) * 3 + offset[1] + 1
        total = 2.0 * jnp.sum(partial[SLOTS + r], axis=1, keepdims=True)
        slot = lists[r, 0]
        at = jnp.where(slot >= 0, block * SLOTS + slot, -1)
        tile = jnp.where(lane == at, total, tile)
    info[...] = tile
    up_z[8:16, :] = tile
    down_z[8:16, :] = tile


def update_kernel(
    held,
    mask,
    centers,
    info,
    west,
    east,
    west_2,
    east_2,
    south,
    north,
    south_2,
    north_2,
    out,
    forces,
    state_next,
    ext,
    turn,
):
    lane = lax.broadcasted_iota(jnp.int32, (8, COLS), 1)
    sub = lax.broadcasted_iota(jnp.int32, (8, COLS), 0)
    row = lane & (ROWS - 1)
    plane = lax.shift_right_logical(lane, 5)
    wall = jnp.inf

    def walled(ref, start):
        values = ref[start : start + 8, :]
        return jnp.where(values[5:6, :] > 0.5, wall, values)

    def side(here, below, above, shifts):
        total = here
        for k, (c_x, c_y) in enumerate(shifts):
            moved = here
            if c_y == 1:
                moved = jnp.where(row == 0, pltpu.roll(below, COLS - 31, 1), pltpu.roll(here, 1, 1))
            if c_y == -1:
                moved = jnp.where(
                    row == ROWS - 1, pltpu.roll(above, 31, 1), pltpu.roll(here, COLS - 1, 1)
                )
            if c_x == 1:
                moved = jnp.where(plane == 0, wall, pltpu.roll(here, 32, 1))
            if c_x == -1:
                moved = jnp.where(plane == PLANES - 1, wall, pltpu.roll(here, COLS - 32, 1))
            total = jnp.where(sub == k, moved, total)
        return total

    turn[...] = jnp.zeros((COLS, COLS), jnp.float32)
    turn[0:8, :] = side(
        walled(west, 0),
        walled(south, EDGE_ROWS),
        walled(north, EDGE_ROWS),
        [VELOCITIES[i][:2] for i in Z_UP],
    )
    turn[8:16, :] = side(
        walled(east, 0),
        walled(south, EDGE_ROWS + 16),
        walled(north, EDGE_ROWS + 16),
        [VELOCITIES[i][:2] for i in Z_DOWN],
    )
    turned = turn[...].T
    turn[...] = turned

    column = lax.broadcasted_iota(jnp.int32, (ROWS, COLS), 1)
    for t in range(PLANES):
        solid = mask[t] > 0
        for i in range(19):
            ext[i, t, 8 : 8 + ROWS, :] = jnp.where(solid, wall, held[i, t])
        flag_low = south[20 + t : 21 + t, :] > 0.5
        flag_high = north[20 + t : 21 + t, :] > 0.5
        for d in range(5):
            r = d * 4 + t
            ext[Y_UP[d], t, 7:8, :] = jnp.where(flag_low, wall, south[r : r + 1, :])
            ext[Y_DOWN[d], t, 8 + ROWS : 9 + ROWS, :] = jnp.where(flag_high, wall, north[r : r + 1, :])
    for t in range(PLANES):
        solid = mask[t] > 0
        for i in range(19):
            c_x, c_y, c_z = VELOCITIES[i]
            source = t - c_x
            if not 0 <= source < PLANES:
                out[i, t] = jnp.where(solid, held[i, t], held[OPPOSITE[i], t])
                continue
            pulled = ext[i, source, 8 - c_y : 8 - c_y + ROWS, :]
            if c_z == 1:
                k = Z_UP.index(i)
                pulled = jnp.where(
                    column == 0, turn[t * ROWS : (t + 1) * ROWS, k : k + 1], pltpu.roll(pulled, 1, 1)
                )
            if c_z == -1:
                k = 8 + Z_DOWN.index(i)
                pulled = jnp.where(
                    column == COLS - 1,
                    turn[t * ROWS : (t + 1) * ROWS, k : k + 1],
                    pltpu.roll(pulled, COLS - 1, 1),
                )
            fluid = jnp.where(pulled == wall, held[OPPOSITE[i], t], pulled)
            out[i, t] = jnp.where(solid, held[i, t], fluid)

    tiles = {(0, 0): info[...]}
    tiles[0, -1] = west[8:16, :]
    tiles[0, 1] = east[8:16, :]
    tiles[0, -2] = west_2[...]
    tiles[0, 2] = east_2[...]
    for a, ref in ((-1, south), (1, north)):
        tiles[a, -1] = ref[EDGE_ROWS + 8 : EDGE_ROWS + 16, :]
        tiles[a, 1] = ref[EDGE_ROWS + 24 : EDGE_ROWS + 32, :]
        tiles[a, 0] = ref[EDGE_ROWS + 32 : EDGE_ROWS + 40, :]
        tiles[a, -2] = ref[EDGE_ROWS + 40 : EDGE_ROWS + 48, :]
        tiles[a, 2] = ref[EDGE_ROWS + 48 : EDGE_ROWS + 56, :]
    for a, ref in ((-2, south_2), (2, north_2)):
        for k, b in enumerate((0, -1, 1, -2, 2)):
            tiles[a, b] = ref[k * 8 : k * 8 + 8, :]
    device = lax.shift_right_logical(centers[1, 0], 5) * 16 + lax.shift_right_logical(centers[2, 0], 7)
    own_lanes = lane < SLOTS
    picked = [jnp.zeros((8, COLS), jnp.float32) for _ in range(SLOTS)]
    for a in (-1, 0, 1):
        for b in (-1, 0, 1):
            force = jnp.zeros((8, COLS), jnp.float32)
            for e in (-1, 0, 1):
                for g in (-1, 0, 1):
                    block = (1 - e) * 3 + 1 - g
                    shift = (COLS - block * SLOTS) % COLS
                    part = tiles[a + e, b + g]
                    force = force + (pltpu.roll(part, shift, 1) if shift else part)
            if a == 0 and b == 0:
                forces[...] = force[0:6, 0:SLOTS]
            record = pltpu.roll(tiles[a, b], COLS - STATE_LANE, 1)
            target = pltpu.roll(tiles[a, b], COLS - DEST_LANE, 1)[0:1, :]
            mass = record[6:7, :] * (3.0 / (4.0 * math.pi * RADIUS * RADIUS * RADIUS))
            spin = mass * record[7:8, :] * (1.0 / (RADIUS * RADIUS))
            gain = jnp.where(sub < 3, force * mass, jnp.where(sub < 6, force * spin, 0.0))
            updated = record + gain
            for j in range(SLOTS):
                wanted = (device * SLOTS + j).astype(jnp.float32)
                picked[j] = picked[j] + jnp.where(own_lanes & (target == wanted), updated, 0.0)
    result = jnp.zeros((8, COLS), jnp.float32)
    for j in range(SLOTS):
        result = jnp.where(lane == j, jnp.sum(picked[j], axis=1, keepdims=True), result)
    state_next[...] = result[:, 0:SLOTS]


VMEM = pl.BlockSpec(memory_space=pltpu.VMEM)
SMEM = pl.BlockSpec(memory_space=pltpu.SMEM)


def passed_along(block, axis, distance):
    count = lax.axis_size(axis)
    return lax.ppermute(block, axis, [((i - distance) % count, i) for i in range(count)])


def f32(*shape):
    return jax.ShapeDtypeStruct(shape, jnp.float32)


def on_device(populations, solid_mask, centers, tile_lists, sphere_state, destination, relax_rates):
    held, up_z, down_z, info, up_y, down_y = pl.pallas_call(
        collide_kernel,
        out_shape=(
            f32(19, GROUPS, 8, COLS),
            f32(16, COLS),
            f32(16, COLS),
            f32(8, COLS),
            f32(EDGE_ROWS, COLS),
            f32(EDGE_ROWS, COLS),
        ),
        in_specs=[VMEM, VMEM, VMEM, SMEM, SMEM, SMEM, SMEM],
        out_specs=(VMEM,) * 6,
        scratch_shapes=[
            pltpu.VMEM((19, GROUPS, 8, COLS), jnp.float32),
            pltpu.VMEM((N_COEF, 8, COLS), jnp.float32),
            pltpu.VMEM((COLS, COLS), jnp.float32),
            pltpu.VMEM((20, 8, COLS), jnp.float32),
        ],
        compiler_params=pltpu.CompilerParams(vmem_limit_bytes=32 * 1024 * 1024),
        name="collide",
    )(
        populations.reshape(19, GROUPS, 8, COLS),
        solid_mask.reshape(GROUPS, 8, COLS),
        sphere_state,
        centers,
        tile_lists,
        destination,
        relax_rates,
    )
    west = passed_along(up_z, "gz", 1)
    east = passed_along(down_z, "gz", -1)
    west_2 = passed_along(info, "gz", 2)
    east_2 = passed_along(info, "gz", -2)
    shared = [west, east, info, west_2, east_2]
    south = passed_along(jnp.concatenate([up_y] + shared), "gy", 1)
    north = passed_along(jnp.concatenate([down_y] + shared), "gy", -1)
    far = jnp.concatenate([info, west[8:16], east[8:16], west_2, east_2])
    south_2 = passed_along(far, "gy", 2)
    north_2 = passed_along(far, "gy", -2)
    return pl.pallas_call(
        update_kernel,
        out_shape=(f32(19, PLANES, ROWS, COLS), f32(6, SLOTS), f32(8, SLOTS)),
        in_specs=[VMEM, VMEM, SMEM] + [VMEM] * 9,
        out_specs=(VMEM,) * 3,
        scratch_shapes=[
            pltpu.VMEM((19, PLANES, ROWS + 16, COLS), jnp.float32),
            pltpu.VMEM((COLS, COLS), jnp.float32),
        ],
        compiler_params=pltpu.CompilerParams(vmem_limit_bytes=32 * 1024 * 1024),
        name="update",
    )(
        held.reshape(19, PLANES, ROWS, COLS),
        solid_mask,
        centers,
        info,
        west,
        east,
        west_2,
        east_2,
        south,
        north,
        south_2,
        north_2,
    )


def solution(mesh):
    return jax.shard_map(
        on_device,
        mesh=mesh,
        in_specs=(
            P(None, None, "gy", "gz"),
            P(None, "gy", "gz"),
            P(None, ("gy", "gz")),
            P(("gy", "gz"), None),
            P(None, ("gy", "gz")),
            P(("gy", "gz")),
            P(),
        ),
        out_specs=(P(None, None, "gy", "gz"), P(None, ("gy", "gz")), P(None, ("gy", "gz"))),
        check_vma=False,
    )
```

profile of v0, /device:TPU:1, one launch (start us, length us, event | category | flops | bytes accessed | tf_op | source)
XLA Modules:
  0.0 37.4 jit_solution(1478117179059655834)
XLA Ops:
  0.6 0.8 %copy.10.state = f32[8,4]{1,0:T(8,128)S(1)} copy(f32[8,4]{0,1:T(4,128)} %param.11) | data formatting | bytes 256 | tf_op args[4]
  1.4 0.8 %copy.11.lists = s32[16,4]{1,0:T(8,128)S(1)} copy(s32[16,4]{0,1:T(4,128)} %param.10) | data formatting | bytes 512 | tf_op args[3]
  2.1 1.3 %copy-done = f32[19,4,32,128]{3,2,1,0:T(8,128)S(1)} copy-done((f32[19,4,32,128]{3,2,1,0:T(8,128)S(1)}, f32[19,4,32,128]{3,2,1,0:T(8,128)}, u32[]{:S(2)}) %copy-start) | copy-done | bytes 1245208
  3.4 0.8 %copy-done.1 = s32[4,32,128]{2,1,0:T(8,128)S(1)} copy-done((s32[4,32,128]{2,1,0:T(8,128)S(1)}, s32[4,32,128]{2,1,0:T(8,128)}, u32[]{:S(2)}) %copy-start.1) | copy-done | bytes 65560
  4.3 0.7 %copy-done.2 = s32[3,4]{1,0:T(4,128)S(1)} copy-done((s32[3,4]{1,0:T(4,128)S(1)}, s32[3,4]{1,0:T(4,128)}, u32[]{:S(2)}) %copy-start.2) | copy-done | bytes 72
  5.0 0.7 %copy-done.3 = s32[4]{0:T(128)S(1)} copy-done((s32[4]{0:T(128)S(1)}, s32[4]{0:T(128)}, u32[]{:S(2)}) %copy-start.3) | copy-done | bytes 40
  5.6 0.7 %copy-done.4 = f32[19]{0:T(128)S(1)} copy-done((f32[19]{0:T(128)S(1)}, f32[19]{0:T(128)}, u32[]{:S(2)}) %copy-start.4) | copy-done | bytes 100
  6.3 4.0 %collide.1 = (f32[19,16,8,128]{3,2,1,0:T(8,128)S(1)}, f32[16,128]{1,0:T(8,128)S(1)}, f32[16,128]{1,0:T(8,128)S(1)}, f32[8,128]{1,0:T(8,128)S(1)}, f32[24,128]{1,0:T(8,128)S(1)}, /*index=5*/f32[24,128]{1,0:T(8,128)S(1)}) custom-call(f32[19,16,8,128]{3,2,1,0:T(8,128)S(1)} %bitcast.3, s32[16,8,128]{2,1,0:T(8,128)S(1)} %bitcast.5, f32[8,4]{1,0:T(8,128)S(1)} %copy.10.state, ...), custom_call_target="tpu_custom_call" | custom-call | tf_op jit(solution)/shard_map/collide/pallas_call | solution.py:521
  10.3 6.3 %collective-permute-start.3 = (f32[8,128]{1,0:T(8,128)S(1)}, f32[8,128]{1,0:T(8,128)S(1)}, u32[]{:S(2)}, u32[]{:S(2)}) collective-permute-start(f32[8,128]{1,0:T(8,128)S(1)} %get-tuple-element.10.info), channel_id=1, source_target_pairs={{2,0},{3,1},{4,2},{5,3},{6,4},{7,5},{8,6},{9,7},{10,8},{11,9},{12,... | collective-permute-start | bytes 12296 | tf_op jit(solution)/shard_map/ppermute | solution.py:513
  16.7 0.0 collective-permute-start.2
  16.7 0.2 collective-permute-start
  16.9 4.6 %collective-permute-start.1 = (f32[16,128]{1,0:T(8,128)S(1)}, f32[16,128]{1,0:T(8,128)S(1)}, u32[]{:S(2)}, u32[]{:S(2)}) collective-permute-start(f32[16,128]{1,0:T(8,128)S(1)} %get-tuple-element.12), channel_id=1, source_target_pairs={{1,0},{2,1},{3,2},{4,3},{5,4},{6,5},{7,6},{8,7},{9,8},{10,9},{11,1... | collective-permute-start | bytes 24584 | tf_op jit(solution)/shard_map/ppermute | solution.py:513
  21.5 1.0 %collective-permute-done.west = f32[16,128]{1,0:T(8,128)S(1)} collective-permute-done((f32[16,128]{1,0:T(8,128)S(1)}, f32[16,128]{1,0:T(8,128)S(1)}, u32[]{:S(2)}, u32[]{:S(2)}) %collective-permute-start) | collective-permute-done | bytes 8224 | tf_op jit(solution)/shard_map/ppermute | solution.py:513
  22.5 0.2 collective-permute-done.2.west_2
  22.7 0.0 collective-permute-done.3.east_2
  22.7 1.8 %collective-permute-start.5 = (f32[80,128]{1,0:T(8,128)S(1)}, f32[80,128]{1,0:T(8,128)S(1)}, u32[]{:S(2)}, u32[]{:S(2)}) collective-permute-start(f32[80,128]{1,0:T(8,128)S(1)} %get-tuple-element.23), channel_id=1, source_target_pairs={{16,0},{32,16},{48,32},{64,48},{80,64},{96,80},{112,96},{0,112},{1... | collective-permute-start | bytes 122888 | tf_op jit(solution)/shard_map/ppermute | solution.py:513
  24.6 1.7 %collective-permute-start.4 = (f32[80,128]{1,0:T(8,128)S(1)}, f32[80,128]{1,0:T(8,128)S(1)}, u32[]{:S(2)}, u32[]{:S(2)}) collective-permute-start(f32[80,128]{1,0:T(8,128)S(1)} %get-tuple-element.24), channel_id=1, source_target_pairs={{112,0},{0,16},{16,32},{32,48},{48,64},{64,80},{80,96},{96,112},{1... | collective-permute-start | bytes 122888 | tf_op jit(solution)/shard_map/ppermute | solution.py:513
  26.3 3.2 %collective-permute-start.7 = (f32[40,128]{1,0:T(8,128)S(1)}, f32[40,128]{1,0:T(8,128)S(1)}, u32[]{:S(2)}, u32[]{:S(2)}) collective-permute-start(f32[40,128]{1,0:T(8,128)S(1)} %get-tuple-element.22), channel_id=1, source_target_pairs={{32,0},{48,16},{64,32},{80,48},{96,64},{112,80},{0,96},{16,112},{3... | collective-permute-start | bytes 61448 | tf_op jit(solution)/shard_map/ppermute | solution.py:513
  29.5 0.0 collective-permute-start.6
  29.5 0.9 %collective-permute-done.7.north_2 = f32[40,128]{1,0:T(8,128)S(1)} collective-permute-done((f32[40,128]{1,0:T(8,128)S(1)}, f32[40,128]{1,0:T(8,128)S(1)}, u32[]{:S(2)}, u32[]{:S(2)}) %collective-permute-start.7) | collective-permute-done | bytes 20512 | tf_op jit(solution)/shard_map/ppermute | solution.py:513
  30.4 3.3 %collective-permute-done.6.south_2 = f32[40,128]{1,0:T(8,128)S(1)} collective-permute-done((f32[40,128]{1,0:T(8,128)S(1)}, f32[40,128]{1,0:T(8,128)S(1)}, u32[]{:S(2)}, u32[]{:S(2)}) %collective-permute-start.6) | collective-permute-done | bytes 20512 | tf_op jit(solution)/shard_map/ppermute | solution.py:513
  33.7 2.4 %update.1 = (f32[19,4,32,128]{3,2,1,0:T(8,128)}, f32[6,4]{1,0:T(8,128)S(1)}, f32[8,4]{1,0:T(8,128)S(1)}) custom-call(f32[19,4,32,128]{3,2,1,0:T(8,128)S(1)} %bitcast.4, s32[4,32,128]{2,1,0:T(8,128)S(1)} %copy-done.1, s32[3,4]{1,0:T(4,128)S(1)} %copy-done.2, f32[8,128]{1,0:T(8,128)S(1)} %get-tuple-element.10.info, f32[16,128]{1,0:T(8,128)S(1)} %collective-permute-done.west, ...), custom_call_target="tpu_custom_call" | custom-call | tf_op jit(solution)/shard_map/update/pallas_call | solution.py:560
  36.1 0.7 %copy.12 = f32[6,4]{0,1:T(4,128)} copy(f32[6,4]{1,0:T(8,128)S(1)} %get-tuple-element.16) | data formatting | bytes 192 | tf_op jit(solution)/shard_map/update/pallas_call | solution.py:560
  36.7 0.7 %copy.13 = f32[8,4]{0,1:T(4,128)} copy(f32[8,4]{1,0:T(8,128)S(1)} %get-tuple-element.17) | data formatting | bytes 256 | tf_op jit(solution)/shard_map/update/pallas_call | solution.py:560
  (16 shorter events, 0.0 us)
Async XLA Ops:
  2.1 1.3 %copy-start = (f32[19,4,32,128]{3,2,1,0:T(8,128)S(1)}, f32[19,4,32,128]{3,2,1,0:T(8,128)}, u32[]{:S(2)}) copy-start(f32[19,4,32,128]{3,2,1,0:T(8,128)} %param.7) | copy-start | bytes 3735556
  3.4 0.8 %copy-start.1 = (s32[4,32,128]{2,1,0:T(8,128)S(1)}, s32[4,32,128]{2,1,0:T(8,128)}, u32[]{:S(2)}) copy-start(s32[4,32,128]{2,1,0:T(8,128)} %mask.1) | copy-start | bytes 196612
  4.3 0.7 %copy-start.2 = (s32[3,4]{1,0:T(4,128)S(1)}, s32[3,4]{1,0:T(4,128)}, u32[]{:S(2)}) copy-start(s32[3,4]{1,0:T(4,128)} %centers.3) | copy-start | bytes 148
  5.0 0.7 %copy-start.3 = (s32[4]{0:T(128)S(1)}, s32[4]{0:T(128)}, u32[]{:S(2)}) copy-start(s32[4]{0:T(128)} %destination.1) | copy-start | bytes 52
  5.6 0.7 %copy-start.4 = (f32[19]{0:T(128)S(1)}, f32[19]{0:T(128)}, u32[]{:S(2)}) copy-start(f32[19]{0:T(128)} %rates.1) | copy-start | bytes 232
  10.3 12.4 %collective-permute-start.3 = (f32[8,128]{1,0:T(8,128)S(1)}, f32[8,128]{1,0:T(8,128)S(1)}, u32[]{:S(2)}, u32[]{:S(2)}) collective-permute-start(f32[8,128]{1,0:T(8,128)S(1)} %get-tuple-element.10.info), channel_id=1, source_target_pairs={{2,0},{3,1},{4,2},{5,3},{6,4},{7,5},{8,6},{9,7},{10,8},{11,9},{12,... | collective-permute-start | bytes 12296 | tf_op jit(solution)/shard_map/ppermute | solution.py:513
  16.7 6.1 %collective-permute-start.2 = (f32[8,128]{1,0:T(8,128)S(1)}, f32[8,128]{1,0:T(8,128)S(1)}, u32[]{:S(2)}, u32[]{:S(2)}) collective-permute-start(f32[8,128]{1,0:T(8,128)S(1)} %get-tuple-element.10.info), channel_id=1, source_target_pairs={{14,0},{15,1},{0,2},{1,3},{2,4},{3,5},{4,6},{5,7},{6,8},{7,9},{8,1... | collective-permute-start | bytes 12296 | tf_op jit(solution)/shard_map/ppermute | solution.py:513
  16.7 5.8 %collective-permute-start = (f32[16,128]{1,0:T(8,128)S(1)}, f32[16,128]{1,0:T(8,128)S(1)}, u32[]{:S(2)}, u32[]{:S(2)}) collective-permute-start(f32[16,128]{1,0:T(8,128)S(1)} %get-tuple-element.11), channel_id=1, source_target_pairs={{15,0},{0,1},{1,2},{2,3},{3,4},{4,5},{5,6},{6,7},{7,8},{8,9},{9,10... | collective-permute-start | bytes 24584 | tf_op jit(solution)/shard_map/ppermute | solution.py:513
  16.9 5.6 %collective-permute-start.1 = (f32[16,128]{1,0:T(8,128)S(1)}, f32[16,128]{1,0:T(8,128)S(1)}, u32[]{:S(2)}, u32[]{:S(2)}) collective-permute-start(f32[16,128]{1,0:T(8,128)S(1)} %get-tuple-element.12), channel_id=1, source_target_pairs={{1,0},{2,1},{3,2},{4,3},{5,4},{6,5},{7,6},{8,7},{9,8},{10,9},{11,1... | collective-permute-start | bytes 24584 | tf_op jit(solution)/shard_map/ppermute | solution.py:513
  22.7 11.0 %collective-permute-start.5 = (f32[80,128]{1,0:T(8,128)S(1)}, f32[80,128]{1,0:T(8,128)S(1)}, u32[]{:S(2)}, u32[]{:S(2)}) collective-permute-start(f32[80,128]{1,0:T(8,128)S(1)} %get-tuple-element.23), channel_id=1, source_target_pairs={{16,0},{32,16},{48,32},{64,48},{80,64},{96,80},{112,96},{0,112},{1... | collective-permute-start | bytes 122888 | tf_op jit(solution)/shard_map/ppermute | solution.py:513
  24.6 9.2 %collective-permute-start.4 = (f32[80,128]{1,0:T(8,128)S(1)}, f32[80,128]{1,0:T(8,128)S(1)}, u32[]{:S(2)}, u32[]{:S(2)}) collective-permute-start(f32[80,128]{1,0:T(8,128)S(1)} %get-tuple-element.24), channel_id=1, source_target_pairs={{112,0},{0,16},{16,32},{32,48},{48,64},{64,80},{80,96},{96,112},{1... | collective-permute-start | bytes 122888 | tf_op jit(solution)/shard_map/ppermute | solution.py:513
  26.3 4.1 %collective-permute-start.7 = (f32[40,128]{1,0:T(8,128)S(1)}, f32[40,128]{1,0:T(8,128)S(1)}, u32[]{:S(2)}, u32[]{:S(2)}) collective-permute-start(f32[40,128]{1,0:T(8,128)S(1)} %get-tuple-element.22), channel_id=1, source_target_pairs={{32,0},{48,16},{64,32},{80,48},{96,64},{112,80},{0,96},{16,112},{3... | collective-permute-start | bytes 61448 | tf_op jit(solution)/shard_map/ppermute | solution.py:513
  29.5 4.2 %collective-permute-start.6 = (f32[40,128]{1,0:T(8,128)S(1)}, f32[40,128]{1,0:T(8,128)S(1)}, u32[]{:S(2)}, u32[]{:S(2)}) collective-permute-start(f32[40,128]{1,0:T(8,128)S(1)} %get-tuple-element.22), channel_id=1, source_target_pairs={{96,0},{112,16},{0,32},{16,48},{32,64},{48,80},{64,96},{80,112},{9... | collective-permute-start | bytes 61448 | tf_op jit(solution)/shard_map/ppermute | solution.py:513
where the time goes:
time: 37.3 us; the launch traced here: 37.4 us
  starting transfers between devices  17.9 us (48%)
  local copies, waits for them, and re-layouts  6.97 us (19%)
  Pallas kernels  6.39 us (17%)
  waiting for transfers between devices  5.46 us (15%)
  between operations  0.68 us (2%)
    ppermute x8, starting transfers between devices, passed_along(): lax.ppermute(block, axis, [((i - distance) % count, i) for i in range(cou...  17.9 us
    unnamed x19, local copies, waits for them, and re-layouts  5.66 us
    ppermute x8, waiting for transfers between devices, passed_along(): lax.ppermute(block, axis, [((i - distance) % count, i) for i in range(cou...  5.46 us
    pallas_call x1, Pallas kernels, on_device(): pl.pallas_call(collide_kernel, out_shape=(f32(19, GROUPS, 8, COLS), f32(1...  4.04 us
    pallas_call x1, Pallas kernels, on_device(): pl.pallas_call(update_kernel, out_shape=(f32(19, PLANES, ROWS, COLS), f32...  2.35 us
    pallas_call x2, local copies, waits for them, and re-layouts, on_device(): pl.pallas_call(update_kernel, out_shape=(f32(19, PLANES, ROWS, COLS), f32...  1.31 us
  transfers between devices with their start and end apart: 8, of which 4 were waited for; matrix products, arithmetic and copies ran while one was open for 0% of the time, Pallas kernels for 0%

commit v1 on v0

--- a/solution.py
+++ b/solution.py
@@ -70,8 +70,9 @@
 ODD_MOMENTS = ((1, 10, 11), (2, 12, 13), (3, 14, 15))
 ODD_CLASSES = ((1, 4, 5), (2, 4, 6), (3, 5, 6))
 CROSS_MOMENTS = (7, 8, 9)
-STATE_LANE = 64
-DEST_LANE = 96
+STATE_LANE = 40
+DEST_LANE = 48
+HALF = 64
 EDGE_ROWS = 24
 
 
@@ -274,6 +275,21 @@
 
 
 def collide_kernel(
+    pops_in,
+    mask_in,
+    state_in,
+    centers_in,
+    lists_in,
+    destination_in,
+    rates_in,
+    held,
+    walls,
+    keep,
+    give,
+    info,
+    inner,
+    outer,
+    meta,
     pops,
     mask,
     state,
@@ -281,26 +297,49 @@
     lists,
     destination,
     rates,
-    held,
-    up_z,
-    down_z,
-    info,
-    up_y,
-    down_y,
     coll,
     coef,
     turn,
     partial,
+    sems,
 ):
+    small = [
+        pltpu.make_async_copy(source, target, sems.at[4 + k])
+        for k, (source, target) in enumerate(
+            (
+                (rates_in, rates),
+                (mask_in, mask),
+                (centers_in, centers),
+                (lists_in, lists),
+                (destination_in, destination),
+                (state_in, state),
+            )
+        )
+    ]
+    large = [
+        pltpu.make_async_copy(
+            pops_in.at[:, pl.ds(t * 4, 4)], pops.at[:, pl.ds(t * 4, 4)], sems.at[t]
+        )
+        for t in range(PLANES)
+    ]
+    small[0].start()
+    small[1].start()
+    for copy in large:
+        copy.start()
+    for copy in small[2:]:
+        copy.start()
     lane = lax.broadcasted_iota(jnp.int32, (8, COLS), 1)
     lane_f = lane.astype(jnp.float32)
     row_f = lax.broadcasted_iota(jnp.int32, (8, COLS), 0).astype(jnp.float32)
+    small[0].wait()
     store_coefficients(rates, coef)
+    small[1].wait()
 
     def group(g, _):
         f = [pops[i, g] for i in range(19)]
         solid = mask[g] > 0
         flag = solid.astype(jnp.float32)
+        walls[g] = flag
         new = collide(f, coef)
         edge = jnp.zeros((8, COLS), jnp.float32)
         for i in range(19):
@@ -313,17 +352,36 @@
         turn[pl.ds(pl.multiple_of(g * 8, 8), 8), :] = edge
         return 0
 
-    lax.fori_loop(0, GROUPS, group, 0)
+    for t in range(PLANES):
+        large[t].wait()
+        lax.fori_loop(t * 4, t * 4 + 4, group, 0)
+    for copy in small[2:]:
+        copy.wait()
+
+    device_y = lax.shift_right_logical(centers[1, 0], 5)
+    device_z = lax.shift_right_logical(centers[2, 0], 7)
+    core = device_y & 1
+    first = core == 0
+    meta[0:1, :] = jnp.full((1, COLS), (device_y * 16 + device_z) * SLOTS, jnp.int32).astype(
+        jnp.float32
+    )
+    meta[1:2, :] = jnp.full((1, COLS), core, jnp.int32).astype(jnp.float32)
+    meta[2:8, :] = jnp.zeros((6, COLS), jnp.float32)
 
     turned = turn[...].T
-    up_z[0:8, :] = turned[0:8, :]
-    down_z[0:8, :] = turned[8:16, :]
+    up_z, down_z = turned[0:8, :], turned[8:16, :]
+    keep[...] = jnp.where(first, up_z, down_z)
+    give[...] = jnp.where(first, down_z, up_z)
     for t in range(PLANES):
         for d in range(5):
-            up_y[d * 4 + t : d * 4 + t + 1, :] = coll[Y_UP[d], t * 4 + 3, 7:8, :]
-            down_y[d * 4 + t : d * 4 + t + 1, :] = coll[Y_DOWN[d], t * 4, 0:1, :]
-        up_y[20 + t : 21 + t, :] = mask[t * 4 + 3, 7:8, :].astype(jnp.float32)
-        down_y[20 + t : 21 + t, :] = mask[t * 4, 0:1, :].astype(jnp.float32)
+            up = coll[Y_UP[d], t * 4 + 3, 7:8, :]
+            down = coll[Y_DOWN[d], t * 4, 0:1, :]
+            inner[d * 4 + t : d * 4 + t + 1, :] = jnp.where(first, up, down)
+            outer[d * 4 + t : d * 4 + t + 1, :] = jnp.where(first, down, up)
+        up = walls[t * 4 + 3, 7:8, :]
+        down = walls[t * 4, 0:1, :]
+        inner[20 + t : 21 + t, :] = jnp.where(first, up, down)
+        outer[20 + t : 21 + t, :] = jnp.where(first, down, up)
 
     def own(s, _):
         partial[s] = sphere_partial(
@@ -336,61 +394,64 @@
     def listed(r, _):
         partial[SLOTS + r] = jnp.zeros((8, COLS), jnp.float32)
 
-        @pl.when(lists[r, 0] >= 0)
+        @pl.when(lists[0, r] >= 0)
         def _():
             partial[SLOTS + r] = sphere_partial(
-                coll, lists[r, 3], lists[r, 1] + TILE // 2, lists[r, 2] + TILE // 2, row_f, lane_f
+                coll, lists[3, r], lists[1, r] + TILE // 2, lists[2, r] + TILE // 2, row_f, lane_f
             )
 
         return 0
 
     lax.fori_loop(0, 16, listed, 0)
 
+    base = core * HALF
     tile = jnp.zeros((8, COLS), jnp.float32)
+    records = state[...].T
     for s in range(SLOTS):
         total = 2.0 * jnp.sum(partial[s], axis=1, keepdims=True)
-        tile = jnp.where(lane == 4 * SLOTS + s, total, tile)
-        tile = jnp.where(lane == STATE_LANE + s, state[:, s : s + 1], tile)
-        tile = jnp.where(lane == DEST_LANE + s, destination[s].astype(jnp.float32), tile)
+        tile = jnp.where(lane == base + 4 * SLOTS + s, total, tile)
+        tile = jnp.where(lane == base + STATE_LANE + s, records[:, s : s + 1], tile)
+        tile = jnp.where(lane == base + DEST_LANE + s, destination[s].astype(jnp.float32), tile)
     for r in range(16):
         offset = DIRECTIONS[r // 2]
         block = (offset[0] + 1) * 3 + offset[1] + 1
         total = 2.0 * jnp.sum(partial[SLOTS + r], axis=1, keepdims=True)
-        slot = lists[r, 0]
-        at = jnp.where(slot >= 0, block * SLOTS + slot, -1)
+        slot = lists[0, r]
+        at = jnp.where(slot >= 0, base + block * SLOTS + slot, -1)
         tile = jnp.where(lane == at, total, tile)
     info[...] = tile
-    up_z[8:16, :] = tile
-    down_z[8:16, :] = tile
 
 
 def update_kernel(
     held,
-    mask,
-    centers,
-    info,
-    west,
-    east,
-    west_2,
-    east_2,
-    south,
-    north,
-    south_2,
-    north_2,
-    out,
+    walls,
+    meta,
+    chip,
+    partner_edge,
+    near_in,
+    near_2,
+    far_in,
+    outer_in,
+    inner_in,
+    out_hbm,
     forces,
     state_next,
     ext,
     turn,
+    out,
+    sems,
 ):
     lane = lax.broadcasted_iota(jnp.int32, (8, COLS), 1)
     sub = lax.broadcasted_iota(jnp.int32, (8, COLS), 0)
     row = lane & (ROWS - 1)
     plane = lax.shift_right_logical(lane, 5)
     wall = jnp.inf
-
-    def walled(ref, start):
-        values = ref[start : start + 8, :]
+    second = jnp.broadcast_to(meta[1:2, :], (8, COLS)) > 0.5
+
+    def swap_if(a, b):
+        return jnp.where(second, b, a), jnp.where(second, a, b)
+
+    def walled(values):
         return jnp.where(values[5:6, :] > 0.5, wall, values)
 
     def side(here, below, above, shifts):
@@ -410,35 +471,43 @@
             total = jnp.where(sub == k, moved, total)
         return total
 
+    west, east = swap_if(walled(near_in[0:8, :]), walled(far_in[8:16, :]))
+    west_partner, east_partner = swap_if(walled(near_in[8:16, :]), walled(far_in[0:8, :]))
+    west_outer, east_outer = swap_if(
+        walled(outer_in[EDGE_ROWS + 8 : EDGE_ROWS + 16, :]), walled(outer_in[EDGE_ROWS : EDGE_ROWS + 8, :])
+    )
+    west_south, west_north = swap_if(west_outer, west_partner)
+    east_south, east_north = swap_if(east_outer, east_partner)
     turn[...] = jnp.zeros((COLS, COLS), jnp.float32)
-    turn[0:8, :] = side(
-        walled(west, 0),
-        walled(south, EDGE_ROWS),
-        walled(north, EDGE_ROWS),
-        [VELOCITIES[i][:2] for i in Z_UP],
-    )
-    turn[8:16, :] = side(
-        walled(east, 0),
-        walled(south, EDGE_ROWS + 16),
-        walled(north, EDGE_ROWS + 16),
-        [VELOCITIES[i][:2] for i in Z_DOWN],
-    )
+    turn[0:8, :] = side(west, west_south, west_north, [VELOCITIES[i][:2] for i in Z_UP])
+    turn[8:16, :] = side(east, east_south, east_north, [VELOCITIES[i][:2] for i in Z_DOWN])
     turned = turn[...].T
     turn[...] = turned
+    pairs = [
+        swap_if(outer_in[k : k + 8, :], partner_edge[k : k + 8, :]) for k in range(0, EDGE_ROWS, 8)
+    ]
+    south = [p[0] for p in pairs]
+    north = [p[1] for p in pairs]
+
+    def edge_row(edge, r):
+        return edge[r // 8][r % 8 : r % 8 + 1, :]
 
     column = lax.broadcasted_iota(jnp.int32, (ROWS, COLS), 1)
     for t in range(PLANES):
-        solid = mask[t] > 0
+        solid = walls[t] > 0.5
         for i in range(19):
             ext[i, t, 8 : 8 + ROWS, :] = jnp.where(solid, wall, held[i, t])
-        flag_low = south[20 + t : 21 + t, :] > 0.5
-        flag_high = north[20 + t : 21 + t, :] > 0.5
+        flag_low = edge_row(south, 20 + t) > 0.5
+        flag_high = edge_row(north, 20 + t) > 0.5
         for d in range(5):
             r = d * 4 + t
-            ext[Y_UP[d], t, 7:8, :] = jnp.where(flag_low, wall, south[r : r + 1, :])
-            ext[Y_DOWN[d], t, 8 + ROWS : 9 + ROWS, :] = jnp.where(flag_high, wall, north[r : r + 1, :])
+            ext[Y_UP[d], t, 7:8, :] = jnp.where(flag_low, wall, edge_row(south, r))
+            ext[Y_DOWN[d], t, 8 + ROWS : 9 + ROWS, :] = jnp.where(
+                flag_high, wall, edge_row(north, r)
+            )
+    copies = []
     for t in range(PLANES):
-        solid = mask[t] > 0
+        solid = walls[t] > 0.5
         for i in range(19):
             c_x, c_y, c_z = VELOCITIES[i]
             source = t - c_x
@@ -460,22 +529,35 @@
                 )
             fluid = jnp.where(pulled == wall, held[OPPOSITE[i], t], pulled)
             out[i, t] = jnp.where(solid, held[i, t], fluid)
-
-    tiles = {(0, 0): info[...]}
-    tiles[0, -1] = west[8:16, :]
-    tiles[0, 1] = east[8:16, :]
-    tiles[0, -2] = west_2[...]
-    tiles[0, 2] = east_2[...]
-    for a, ref in ((-1, south), (1, north)):
-        tiles[a, -1] = ref[EDGE_ROWS + 8 : EDGE_ROWS + 16, :]
-        tiles[a, 1] = ref[EDGE_ROWS + 24 : EDGE_ROWS + 32, :]
-        tiles[a, 0] = ref[EDGE_ROWS + 32 : EDGE_ROWS + 40, :]
-        tiles[a, -2] = ref[EDGE_ROWS + 40 : EDGE_ROWS + 48, :]
-        tiles[a, 2] = ref[EDGE_ROWS + 48 : EDGE_ROWS + 56, :]
-    for a, ref in ((-2, south_2), (2, north_2)):
-        for k, b in enumerate((0, -1, 1, -2, 2)):
-            tiles[a, b] = ref[k * 8 : k * 8 + 8, :]
-    device = lax.shift_right_logical(centers[1, 0], 5) * 16 + lax.shift_right_logical(centers[2, 0], 7)
+        copies.append(pltpu.make_async_copy(out.at[:, t], out_hbm.at[:, t], sems.at[t]))
+        copies[t].start()
+
+    middle = {0: chip[...]}
+    middle[-1], middle[1] = swap_if(near_in[16:24, :], far_in[16:24, :])
+    middle[-2], middle[2] = swap_if(near_2[...], far_in[24:32, :])
+    arrived = []
+    for ref, start in ((outer_in, EDGE_ROWS + 16), (inner_in, 0)):
+        group = [ref[start + 8 * k : start + 8 * k + 8, :] for k in range(5)]
+        columns = {0: group[0]}
+        columns[-1], columns[1] = swap_if(group[3], group[1])
+        columns[-2], columns[2] = swap_if(group[4], group[2])
+        arrived.append(columns)
+    tiles = {}
+    low = lane < HALF
+    for b in range(-2, 3):
+        before, after = swap_if(arrived[0][b], arrived[1][b])
+        turned_before, turned_own, turned_after = (
+            pltpu.roll(part, HALF, 1) for part in (before, middle[b], after)
+        )
+        tiles[0, b] = jnp.where(second, jnp.where(low, turned_before, turned_own), before)
+        tiles[1, b] = jnp.where(second, jnp.where(low, turned_own, turned_after), middle[b])
+        tiles[2, b] = jnp.where(second, turned_after, after)
+
+    def device_lanes(a, b, at):
+        shift = (COLS - (at + HALF * (a % 2))) % COLS
+        part = tiles[(a + 2) // 2, b]
+        return pltpu.roll(part, shift, 1) if shift else part
+
     own_lanes = lane < SLOTS
     picked = [jnp.zeros((8, COLS), jnp.float32) for _ in range(SLOTS)]
     for a in (-1, 0, 1):
@@ -484,104 +566,127 @@
             for e in (-1, 0, 1):
                 for g in (-1, 0, 1):
                     block = (1 - e) * 3 + 1 - g
-                    shift = (COLS - block * SLOTS) % COLS
-                    part = tiles[a + e, b + g]
-                    force = force + (pltpu.roll(part, shift, 1) if shift else part)
+                    force = force + device_lanes(a + e, b + g, block * SLOTS)
             if a == 0 and b == 0:
-                forces[...] = force[0:6, 0:SLOTS]
-            record = pltpu.roll(tiles[a, b], COLS - STATE_LANE, 1)
-            target = pltpu.roll(tiles[a, b], COLS - DEST_LANE, 1)[0:1, :]
+                own_force = force
+            record = device_lanes(a, b, STATE_LANE)
+            target = device_lanes(a, b, DEST_LANE)[0:1, :]
             mass = record[6:7, :] * (3.0 / (4.0 * math.pi * RADIUS * RADIUS * RADIUS))
             spin = mass * record[7:8, :] * (1.0 / (RADIUS * RADIUS))
             gain = jnp.where(sub < 3, force * mass, jnp.where(sub < 6, force * spin, 0.0))
             updated = record + gain
             for j in range(SLOTS):
-                wanted = (device * SLOTS + j).astype(jnp.float32)
+                wanted = meta[0:1, :] + float(j)
                 picked[j] = picked[j] + jnp.where(own_lanes & (target == wanted), updated, 0.0)
     result = jnp.zeros((8, COLS), jnp.float32)
     for j in range(SLOTS):
         result = jnp.where(lane == j, jnp.sum(picked[j], axis=1, keepdims=True), result)
-    state_next[...] = result[:, 0:SLOTS]
+    turn[0:8, :] = result
+    turn[8:16, :] = own_force
+    turned = turn[...].T
+    state_next[...] = turned[0:SLOTS, 0:8]
+    forces[...] = turned[0:SLOTS, 8:14]
+    for copy in copies:
+        copy.wait()
 
 
 VMEM = pl.BlockSpec(memory_space=pltpu.VMEM)
-SMEM = pl.BlockSpec(memory_space=pltpu.SMEM)
-
-
-def passed_along(block, axis, distance):
-    count = lax.axis_size(axis)
-    return lax.ppermute(block, axis, [((i - distance) % count, i) for i in range(count)])
+HBM = pl.BlockSpec(memory_space=pltpu.HBM)
 
 
 def f32(*shape):
     return jax.ShapeDtypeStruct(shape, jnp.float32)
 
 
+def swapped(block, distance):
+    count = lax.axis_size("gy")
+    route = [(p, (p + (distance if p % 2 == 0 else -distance)) % count) for p in range(count)]
+    return lax.ppermute(block, "gy", route)
+
+
+def spread(block, distance):
+    count_y, count_z = lax.axis_size("gy"), lax.axis_size("gz")
+    route = []
+    for p in range(count_y):
+        step = distance if p % 2 == 0 else -distance
+        route += [(p * count_z + q, p * count_z + (q + step) % count_z) for q in range(count_z)]
+    return lax.ppermute(block, ("gy", "gz"), route)
+
+
 def on_device(populations, solid_mask, centers, tile_lists, sphere_state, destination, relax_rates):
-    held, up_z, down_z, info, up_y, down_y = pl.pallas_call(
+    held, walls, keep, give, info, inner, outer, meta = pl.pallas_call(
         collide_kernel,
         out_shape=(
             f32(19, GROUPS, 8, COLS),
-            f32(16, COLS),
-            f32(16, COLS),
+            f32(GROUPS, 8, COLS),
+            f32(8, COLS),
+            f32(8, COLS),
             f32(8, COLS),
             f32(EDGE_ROWS, COLS),
             f32(EDGE_ROWS, COLS),
+            f32(8, COLS),
         ),
-        in_specs=[VMEM, VMEM, VMEM, SMEM, SMEM, SMEM, SMEM],
-        out_specs=(VMEM,) * 6,
+        in_specs=[HBM] * 7,
+        out_specs=(VMEM,) * 8,
         scratch_shapes=[
+            pltpu.VMEM((19, GROUPS, 8, COLS), jnp.float32),
+            pltpu.VMEM((GROUPS, 8, COLS), jnp.int32),
+            pltpu.VMEM((SLOTS, 8), jnp.float32),
+            pltpu.SMEM((3, SLOTS), jnp.int32),
+            pltpu.SMEM((4, 16), jnp.int32),
+            pltpu.SMEM((SLOTS,), jnp.int32),
+            pltpu.SMEM((19,), jnp.float32),
             pltpu.VMEM((19, GROUPS, 8, COLS), jnp.float32),
             pltpu.VMEM((N_COEF, 8, COLS), jnp.float32),
             pltpu.VMEM((COLS, COLS), jnp.float32),
             pltpu.VMEM((20, 8, COLS), jnp.float32),
+            pltpu.SemaphoreType.DMA((10,)),
         ],
         compiler_params=pltpu.CompilerParams(vmem_limit_bytes=32 * 1024 * 1024),
         name="collide",
     )(
         populations.reshape(19, GROUPS, 8, COLS),
         solid_mask.reshape(GROUPS, 8, COLS),
-        sphere_state,
+        sphere_state.T,
         centers,
-        tile_lists,
+        tile_lists.T,
         destination,
         relax_rates,
     )
-    west = passed_along(up_z, "gz", 1)
-    east = passed_along(down_z, "gz", -1)
-    west_2 = passed_along(info, "gz", 2)
-    east_2 = passed_along(info, "gz", -2)
-    shared = [west, east, info, west_2, east_2]
-    south = passed_along(jnp.concatenate([up_y] + shared), "gy", 1)
-    north = passed_along(jnp.concatenate([down_y] + shared), "gy", -1)
-    far = jnp.concatenate([info, west[8:16], east[8:16], west_2, east_2])
-    south_2 = passed_along(far, "gy", 2)
-    north_2 = passed_along(far, "gy", -2)
-    return pl.pallas_call(
+    partner = swapped(jnp.concatenate([give, info, inner]), 1)
+    chip = info + partner[8:16]
+    near_2 = spread(chip, 2)
+    near = spread(jnp.concatenate([keep, partner[0:8], chip]), 1)
+    far = swapped(jnp.concatenate([near, near_2]), 1)
+    spheres = [chip, near[16:24], near_2, far[16:32]]
+    from_outer = swapped(jnp.concatenate([outer, near[0:8], far[8:16]] + spheres), -1)
+    from_inner = swapped(jnp.concatenate(spheres), 3)
+    populations_next, forces, state_next = pl.pallas_call(
         update_kernel,
-        out_shape=(f32(19, PLANES, ROWS, COLS), f32(6, SLOTS), f32(8, SLOTS)),
-        in_specs=[VMEM, VMEM, SMEM] + [VMEM] * 9,
-        out_specs=(VMEM,) * 3,
+        out_shape=(f32(19, PLANES, ROWS, COLS), f32(SLOTS, 6), f32(SLOTS, 8)),
+        in_specs=[VMEM] * 10,
+        out_specs=(HBM, VMEM, VMEM),
         scratch_shapes=[
             pltpu.VMEM((19, PLANES, ROWS + 16, COLS), jnp.float32),
             pltpu.VMEM((COLS, COLS), jnp.float32),
+            pltpu.VMEM((19, PLANES, ROWS, COLS), jnp.float32),
+            pltpu.SemaphoreType.DMA((PLANES,)),
         ],
         compiler_params=pltpu.CompilerParams(vmem_limit_bytes=32 * 1024 * 1024),
         name="update",
     )(
         held.reshape(19, PLANES, ROWS, COLS),
-        solid_mask,
-        centers,
-        info,
-        west,
-        east,
-        west_2,
-        east_2,
-        south,
-        north,
-        south_2,
-        north_2,
+        walls.reshape(PLANES, ROWS, COLS),
+        meta,
+        chip,
+        partner[16:40],
+        near,
+        near_2,
+        far,
+        from_outer,
+        from_inner,
     )
+    return populations_next, forces.T, state_next.T
 
 
 def solution(mesh):

time: 37.3 us -> 33.3 us (0.89)
  starting transfers between devices: 17.9 us -> 14.7 us
  local copies, waits for them, and re-layouts: 6.97 us -> 5.49 us
    ppermute x8 -> x6, starting transfers between devices: 17.9 us -> 14.7 us  [the longest x4 8.56 us: swapped(): return lax.ppermute(block, 'gy', route)]
    pallas_call x2 -> x0, local copies, waits for them, and re-layouts: 1.31 us -> none  [on_device(): pl.pallas_call(update_kernel, out_shape=(f32(19, PLANES, ROWS, COLS), f32...]
    ppermute x8 -> x6, waiting for transfers between devices: 5.46 us -> 5.49 us  [the longest x4 3.75 us: swapped(): return lax.ppermute(block, 'gy', route)]
  transfers between devices with their start and end apart: 8 -> 6, of which waited for: 4 -> 4; matrix products, arithmetic and copies ran while one was open for 0% -> 0% of each run, Pallas kernels for 0% -> 0%
where the time goes in v1:
time: 33.3 us; the launch traced here: 33 us
  starting transfers between devices  14.7 us (44%)
  Pallas kernels  6.64 us (20%)
  local copies, waits for them, and re-layouts  5.49 us (16%)
  waiting for transfers between devices  5.49 us (16%)
  between operations  0.68 us (2%)
    ppermute x4, starting transfers between devices, swapped(): return lax.ppermute(block, 'gy', route)  8.56 us
    ppermute x2, starting transfers between devices, spread(): return lax.ppermute(block, ('gy', 'gz'), route)  6.14 us
    unnamed x19, local copies, waits for them, and re-layouts  5.49 us
    pallas_call x1, Pallas kernels, on_device(): pl.pallas_call(collide_kernel, out_shape=(f32(19, GROUPS, 8, COLS), f32(G...  4.1 us
    ppermute x4, waiting for transfers between devices, swapped(): return lax.ppermute(block, 'gy', route)  3.75 us
    pallas_call x1, Pallas kernels, on_device(): pl.pallas_call(update_kernel, out_shape=(f32(19, PLANES, ROWS, COLS), f32...  2.54 us
    ppermute x2, waiting for transfers between devices, spread(): return lax.ppermute(block, ('gy', 'gz'), route)  1.74 us
  transfers between devices with their start and end apart: 6, of which 4 were waited for; matrix products, arithmetic and copies ran while one was open for 0% of the time, Pallas kernels for 0%

profile of v1, /device:TPU:1, one launch (start us, length us, event | category | flops | bytes accessed | tf_op | source)
XLA Modules:
  0.0 33.0 jit_solution(16531667468829993548)
XLA Ops:
  0.6 0.0 copy-start
  0.6 1.3 %copy-done = f32[19,4,32,128]{3,2,1,0:T(8,128)S(1)} copy-done((f32[19,4,32,128]{3,2,1,0:T(8,128)S(1)}, f32[19,4,32,128]{3,2,1,0:T(8,128)}, u32[]{:S(2)}) %copy-start) | copy-done | bytes 1245208
  1.9 0.0 copy-start.1
  1.9 0.8 %copy-done.1 = s32[4,32,128]{2,1,0:T(8,128)S(1)} copy-done((s32[4,32,128]{2,1,0:T(8,128)S(1)}, s32[4,32,128]{2,1,0:T(8,128)}, u32[]{:S(2)}) %copy-start.1) | copy-done | bytes 65560
  2.8 0.0 copy-start.2
  2.8 0.7 %copy-done.2 = f32[8,4]{0,1:T(4,128)S(1)} copy-done((f32[8,4]{0,1:T(4,128)S(1)}, f32[8,4]{0,1:T(4,128)}, u32[]{:S(2)}) %copy-start.2) | copy-done | bytes 152
  3.5 0.7 %copy-done.3 = s32[3,4]{1,0:T(4,128)S(1)} copy-done((s32[3,4]{1,0:T(4,128)S(1)}, s32[3,4]{1,0:T(4,128)}, u32[]{:S(2)}) %copy-start.3) | copy-done | bytes 72
  4.1 0.7 %copy-done.4 = s32[16,4]{0,1:T(4,128)S(1)} copy-done((s32[16,4]{0,1:T(4,128)S(1)}, s32[16,4]{0,1:T(4,128)}, u32[]{:S(2)}) %copy-start.4) | copy-done | bytes 280
  4.8 0.7 %copy-done.5 = s32[4]{0:T(128)S(1)} copy-done((s32[4]{0:T(128)S(1)}, s32[4]{0:T(128)}, u32[]{:S(2)}) %copy-start.5) | copy-done | bytes 40
  5.5 0.7 %copy-done.6 = f32[19]{0:T(128)S(1)} copy-done((f32[19]{0:T(128)S(1)}, f32[19]{0:T(128)}, u32[]{:S(2)}) %copy-start.6) | copy-done | bytes 100
  6.1 4.1 %collide.1 = (f32[19,16,8,128]{3,2,1,0:T(8,128)S(1)}, f32[16,8,128]{2,1,0:T(8,128)S(1)}, f32[8,128]{1,0:T(8,128)S(1)}, f32[8,128]{1,0:T(8,128)S(1)}, f32[8,128]{...) custom-call(f32[19,16,8,128]{3,2,1,0:T(8,128)S(1)} %bitcast.8, ...), custom_call_target="tpu_custom_call" | custom-call | tf_op jit(solution)/shard_map/collide/pallas_call | solution.py:617
  10.2 1.6 %collective-permute-start = (f32[40,128]{1,0:T(8,128)S(1)}, f32[40,128]{1,0:T(8,128)S(1)}, u32[]{:S(2)}, u32[]{:S(2)}) collective-permute-start(f32[40,128]{1,0:T(8,128)S(1)} %pad_maximum_fusion), channel_id=1, source_target_pairs={{0,16},{16,0},{32,48},{48,32},{64,80},{80,64},{96,112},{112,96},{1... | collective-permute-start | bytes 61448 | tf_op jit(solution)/shard_map/ppermute | solution.py:604
  11.8 0.8 %collective-permute-done = f32[40,128]{1,0:T(8,128)S(1)} collective-permute-done((f32[40,128]{1,0:T(8,128)S(1)}, f32[40,128]{1,0:T(8,128)S(1)}, u32[]{:S(2)}, u32[]{:S(2)}) %collective-permute-start) | collective-permute-done | bytes 20512 | tf_op jit(solution)/shard_map/ppermute | solution.py:604
  12.7 5.3 %collective-permute-start.2 = (f32[8,128]{1,0:T(8,128)S(1)}, f32[8,128]{1,0:T(8,128)S(1)}, u32[]{:S(2)}, u32[]{:S(2)}) collective-permute-start(f32[8,128]{1,0:T(8,128)S(1)} %get-tuple-element.26.chip), channel_id=1, source_target_pairs={{0,2},{1,3},{2,4},{3,5},{4,6},{5,7},{6,8},{7,9},{8,10},{9,11},{10,... | collective-permute-start | bytes 12296 | tf_op jit(solution)/shard_map/ppermute | solution.py:613
  18.0 0.8 %collective-permute-start.1 = (f32[24,128]{1,0:T(8,128)S(1)}, f32[24,128]{1,0:T(8,128)S(1)}, u32[]{:S(2)}, u32[]{:S(2)}) collective-permute-start(f32[24,128]{1,0:T(8,128)S(1)} %pad_maximum_fusion.3), channel_id=1, source_target_pairs={{0,1},{1,2},{2,3},{3,4},{4,5},{5,6},{6,7},{7,8},{8,9},{9,10},{10,1... | collective-permute-start | bytes 36872 | tf_op jit(solution)/shard_map/ppermute | solution.py:613
  18.8 0.0 collective-permute-done.2.near_2
  18.8 1.7 %collective-permute-done.1.near_in = f32[24,128]{1,0:T(8,128)S(1)} collective-permute-done((f32[24,128]{1,0:T(8,128)S(1)}, f32[24,128]{1,0:T(8,128)S(1)}, u32[]{:S(2)}, u32[]{:S(2)}) %collective-permute-start.1) | collective-permute-done | bytes 12320 | tf_op jit(solution)/shard_map/ppermute | solution.py:613
  20.6 2.7 %collective-permute-start.3 = (f32[32,128]{1,0:T(8,128)S(1)}, f32[32,128]{1,0:T(8,128)S(1)}, u32[]{:S(2)}, u32[]{:S(2)}) collective-permute-start(f32[32,128]{1,0:T(8,128)S(1)} %pad_maximum_fusion.2), channel_id=1, source_target_pairs={{0,16},{16,0},{32,48},{48,32},{64,80},{80,64},{96,112},{112,96},{1... | collective-permute-start | bytes 49160 | tf_op jit(solution)/shard_map/ppermute | solution.py:604
  23.3 0.8 %collective-permute-done.3.far_in = f32[32,128]{1,0:T(8,128)S(1)} collective-permute-done((f32[32,128]{1,0:T(8,128)S(1)}, f32[32,128]{1,0:T(8,128)S(1)}, u32[]{:S(2)}, u32[]{:S(2)}) %collective-permute-start.3) | collective-permute-done | bytes 16416 | tf_op jit(solution)/shard_map/ppermute | solution.py:604
  24.2 1.9 %collective-permute-start.4 = (f32[80,128]{1,0:T(8,128)S(1)}, f32[80,128]{1,0:T(8,128)S(1)}, u32[]{:S(2)}, u32[]{:S(2)}) collective-permute-start(f32[80,128]{1,0:T(8,128)S(1)} %get-tuple-element.28), channel_id=1, source_target_pairs={{0,112},{16,32},{32,16},{48,64},{64,48},{80,96},{96,80},{112,0},{1... | collective-permute-start | bytes 122888 | tf_op jit(solution)/shard_map/ppermute | solution.py:604
  26.1 2.4 %collective-permute-start.5 = (f32[40,128]{1,0:T(8,128)S(1)}, f32[40,128]{1,0:T(8,128)S(1)}, u32[]{:S(2)}, u32[]{:S(2)}) collective-permute-start(f32[40,128]{1,0:T(8,128)S(1)} %pad_maximum_fusion.1), channel_id=1, source_target_pairs={{0,48},{16,96},{32,80},{48,0},{64,112},{80,32},{96,16},{112,64},{1... | collective-permute-start | bytes 61448 | tf_op jit(solution)/shard_map/ppermute | solution.py:604
  28.4 2.1 %collective-permute-done.5.inner_in = f32[40,128]{1,0:T(8,128)S(1)} collective-permute-done((f32[40,128]{1,0:T(8,128)S(1)}, f32[40,128]{1,0:T(8,128)S(1)}, u32[]{:S(2)}, u32[]{:S(2)}) %collective-permute-start.5) | collective-permute-done | bytes 20512 | tf_op jit(solution)/shard_map/ppermute | solution.py:604
  30.5 0.0 collective-permute-done.4.outer_in
  30.5 2.5 %update.1 = (f32[19,4,32,128]{3,2,1,0:T(8,128)}, f32[4,6]{1,0:T(4,128)}, f32[4,8]{1,0:T(4,128)}) custom-call(f32[19,4,32,128]{3,2,1,0:T(8,128)S(1)} %bitcast.9, f32[4,32,128]{2,1,0:T(8,128)S(1)} %bitcast.11, f32[8,128]{1,0:T(8,128)S(1)} %get-tuple-element.16.meta, f32[8,128]{1,0:T(8,128)S(1)} %get-tuple-element.26.chip, f32[24,128]{1,0:T(8,128)S(1)} %slice.29.partner_edge, ...), custom_call_target="tpu_custom_call" | custom-call | tf_op jit(solution)/shard_map/update/pallas_call | solution.py:664
  (17 shorter events, 0.0 us)
Async XLA Ops:
  0.6 1.3 %copy-start = (f32[19,4,32,128]{3,2,1,0:T(8,128)S(1)}, f32[19,4,32,128]{3,2,1,0:T(8,128)}, u32[]{:S(2)}) copy-start(f32[19,4,32,128]{3,2,1,0:T(8,128)} %param.7) | copy-start | bytes 3735556
  1.9 0.8 %copy-start.1 = (s32[4,32,128]{2,1,0:T(8,128)S(1)}, s32[4,32,128]{2,1,0:T(8,128)}, u32[]{:S(2)}) copy-start(s32[4,32,128]{2,1,0:T(8,128)} %param.8) | copy-start | bytes 196612
  2.8 0.7 %copy-start.2 = (f32[8,4]{0,1:T(4,128)S(1)}, f32[8,4]{0,1:T(4,128)}, u32[]{:S(2)}) copy-start(f32[8,4]{0,1:T(4,128)} %param.11) | copy-start | bytes 388
  3.4 0.7 %copy-start.3 = (s32[3,4]{1,0:T(4,128)S(1)}, s32[3,4]{1,0:T(4,128)}, u32[]{:S(2)}) copy-start(s32[3,4]{1,0:T(4,128)} %centers_in.1) | copy-start | bytes 148
  4.1 0.7 %copy-start.4 = (s32[16,4]{0,1:T(4,128)S(1)}, s32[16,4]{0,1:T(4,128)}, u32[]{:S(2)}) copy-start(s32[16,4]{0,1:T(4,128)} %param.10) | copy-start | bytes 772
  4.8 0.7 %copy-start.5 = (s32[4]{0:T(128)S(1)}, s32[4]{0:T(128)}, u32[]{:S(2)}) copy-start(s32[4]{0:T(128)} %destination_in.1) | copy-start | bytes 52
  5.5 0.7 %copy-start.6 = (f32[19]{0:T(128)S(1)}, f32[19]{0:T(128)}, u32[]{:S(2)}) copy-start(f32[19]{0:T(128)} %rates_in.1) | copy-start | bytes 232
  10.2 2.4 %collective-permute-start = (f32[40,128]{1,0:T(8,128)S(1)}, f32[40,128]{1,0:T(8,128)S(1)}, u32[]{:S(2)}, u32[]{:S(2)}) collective-permute-start(f32[40,128]{1,0:T(8,128)S(1)} %pad_maximum_fusion), channel_id=1, source_target_pairs={{0,16},{16,0},{32,48},{48,32},{64,80},{80,64},{96,112},{112,96},{1... | collective-permute-start | bytes 61448 | tf_op jit(solution)/shard_map/ppermute | solution.py:604
  12.7 6.1 %collective-permute-start.2 = (f32[8,128]{1,0:T(8,128)S(1)}, f32[8,128]{1,0:T(8,128)S(1)}, u32[]{:S(2)}, u32[]{:S(2)}) collective-permute-start(f32[8,128]{1,0:T(8,128)S(1)} %get-tuple-element.26.chip), channel_id=1, source_target_pairs={{0,2},{1,3},{2,4},{3,5},{4,6},{5,7},{6,8},{7,9},{8,10},{9,11},{10,... | collective-permute-start | bytes 12296 | tf_op jit(solution)/shard_map/ppermute | solution.py:613
  18.0 2.5 %collective-permute-start.1 = (f32[24,128]{1,0:T(8,128)S(1)}, f32[24,128]{1,0:T(8,128)S(1)}, u32[]{:S(2)}, u32[]{:S(2)}) collective-permute-start(f32[24,128]{1,0:T(8,128)S(1)} %pad_maximum_fusion.3), channel_id=1, source_target_pairs={{0,1},{1,2},{2,3},{3,4},{4,5},{5,6},{6,7},{7,8},{8,9},{9,10},{10,1... | collective-permute-start | bytes 36872 | tf_op jit(solution)/shard_map/ppermute | solution.py:613
  20.6 3.6 %collective-permute-start.3 = (f32[32,128]{1,0:T(8,128)S(1)}, f32[32,128]{1,0:T(8,128)S(1)}, u32[]{:S(2)}, u32[]{:S(2)}) collective-permute-start(f32[32,128]{1,0:T(8,128)S(1)} %pad_maximum_fusion.2), channel_id=1, source_target_pairs={{0,16},{16,0},{32,48},{48,32},{64,80},{80,64},{96,112},{112,96},{1... | collective-permute-start | bytes 49160 | tf_op jit(solution)/shard_map/ppermute | solution.py:604
  24.2 6.3 %collective-permute-start.4 = (f32[80,128]{1,0:T(8,128)S(1)}, f32[80,128]{1,0:T(8,128)S(1)}, u32[]{:S(2)}, u32[]{:S(2)}) collective-permute-start(f32[80,128]{1,0:T(8,128)S(1)} %get-tuple-element.28), channel_id=1, source_target_pairs={{0,112},{16,32},{32,16},{48,64},{64,48},{80,96},{96,80},{112,0},{1... | collective-permute-start | bytes 122888 | tf_op jit(solution)/shard_map/ppermute | solution.py:604
  26.1 4.4 %collective-permute-start.5 = (f32[40,128]{1,0:T(8,128)S(1)}, f32[40,128]{1,0:T(8,128)S(1)}, u32[]{:S(2)}, u32[]{:S(2)}) collective-permute-start(f32[40,128]{1,0:T(8,128)S(1)} %pad_maximum_fusion.1), channel_id=1, source_target_pairs={{0,48},{16,96},{32,80},{48,0},{64,112},{80,32},{96,16},{112,64},{1... | collective-permute-start | bytes 61448 | tf_op jit(solution)/shard_map/ppermute | solution.py:604

commit v2 on v1

--- a/solution.py
+++ b/solution.py
@@ -598,6 +598,10 @@
     return jax.ShapeDtypeStruct(shape, jnp.float32)
 
 
+def in_hbm(array):
+    return pltpu.with_memory_space_constraint(array, pltpu.HBM)
+
+
 def swapped(block, distance):
     count = lax.axis_size("gy")
     route = [(p, (p + (distance if p % 2 == 0 else -distance)) % count) for p in range(count)]
@@ -645,13 +649,13 @@
         compiler_params=pltpu.CompilerParams(vmem_limit_bytes=32 * 1024 * 1024),
         name="collide",
     )(
-        populations.reshape(19, GROUPS, 8, COLS),
-        solid_mask.reshape(GROUPS, 8, COLS),
-        sphere_state.T,
-        centers,
-        tile_lists.T,
-        destination,
-        relax_rates,
+        in_hbm(populations.reshape(19, GROUPS, 8, COLS)),
+        in_hbm(solid_mask.reshape(GROUPS, 8, COLS)),
+        in_hbm(sphere_state.T),
+        in_hbm(centers),
+        in_hbm(tile_lists.T),
+        in_hbm(destination),
+        in_hbm(relax_rates),
     )
     partner = swapped(jnp.concatenate([give, info, inner]), 1)
     chip = info + partner[8:16]

time: 33.3 us -> 27.9 us (0.84)
  local copies, waits for them, and re-layouts: 5.49 us -> 0.01 us
  Pallas kernels: 6.64 us -> 7.32 us
    unnamed x19 -> x5, local copies, waits for them, and re-layouts: 5.49 us -> 0.01 us
    pallas_call x1, Pallas kernels: 4.1 us -> 4.83 us  [on_device(): pl.pallas_call(collide_kernel, out_shape=(f32(19, GROUPS, 8, COLS), f32(G...]
where the time goes in v2:
time: 27.9 us; the launch traced here: 27.6 us
  starting transfers between devices  14.4 us (52%)
  Pallas kernels  7.32 us (26%)
  waiting for transfers between devices  5.25 us (19%)
  between operations  0.66 us (2%)
    ppermute x4, starting transfers between devices, swapped(): return lax.ppermute(block, 'gy', route)  8.39 us
    ppermute x2, starting transfers between devices, spread(): return lax.ppermute(block, ('gy', 'gz'), route)  5.98 us
    pallas_call x1, Pallas kernels, on_device(): pl.pallas_call(collide_kernel, out_shape=(f32(19, GROUPS, 8, COLS), f32(G...  4.83 us
    ppermute x4, waiting for transfers between devices, swapped(): return lax.ppermute(block, 'gy', route)  3.63 us
    pallas_call x1, Pallas kernels, on_device(): pl.pallas_call(update_kernel, out_shape=(f32(19, PLANES, ROWS, COLS), f32...  2.5 us
    ppermute x2, waiting for transfers between devices, spread(): return lax.ppermute(block, ('gy', 'gz'), route)  1.62 us
  transfers between devices with their start and end apart: 6, of which 4 were waited for; matrix products, arithmetic and copies ran while one was open for 0% of the time, Pallas kernels for 0%

profile of v2, /device:TPU:1, one launch (start us, length us, event | category | flops | bytes accessed | tf_op | source)
XLA Modules:
  0.0 27.6 jit_solution(10865638956659506629)
XLA Ops:
  0.6 4.8 %collide.1 = (f32[19,16,8,128]{3,2,1,0:T(8,128)S(1)}, f32[16,8,128]{2,1,0:T(8,128)S(1)}, f32[8,128]{1,0:T(8,128)S(1)}, f32[8,128]{1,0:T(8,128)S(1)}, f32[8,128]{...) custom-call(f32[19,16,8,128]{3,2,1,0:T(8,128)} %bitcast.10, ...), custom_call_target="tpu_custom_call" | custom-call | tf_op jit(solution)/shard_map/collide/pallas_call | solution.py:621
  5.5 1.5 %collective-permute-start = (f32[40,128]{1,0:T(8,128)S(1)}, f32[40,128]{1,0:T(8,128)S(1)}, u32[]{:S(2)}, u32[]{:S(2)}) collective-permute-start(f32[40,128]{1,0:T(8,128)S(1)} %pad_maximum_fusion), channel_id=1, source_target_pairs={{0,16},{16,0},{32,48},{48,32},{64,80},{80,64},{96,112},{112,96},{1... | collective-permute-start | bytes 61448 | tf_op jit(solution)/shard_map/ppermute | solution.py:608
  6.9 0.8 %collective-permute-done = f32[40,128]{1,0:T(8,128)S(1)} collective-permute-done((f32[40,128]{1,0:T(8,128)S(1)}, f32[40,128]{1,0:T(8,128)S(1)}, u32[]{:S(2)}, u32[]{:S(2)}) %collective-permute-start) | collective-permute-done | bytes 20512 | tf_op jit(solution)/shard_map/ppermute | solution.py:608
  7.8 5.1 %collective-permute-start.2 = (f32[8,128]{1,0:T(8,128)S(1)}, f32[8,128]{1,0:T(8,128)S(1)}, u32[]{:S(2)}, u32[]{:S(2)}) collective-permute-start(f32[8,128]{1,0:T(8,128)S(1)} %get-tuple-element.26.chip), channel_id=1, source_target_pairs={{0,2},{1,3},{2,4},{3,5},{4,6},{5,7},{6,8},{7,9},{8,10},{9,11},{10,... | collective-permute-start | bytes 12296 | tf_op jit(solution)/shard_map/ppermute | solution.py:617
  12.8 0.9 %collective-permute-start.1 = (f32[24,128]{1,0:T(8,128)S(1)}, f32[24,128]{1,0:T(8,128)S(1)}, u32[]{:S(2)}, u32[]{:S(2)}) collective-permute-start(f32[24,128]{1,0:T(8,128)S(1)} %pad_maximum_fusion.3), channel_id=1, source_target_pairs={{0,1},{1,2},{2,3},{3,4},{4,5},{5,6},{6,7},{7,8},{8,9},{9,10},{10,1... | collective-permute-start | bytes 36872 | tf_op jit(solution)/shard_map/ppermute | solution.py:617
  13.8 0.0 collective-permute-done.2.near_2
  13.8 1.6 %collective-permute-done.1.near_in = f32[24,128]{1,0:T(8,128)S(1)} collective-permute-done((f32[24,128]{1,0:T(8,128)S(1)}, f32[24,128]{1,0:T(8,128)S(1)}, u32[]{:S(2)}, u32[]{:S(2)}) %collective-permute-start.1) | collective-permute-done | bytes 12320 | tf_op jit(solution)/shard_map/ppermute | solution.py:617
  15.4 2.8 %collective-permute-start.3 = (f32[32,128]{1,0:T(8,128)S(1)}, f32[32,128]{1,0:T(8,128)S(1)}, u32[]{:S(2)}, u32[]{:S(2)}) collective-permute-start(f32[32,128]{1,0:T(8,128)S(1)} %pad_maximum_fusion.2), channel_id=1, source_target_pairs={{0,16},{16,0},{32,48},{48,32},{64,80},{80,64},{96,112},{112,96},{1... | collective-permute-start | bytes 49160 | tf_op jit(solution)/shard_map/ppermute | solution.py:608
  18.2 0.8 %collective-permute-done.3.far_in = f32[32,128]{1,0:T(8,128)S(1)} collective-permute-done((f32[32,128]{1,0:T(8,128)S(1)}, f32[32,128]{1,0:T(8,128)S(1)}, u32[]{:S(2)}, u32[]{:S(2)}) %collective-permute-start.3) | collective-permute-done | bytes 16416 | tf_op jit(solution)/shard_map/ppermute | solution.py:608
  19.0 1.7 %collective-permute-start.4 = (f32[80,128]{1,0:T(8,128)S(1)}, f32[80,128]{1,0:T(8,128)S(1)}, u32[]{:S(2)}, u32[]{:S(2)}) collective-permute-start(f32[80,128]{1,0:T(8,128)S(1)} %get-tuple-element.28), channel_id=1, source_target_pairs={{0,112},{16,32},{32,16},{48,64},{64,48},{80,96},{96,80},{112,0},{1... | collective-permute-start | bytes 122888 | tf_op jit(solution)/shard_map/ppermute | solution.py:608
  20.7 2.5 %collective-permute-start.5 = (f32[40,128]{1,0:T(8,128)S(1)}, f32[40,128]{1,0:T(8,128)S(1)}, u32[]{:S(2)}, u32[]{:S(2)}) collective-permute-start(f32[40,128]{1,0:T(8,128)S(1)} %pad_maximum_fusion.1), channel_id=1, source_target_pairs={{0,48},{16,96},{32,80},{48,0},{64,112},{80,32},{96,16},{112,64},{1... | collective-permute-start | bytes 61448 | tf_op jit(solution)/shard_map/ppermute | solution.py:608
  23.2 1.9 %collective-permute-done.5.inner_in = f32[40,128]{1,0:T(8,128)S(1)} collective-permute-done((f32[40,128]{1,0:T(8,128)S(1)}, f32[40,128]{1,0:T(8,128)S(1)}, u32[]{:S(2)}, u32[]{:S(2)}) %collective-permute-start.5) | collective-permute-done | bytes 20512 | tf_op jit(solution)/shard_map/ppermute | solution.py:608
  25.1 0.0 collective-permute-done.4.outer_in
  25.1 2.5 %update.1 = (f32[19,4,32,128]{3,2,1,0:T(8,128)}, f32[4,6]{1,0:T(4,128)}, f32[4,8]{1,0:T(4,128)}) custom-call(f32[19,4,32,128]{3,2,1,0:T(8,128)S(1)} %bitcast.8, f32[4,32,128]{2,1,0:T(8,128)S(1)} %bitcast.9, f32[8,128]{1,0:T(8,128)S(1)} %get-tuple-element.16.meta, f32[8,128]{1,0:T(8,128)S(1)} %get-tuple-element.26.chip, f32[24,128]{1,0:T(8,128)S(1)} %slice.29.partner_edge, ...), custom_call_target="tpu_custom_call" | custom-call | tf_op jit(solution)/shard_map/update/pallas_call | solution.py:668
  (13 shorter events, 0.0 us)
Async XLA Ops:
  5.5 2.3 %collective-permute-start = (f32[40,128]{1,0:T(8,128)S(1)}, f32[40,128]{1,0:T(8,128)S(1)}, u32[]{:S(2)}, u32[]{:S(2)}) collective-permute-start(f32[40,128]{1,0:T(8,128)S(1)} %pad_maximum_fusion), channel_id=1, source_target_pairs={{0,16},{16,0},{32,48},{48,32},{64,80},{80,64},{96,112},{112,96},{1... | collective-permute-start | bytes 61448 | tf_op jit(solution)/shard_map/ppermute | solution.py:608
  7.8 6.0 %collective-permute-start.2 = (f32[8,128]{1,0:T(8,128)S(1)}, f32[8,128]{1,0:T(8,128)S(1)}, u32[]{:S(2)}, u32[]{:S(2)}) collective-permute-start(f32[8,128]{1,0:T(8,128)S(1)} %get-tuple-element.26.chip), channel_id=1, source_target_pairs={{0,2},{1,3},{2,4},{3,5},{4,6},{5,7},{6,8},{7,9},{8,10},{9,11},{10,... | collective-permute-start | bytes 12296 | tf_op jit(solution)/shard_map/ppermute | solution.py:617
  12.8 2.5 %collective-permute-start.1 = (f32[24,128]{1,0:T(8,128)S(1)}, f32[24,128]{1,0:T(8,128)S(1)}, u32[]{:S(2)}, u32[]{:S(2)}) collective-permute-start(f32[24,128]{1,0:T(8,128)S(1)} %pad_maximum_fusion.3), channel_id=1, source_target_pairs={{0,1},{1,2},{2,3},{3,4},{4,5},{5,6},{6,7},{7,8},{8,9},{9,10},{10,1... | collective-permute-start | bytes 36872 | tf_op jit(solution)/shard_map/ppermute | solution.py:617
  15.4 3.6 %collective-permute-start.3 = (f32[32,128]{1,0:T(8,128)S(1)}, f32[32,128]{1,0:T(8,128)S(1)}, u32[]{:S(2)}, u32[]{:S(2)}) collective-permute-start(f32[32,128]{1,0:T(8,128)S(1)} %pad_maximum_fusion.2), channel_id=1, source_target_pairs={{0,16},{16,0},{32,48},{48,32},{64,80},{80,64},{96,112},{112,96},{1... | collective-permute-start | bytes 49160 | tf_op jit(solution)/shard_map/ppermute | solution.py:608
  19.0 6.1 %collective-permute-start.4 = (f32[80,128]{1,0:T(8,128)S(1)}, f32[80,128]{1,0:T(8,128)S(1)}, u32[]{:S(2)}, u32[]{:S(2)}) collective-permute-start(f32[80,128]{1,0:T(8,128)S(1)} %get-tuple-element.28), channel_id=1, source_target_pairs={{0,112},{16,32},{32,16},{48,64},{64,48},{80,96},{96,80},{112,0},{1... | collective-permute-start | bytes 122888 | tf_op jit(solution)/shard_map/ppermute | solution.py:608
  20.7 4.4 %collective-permute-start.5 = (f32[40,128]{1,0:T(8,128)S(1)}, f32[40,128]{1,0:T(8,128)S(1)}, u32[]{:S(2)}, u32[]{:S(2)}) collective-permute-start(f32[40,128]{1,0:T(8,128)S(1)} %pad_maximum_fusion.1), channel_id=1, source_target_pairs={{0,48},{16,96},{32,80},{48,0},{64,112},{80,32},{96,16},{112,64},{1... | collective-permute-start | bytes 61448 | tf_op jit(solution)/shard_map/ppermute | solution.py:608

commit v3 on v2

--- a/solution.py
+++ b/solution.py
@@ -233,26 +233,28 @@
             outside = dist > float(RADIUS * RADIUS)
             half = jnp.where(outside, (RADIUS * RADIUS - 1.0) * 0.5 - 0.5 * dist, -1e9)
             half_2 = half - 0.5
-
-            def linked(i, along, limit):
+            limits = {1: (half, -half), 2: (half_2, -half_2)}
+
+            def linked(i, along, kind):
+                limit, negative = limits[kind]
                 up, down = VELOCITIES[i][0], VELOCITIES[i + 1][0]
                 total = None
                 if 0 <= t + up < PLANES:
                     total = jnp.where(along <= limit, coll[i, t * 4 + tile], 0.0)
                 if 0 <= t + down < PLANES:
-                    back = jnp.where(-along <= limit, coll[i + 1, t * 4 + tile], 0.0)
+                    back = jnp.where(along >= negative, coll[i + 1, t * 4 + tile], 0.0)
                     total = -back if total is None else total - back
                 return total
 
-            l_x = linked(1, r_x, half)
-            l_y = linked(3, r_y, half)
-            l_z = linked(5, r_z, half)
-            l_xy = linked(7, r_y + r_x, half_2)
-            l_xmy = linked(9, r_x - r_y, half_2)
-            l_xz = linked(11, r_z + r_x, half_2)
-            l_xmz = linked(13, r_x - r_z, half_2)
-            l_yz = linked(15, y_plus_z, half_2)
-            l_ymz = linked(17, y_minus_z, half_2)
+            l_x = linked(1, r_x, 1)
+            l_y = linked(3, r_y, 1)
+            l_z = linked(5, r_z, 1)
+            l_xy = linked(7, r_y + r_x, 2)
+            l_xmy = linked(9, r_x - r_y, 2)
+            l_xz = linked(11, r_z + r_x, 2)
+            l_xmz = linked(13, r_x - r_z, 2)
+            l_yz = linked(15, y_plus_z, 2)
+            l_ymz = linked(17, y_minus_z, 2)
             m_x = l_x + ((l_xy + l_xmy) + (l_xz + l_xmz))
             m_y = l_y + ((l_xy - l_xmy) + (l_yz + l_ymz))
             m_z = l_z + ((l_xz - l_xmz) + (l_yz - l_ymz))
@@ -289,6 +291,7 @@
     info,
     inner,
     outer,
+    border,
     meta,
     pops,
     mask,
@@ -341,15 +344,9 @@
         flag = solid.astype(jnp.float32)
         walls[g] = flag
         new = collide(f, coef)
-        edge = jnp.zeros((8, COLS), jnp.float32)
         for i in range(19):
             coll[i, g] = new[i]
             held[i, g] = jnp.where(solid, f[i], new[i])
-        for k, values in enumerate([new[i] for i in Z_UP] + [flag]):
-            edge = jnp.where(lane == k, pltpu.roll(values, k + 1, 1), edge)
-        for k, values in enumerate([new[i] for i in Z_DOWN] + [flag]):
-            edge = jnp.where(lane == 8 + k, pltpu.roll(values, 8 + k, 1), edge)
-        turn[pl.ds(pl.multiple_of(g * 8, 8), 8), :] = edge
         return 0
 
     for t in range(PLANES):
@@ -368,8 +365,18 @@
     meta[1:2, :] = jnp.full((1, COLS), core, jnp.int32).astype(jnp.float32)
     meta[2:8, :] = jnp.zeros((6, COLS), jnp.float32)
 
+    for g in range(GROUPS):
+        edge = jnp.zeros((8, COLS), jnp.float32)
+        for k in range(6):
+            values = coll[Z_UP[k], g] if k < 5 else walls[g]
+            edge = jnp.where(lane == k, pltpu.roll(values, k + 1, 1), edge)
+        for k in range(6):
+            values = coll[Z_DOWN[k], g] if k < 5 else walls[g]
+            edge = jnp.where(lane == 8 + k, pltpu.roll(values, 8 + k, 1), edge)
+        turn[g * 8 : g * 8 + 8, :] = edge
     turned = turn[...].T
     up_z, down_z = turned[0:8, :], turned[8:16, :]
+    border[...] = turned[0:16, :]
     keep[...] = jnp.where(first, up_z, down_z)
     give[...] = jnp.where(first, down_z, up_z)
     for t in range(PLANES):
@@ -406,11 +413,13 @@
 
     base = core * HALF
     tile = jnp.zeros((8, COLS), jnp.float32)
-    records = state[...].T
     for s in range(SLOTS):
         total = 2.0 * jnp.sum(partial[s], axis=1, keepdims=True)
         tile = jnp.where(lane == base + 4 * SLOTS + s, total, tile)
-        tile = jnp.where(lane == base + STATE_LANE + s, records[:, s : s + 1], tile)
+        column = jnp.zeros((8, COLS), jnp.float32)
+        for r in range(8):
+            column = jnp.where(row_f == float(r), state[s, r], column)
+        tile = jnp.where(lane == base + STATE_LANE + s, column, tile)
         tile = jnp.where(lane == base + DEST_LANE + s, destination[s].astype(jnp.float32), tile)
     for r in range(16):
         offset = DIRECTIONS[r // 2]
@@ -422,9 +431,59 @@
     info[...] = tile
 
 
+Z_ALL = (5, 6, 11, 12, 13, 14, 15, 16, 17, 18)
+Y_ONLY = (3, 4, 7, 8, 9, 10)
+
+
+def stream_kernel(held, walls, out_hbm, z_part, y_part, ext, out, sems):
+    wall = jnp.inf
+    column = lax.broadcasted_iota(jnp.int32, (ROWS, COLS), 1)
+    for t in range(PLANES):
+        solid = walls[t] > 0.5
+        for i in range(19):
+            ext[i, t, 8 : 8 + ROWS, :] = jnp.where(solid, wall, held[i, t])
+            c_y = VELOCITIES[i][1]
+            if c_y == 1:
+                ext[i, t, 7:8, :] = jnp.full((1, COLS), wall, jnp.float32)
+            if c_y == -1:
+                ext[i, t, 8 + ROWS : 9 + ROWS, :] = jnp.full((1, COLS), wall, jnp.float32)
+    for t in range(PLANES):
+        solid = walls[t] > 0.5
+        for i in range(19):
+            c_x, c_y, c_z = VELOCITIES[i]
+            source = t - c_x
+            if 0 <= source < PLANES:
+                pulled = ext[i, source, 8 - c_y : 8 - c_y + ROWS, :]
+                if c_z == 1:
+                    pulled = jnp.where(column == 0, wall, pltpu.roll(pulled, 1, 1))
+                if c_z == -1:
+                    pulled = jnp.where(column == COLS - 1, wall, pltpu.roll(pulled, COLS - 1, 1))
+                fluid = jnp.where(pulled == wall, held[OPPOSITE[i], t], pulled)
+            else:
+                fluid = held[OPPOSITE[i], t]
+            result = jnp.where(solid, held[i, t], fluid)
+            if c_z == 0:
+                out[i, t] = result
+            else:
+                z_part[Z_ALL.index(i), t] = result
+            if i in Y_ONLY:
+                y_part[Y_ONLY.index(i), t] = result[0:8] if c_y == 1 else result[ROWS - 8 : ROWS]
+    copies = [
+        pltpu.make_async_copy(out.at[lo:hi], out_hbm.at[lo:hi], sems.at[k])
+        for k, (lo, hi) in enumerate(((0, 5), (7, 11)))
+    ]
+    for copy in copies:
+        copy.start()
+    for copy in copies:
+        copy.wait()
+
+
 def update_kernel(
-    held,
+    streamed,
+    z_part,
+    y_part,
     walls,
+    border,
     meta,
     chip,
     partner_edge,
@@ -436,11 +495,12 @@
     out_hbm,
     forces,
     state_next,
-    ext,
     turn,
-    out,
+    z_new,
+    y_new,
     sems,
 ):
+    del streamed
     lane = lax.broadcasted_iota(jnp.int32, (8, COLS), 1)
     sub = lax.broadcasted_iota(jnp.int32, (8, COLS), 0)
     row = lane & (ROWS - 1)
@@ -478,9 +538,15 @@
     )
     west_south, west_north = swap_if(west_outer, west_partner)
     east_south, east_north = swap_if(east_outer, east_partner)
+    low_solid = border[13:14, :] > 0.5
+    high_solid = border[5:6, :] > 0.5
     turn[...] = jnp.zeros((COLS, COLS), jnp.float32)
-    turn[0:8, :] = side(west, west_south, west_north, [VELOCITIES[i][:2] for i in Z_UP])
-    turn[8:16, :] = side(east, east_south, east_north, [VELOCITIES[i][:2] for i in Z_DOWN])
+    turn[0:8, :] = jnp.where(
+        low_solid, wall, side(west, west_south, west_north, [VELOCITIES[i][:2] for i in Z_UP])
+    )
+    turn[8:16, :] = jnp.where(
+        high_solid, wall, side(east, east_south, east_north, [VELOCITIES[i][:2] for i in Z_DOWN])
+    )
     turned = turn[...].T
     turn[...] = turned
     pairs = [
@@ -492,45 +558,56 @@
     def edge_row(edge, r):
         return edge[r // 8][r % 8 : r % 8 + 1, :]
 
+    def border_row(i, t):
+        c_x, c_y, _ = VELOCITIES[i]
+        edge, order, cells = (
+            (south, Y_UP, walls[t, 0:1, :]) if c_y == 1 else (north, Y_DOWN, walls[t, ROWS - 1 : ROWS, :])
+        )
+        values = edge_row(edge, order.index(i) * 4 + t - c_x)
+        return jnp.where(edge_row(edge, 20 + t - c_x) > 0.5, wall, values), cells > 0.5
+
+    def mended(tile, i, values):
+        changed = (sub == (0 if VELOCITIES[i][1] == 1 else 7)) & (values != wall)
+        return jnp.where(changed, values, tile)
+
     column = lax.broadcasted_iota(jnp.int32, (ROWS, COLS), 1)
-    for t in range(PLANES):
-        solid = walls[t] > 0.5
-        for i in range(19):
-            ext[i, t, 8 : 8 + ROWS, :] = jnp.where(solid, wall, held[i, t])
-        flag_low = edge_row(south, 20 + t) > 0.5
-        flag_high = edge_row(north, 20 + t) > 0.5
-        for d in range(5):
-            r = d * 4 + t
-            ext[Y_UP[d], t, 7:8, :] = jnp.where(flag_low, wall, edge_row(south, r))
-            ext[Y_DOWN[d], t, 8 + ROWS : 9 + ROWS, :] = jnp.where(
-                flag_high, wall, edge_row(north, r)
-            )
+    first_lane = lax.broadcasted_iota(jnp.int32, (1, COLS), 1)
     copies = []
-    for t in range(PLANES):
-        solid = walls[t] > 0.5
-        for i in range(19):
-            c_x, c_y, c_z = VELOCITIES[i]
-            source = t - c_x
-            if not 0 <= source < PLANES:
-                out[i, t] = jnp.where(solid, held[i, t], held[OPPOSITE[i], t])
-                continue
-            pulled = ext[i, source, 8 - c_y : 8 - c_y + ROWS, :]
-            if c_z == 1:
-                k = Z_UP.index(i)
-                pulled = jnp.where(
-                    column == 0, turn[t * ROWS : (t + 1) * ROWS, k : k + 1], pltpu.roll(pulled, 1, 1)
-                )
-            if c_z == -1:
-                k = 8 + Z_DOWN.index(i)
-                pulled = jnp.where(
-                    column == COLS - 1,
-                    turn[t * ROWS : (t + 1) * ROWS, k : k + 1],
-                    pltpu.roll(pulled, COLS - 1, 1),
-                )
-            fluid = jnp.where(pulled == wall, held[OPPOSITE[i], t], pulled)
-            out[i, t] = jnp.where(solid, held[i, t], fluid)
-        copies.append(pltpu.make_async_copy(out.at[:, t], out_hbm.at[:, t], sems.at[t]))
-        copies[t].start()
+
+    def send(source, target):
+        copies.append(pltpu.make_async_copy(source, target, sems.at[len(copies)]))
+        copies[-1].start()
+
+    for z, i in enumerate(Z_ALL):
+        _, c_y, c_z = VELOCITIES[i]
+        k = Z_UP.index(i) if c_z == 1 else 8 + Z_DOWN.index(i)
+        edge = 0 if c_z == 1 else COLS - 1
+        for t in range(PLANES):
+            entering = turn[t * ROWS : (t + 1) * ROWS, k : k + 1]
+            values = jnp.where((column == edge) & (entering != wall), entering, z_part[z, t])
+            z_new[z, t] = values
+            if c_y != 0:
+                values_in, solid = border_row(i, t)
+                values_in = pltpu.roll(values_in, 1 if c_z == 1 else COLS - 1, 1)
+                values_in = jnp.where(solid | (first_lane == edge), wall, values_in)
+                at = 0 if c_y == 1 else ROWS - 8
+                z_new[z, t, at : at + 8, :] = mended(values[at : at + 8], i, values_in)
+        if z == 1:
+            send(z_new.at[0:2], out_hbm.at[5:7])
+        if z == 5:
+            send(z_new.at[2:6], out_hbm.at[11:15])
+        if z == 9:
+            send(z_new.at[6:10], out_hbm.at[15:19])
+    for y, i in enumerate(Y_ONLY):
+        c_x, c_y, _ = VELOCITIES[i]
+        for t in range(PLANES):
+            tile = y_part[y, t]
+            if 0 <= t - c_x < PLANES:
+                values_in, solid = border_row(i, t)
+                tile = mended(tile, i, jnp.where(solid, wall, values_in))
+            y_new[y, t] = tile
+        at = 0 if c_y == 1 else ROWS - 8
+        send(y_new.at[y], out_hbm.at[i, :, at : at + 8])
 
     middle = {0: chip[...]}
     middle[-1], middle[1] = swap_if(near_in[16:24, :], far_in[16:24, :])
@@ -618,7 +695,7 @@
 
 
 def on_device(populations, solid_mask, centers, tile_lists, sphere_state, destination, relax_rates):
-    held, walls, keep, give, info, inner, outer, meta = pl.pallas_call(
+    held, walls, keep, give, info, inner, outer, border, meta = pl.pallas_call(
         collide_kernel,
         out_shape=(
             f32(19, GROUPS, 8, COLS),
@@ -628,14 +705,15 @@
             f32(8, COLS),
             f32(EDGE_ROWS, COLS),
             f32(EDGE_ROWS, COLS),
+            f32(16, COLS),
             f32(8, COLS),
         ),
         in_specs=[HBM] * 7,
-        out_specs=(VMEM,) * 8,
+        out_specs=(VMEM,) * 9,
         scratch_shapes=[
             pltpu.VMEM((19, GROUPS, 8, COLS), jnp.float32),
             pltpu.VMEM((GROUPS, 8, COLS), jnp.int32),
-            pltpu.VMEM((SLOTS, 8), jnp.float32),
+            pltpu.SMEM((SLOTS, 8), jnp.float32),
             pltpu.SMEM((3, SLOTS), jnp.int32),
             pltpu.SMEM((4, 16), jnp.int32),
             pltpu.SMEM((SLOTS,), jnp.int32),
@@ -665,22 +743,45 @@
     spheres = [chip, near[16:24], near_2, far[16:32]]
     from_outer = swapped(jnp.concatenate([outer, near[0:8], far[8:16]] + spheres), -1)
     from_inner = swapped(jnp.concatenate(spheres), 3)
+    walls = walls.reshape(PLANES, ROWS, COLS)
+    streamed, z_part, y_part = pl.pallas_call(
+        stream_kernel,
+        out_shape=(
+            f32(19, PLANES, ROWS, COLS),
+            f32(10, PLANES, ROWS, COLS),
+            f32(6, PLANES, 8, COLS),
+        ),
+        in_specs=[VMEM] * 2,
+        out_specs=(HBM, VMEM, VMEM),
+        scratch_shapes=[
+            pltpu.VMEM((19, PLANES, ROWS + 16, COLS), jnp.float32),
+            pltpu.VMEM((11, PLANES, ROWS, COLS), jnp.float32),
+            pltpu.SemaphoreType.DMA((2,)),
+        ],
+        compiler_params=pltpu.CompilerParams(vmem_limit_bytes=32 * 1024 * 1024),
+        cost_estimate=pl.CostEstimate(flops=4_000_000, bytes_accessed=4_000_000, transcendentals=0),
+        name="stream",
+    )(held.reshape(19, PLANES, ROWS, COLS), walls)
     populations_next, forces, state_next = pl.pallas_call(
         update_kernel,
         out_shape=(f32(19, PLANES, ROWS, COLS), f32(SLOTS, 6), f32(SLOTS, 8)),
-        in_specs=[VMEM] * 10,
+        in_specs=[HBM] + [VMEM] * 12,
         out_specs=(HBM, VMEM, VMEM),
         scratch_shapes=[
-            pltpu.VMEM((19, PLANES, ROWS + 16, COLS), jnp.float32),
             pltpu.VMEM((COLS, COLS), jnp.float32),
-            pltpu.VMEM((19, PLANES, ROWS, COLS), jnp.float32),
-            pltpu.SemaphoreType.DMA((PLANES,)),
+            pltpu.VMEM((10, PLANES, ROWS, COLS), jnp.float32),
+            pltpu.VMEM((6, PLANES, 8, COLS), jnp.float32),
+            pltpu.SemaphoreType.DMA((9,)),
         ],
+        input_output_aliases={0: 0},
         compiler_params=pltpu.CompilerParams(vmem_limit_bytes=32 * 1024 * 1024),
         name="update",
     )(
-        held.reshape(19, PLANES, ROWS, COLS),
-        walls.reshape(PLANES, ROWS, COLS),
+        in_hbm(streamed),
+        z_part,
+        y_part,
+        walls,
+        border,
         meta,
         chip,
         partner[16:40],

time: 27.9 us -> 27 us (0.968); the launches traced: 27.6 us -> 27 us
  waiting for transfers between devices: 5.25 us -> 4.61 us
    pallas_call x0 -> x1, Pallas kernels: none -> 1.03 us  [on_device(): pl.pallas_call(stream_kernel, out_shape=(f32(19, PLANES, ROWS, COLS), f32...]
    pallas_call x1, Pallas kernels: 4.83 us -> 3.82 us  [on_device(): pl.pallas_call(collide_kernel, out_shape=(f32(19, GROUPS, 8, COLS), f32(G...]
    ppermute x4, waiting for transfers between devices: 3.63 us -> 3.01 us  [swapped(): return lax.ppermute(block, 'gy', route)]
  transfers between devices with their start and end apart: 6 -> 6, of which waited for: 4 -> 4; matrix products, arithmetic and copies ran while one was open for 0% -> 0% of each run, Pallas kernels for 0% -> 4%
where the time goes in v3:
time: 27 us
  starting transfers between devices  14.5 us (54%)
  Pallas kernels  7.18 us (27%)
  waiting for transfers between devices  4.61 us (17%)
  between operations  0.68 us (3%)
    ppermute x4, starting transfers between devices, swapped(): return lax.ppermute(block, 'gy', route)  8.56 us
    ppermute x2, starting transfers between devices, spread(): return lax.ppermute(block, ('gy', 'gz'), route)  5.98 us
    pallas_call x1, Pallas kernels, on_device(): pl.pallas_call(collide_kernel, out_shape=(f32(19, GROUPS, 8, COLS), f32(G...  3.82 us
    ppermute x4, waiting for transfers between devices, swapped(): return lax.ppermute(block, 'gy', route)  3.01 us
    pallas_call x1, Pallas kernels, on_device(): pl.pallas_call(update_kernel, out_shape=(f32(19, PLANES, ROWS, COLS), f32...  2.32 us
    ppermute x2, waiting for transfers between devices, spread(): return lax.ppermute(block, ('gy', 'gz'), route)  1.6 us
    pallas_call x1, Pallas kernels, on_device(): pl.pallas_call(stream_kernel, out_shape=(f32(19, PLANES, ROWS, COLS), f32...  1.03 us
  transfers between devices with their start and end apart: 6, of which 4 were waited for; matrix products, arithmetic and copies ran while one was open for 0% of the time, Pallas kernels for 4%

profile of v3, /device:TPU:1, one launch (start us, length us, event | category | flops | bytes accessed | tf_op | source)
XLA Modules:
  0.0 27.0 jit_solution(15260840361428253834)
XLA Ops:
  0.6 3.8 %collide.1 = (f32[19,16,8,128]{3,2,1,0:T(8,128)S(1)}, f32[16,8,128]{2,1,0:T(8,128)S(1)}, f32[8,128]{1,0:T(8,128)S(1)}, f32[8,128]{1,0:T(8,128)S(1)}, f32[8,128]{...) custom-call(f32[19,16,8,128]{3,2,1,0:T(8,128)} %bitcast.11, ...), custom_call_target="tpu_custom_call" | custom-call | tf_op jit(solution)/shard_map/collide/pallas_call | solution.py:698
  4.5 1.5 %collective-permute-start = (f32[40,128]{1,0:T(8,128)S(1)}, f32[40,128]{1,0:T(8,128)S(1)}, u32[]{:S(2)}, u32[]{:S(2)}) collective-permute-start(f32[40,128]{1,0:T(8,128)S(1)} %pad_maximum_fusion), channel_id=1, source_target_pairs={{0,16},{16,0},{32,48},{48,32},{64,80},{80,64},{96,112},{112,96},{1... | collective-permute-start | bytes 61448 | tf_op jit(solution)/shard_map/ppermute | solution.py:685
  5.9 0.8 %collective-permute-done = f32[40,128]{1,0:T(8,128)S(1)} collective-permute-done((f32[40,128]{1,0:T(8,128)S(1)}, f32[40,128]{1,0:T(8,128)S(1)}, u32[]{:S(2)}, u32[]{:S(2)}) %collective-permute-start) | collective-permute-done | bytes 20512 | tf_op jit(solution)/shard_map/ppermute | solution.py:685
  6.8 5.0 %collective-permute-start.2 = (f32[8,128]{1,0:T(8,128)S(1)}, f32[8,128]{1,0:T(8,128)S(1)}, u32[]{:S(2)}, u32[]{:S(2)}) collective-permute-start(f32[8,128]{1,0:T(8,128)S(1)} %get-tuple-element.34.chip), channel_id=1, source_target_pairs={{0,2},{1,3},{2,4},{3,5},{4,6},{5,7},{6,8},{7,9},{8,10},{9,11},{10,... | collective-permute-start | bytes 12296 | tf_op jit(solution)/shard_map/ppermute | solution.py:694
  11.8 0.9 %collective-permute-start.1 = (f32[24,128]{1,0:T(8,128)S(1)}, f32[24,128]{1,0:T(8,128)S(1)}, u32[]{:S(2)}, u32[]{:S(2)}) collective-permute-start(f32[24,128]{1,0:T(8,128)S(1)} %pad_maximum_fusion.3), channel_id=1, source_target_pairs={{0,1},{1,2},{2,3},{3,4},{4,5},{5,6},{6,7},{7,8},{8,9},{9,10},{10,1... | collective-permute-start | bytes 36872 | tf_op jit(solution)/shard_map/ppermute | solution.py:694
  12.8 0.0 collective-permute-done.2.near_2
  12.8 1.6 %collective-permute-done.1.near_in = f32[24,128]{1,0:T(8,128)S(1)} collective-permute-done((f32[24,128]{1,0:T(8,128)S(1)}, f32[24,128]{1,0:T(8,128)S(1)}, u32[]{:S(2)}, u32[]{:S(2)}) %collective-permute-start.1) | collective-permute-done | bytes 12320 | tf_op jit(solution)/shard_map/ppermute | solution.py:694
  14.4 2.7 %collective-permute-start.3 = (f32[32,128]{1,0:T(8,128)S(1)}, f32[32,128]{1,0:T(8,128)S(1)}, u32[]{:S(2)}, u32[]{:S(2)}) collective-permute-start(f32[32,128]{1,0:T(8,128)S(1)} %pad_maximum_fusion.2), channel_id=1, source_target_pairs={{0,16},{16,0},{32,48},{48,32},{64,80},{80,64},{96,112},{112,96},{1... | collective-permute-start | bytes 49160 | tf_op jit(solution)/shard_map/ppermute | solution.py:685
  17.1 0.8 %collective-permute-done.3.far_in = f32[32,128]{1,0:T(8,128)S(1)} collective-permute-done((f32[32,128]{1,0:T(8,128)S(1)}, f32[32,128]{1,0:T(8,128)S(1)}, u32[]{:S(2)}, u32[]{:S(2)}) %collective-permute-start.3) | collective-permute-done | bytes 16416 | tf_op jit(solution)/shard_map/ppermute | solution.py:685
  18.0 2.3 %collective-permute-start.4 = (f32[80,128]{1,0:T(8,128)S(1)}, f32[80,128]{1,0:T(8,128)S(1)}, u32[]{:S(2)}, u32[]{:S(2)}) collective-permute-start(f32[80,128]{1,0:T(8,128)S(1)} %get-tuple-element.36), channel_id=1, source_target_pairs={{0,112},{16,32},{32,16},{48,64},{64,48},{80,96},{96,80},{112,0},{1... | collective-permute-start | bytes 122888 | tf_op jit(solution)/shard_map/ppermute | solution.py:685
  20.3 2.0 %collective-permute-start.5 = (f32[40,128]{1,0:T(8,128)S(1)}, f32[40,128]{1,0:T(8,128)S(1)}, u32[]{:S(2)}, u32[]{:S(2)}) collective-permute-start(f32[40,128]{1,0:T(8,128)S(1)} %pad_maximum_fusion.1), channel_id=1, source_target_pairs={{0,48},{16,96},{32,80},{48,0},{64,112},{80,32},{96,16},{112,64},{1... | collective-permute-start | bytes 61448 | tf_op jit(solution)/shard_map/ppermute | solution.py:685
  22.3 1.0 %stream.1 = (f32[19,4,32,128]{3,2,1,0:T(8,128)}, f32[10,4,32,128]{3,2,1,0:T(8,128)S(1)}, f32[6,4,8,128]{3,2,1,0:T(8,128)S(1)}) custom-call(f32[19,4,32,128]{3,2,1,0:T(8,128)S(1)} %bitcast.8, f32[4,32,128]{2,1,0:T(8,128)S(1)} %bitcast.9), custom_call_target="tpu_custom_call" | custom-call | flops 4000000 | bytes 4000000 | tf_op jit(solution)/shard_map/stream/pallas_call | solution.py:747
  23.4 1.3 %collective-permute-done.5.inner_in = f32[40,128]{1,0:T(8,128)S(1)} collective-permute-done((f32[40,128]{1,0:T(8,128)S(1)}, f32[40,128]{1,0:T(8,128)S(1)}, u32[]{:S(2)}, u32[]{:S(2)}) %collective-permute-start.5) | collective-permute-done | bytes 20512 | tf_op jit(solution)/shard_map/ppermute | solution.py:685
  24.7 0.0 collective-permute-done.4.outer_in
  24.7 2.3 %update.1 = (f32[19,4,32,128]{3,2,1,0:T(8,128)}, f32[4,6]{1,0:T(4,128)}, f32[4,8]{1,0:T(4,128)}) custom-call(f32[19,4,32,128]{3,2,1,0:T(8,128)} %get-tuple-element.20.streamed, f32[10,4,32,128]{3,2,1,0:T(8,128)S(1)} %get-tuple-element.21.z_part, f32[6,4,8,128]{3,2,1,0:T(8,128)S(1)} %get-tuple-element.22.y_part, ...), custom_call_target="tpu_custom_call", output_to_operand_aliasing={{0}: (0, {})} | custom-call | tf_op jit(solution)/shard_map/update/pallas_call | solution.py:765
  (13 shorter events, 0.0 us)
Async XLA Ops:
  4.5 2.3 %collective-permute-start = (f32[40,128]{1,0:T(8,128)S(1)}, f32[40,128]{1,0:T(8,128)S(1)}, u32[]{:S(2)}, u32[]{:S(2)}) collective-permute-start(f32[40,128]{1,0:T(8,128)S(1)} %pad_maximum_fusion), channel_id=1, source_target_pairs={{0,16},{16,0},{32,48},{48,32},{64,80},{80,64},{96,112},{112,96},{1... | collective-permute-start | bytes 61448 | tf_op jit(solution)/shard_map/ppermute | solution.py:685
  6.8 6.0 %collective-permute-start.2 = (f32[8,128]{1,0:T(8,128)S(1)}, f32[8,128]{1,0:T(8,128)S(1)}, u32[]{:S(2)}, u32[]{:S(2)}) collective-permute-start(f32[8,128]{1,0:T(8,128)S(1)} %get-tuple-element.34.chip), channel_id=1, source_target_pairs={{0,2},{1,3},{2,4},{3,5},{4,6},{5,7},{6,8},{7,9},{8,10},{9,11},{10,... | collective-permute-start | bytes 12296 | tf_op jit(solution)/shard_map/ppermute | solution.py:694
  11.8 2.5 %collective-permute-start.1 = (f32[24,128]{1,0:T(8,128)S(1)}, f32[24,128]{1,0:T(8,128)S(1)}, u32[]{:S(2)}, u32[]{:S(2)}) collective-permute-start(f32[24,128]{1,0:T(8,128)S(1)} %pad_maximum_fusion.3), channel_id=1, source_target_pairs={{0,1},{1,2},{2,3},{3,4},{4,5},{5,6},{6,7},{7,8},{8,9},{9,10},{10,1... | collective-permute-start | bytes 36872 | tf_op jit(solution)/shard_map/ppermute | solution.py:694
  14.4 3.6 %collective-permute-start.3 = (f32[32,128]{1,0:T(8,128)S(1)}, f32[32,128]{1,0:T(8,128)S(1)}, u32[]{:S(2)}, u32[]{:S(2)}) collective-permute-start(f32[32,128]{1,0:T(8,128)S(1)} %pad_maximum_fusion.2), channel_id=1, source_target_pairs={{0,16},{16,0},{32,48},{48,32},{64,80},{80,64},{96,112},{112,96},{1... | collective-permute-start | bytes 49160 | tf_op jit(solution)/shard_map/ppermute | solution.py:685
  18.0 6.8 %collective-permute-start.4 = (f32[80,128]{1,0:T(8,128)S(1)}, f32[80,128]{1,0:T(8,128)S(1)}, u32[]{:S(2)}, u32[]{:S(2)}) collective-permute-start(f32[80,128]{1,0:T(8,128)S(1)} %get-tuple-element.36), channel_id=1, source_target_pairs={{0,112},{16,32},{32,16},{48,64},{64,48},{80,96},{96,80},{112,0},{1... | collective-permute-start | bytes 122888 | tf_op jit(solution)/shard_map/ppermute | solution.py:685
  20.3 4.4 %collective-permute-start.5 = (f32[40,128]{1,0:T(8,128)S(1)}, f32[40,128]{1,0:T(8,128)S(1)}, u32[]{:S(2)}, u32[]{:S(2)}) collective-permute-start(f32[40,128]{1,0:T(8,128)S(1)} %pad_maximum_fusion.1), channel_id=1, source_target_pairs={{0,48},{16,96},{32,80},{48,0},{64,112},{80,32},{96,16},{112,64},{1... | collective-permute-start | bytes 61448 | tf_op jit(solution)/shard_map/ppermute | solution.py:685

commit v4 on v3

--- a/solution.py
+++ b/solution.py
@@ -213,7 +213,7 @@
     return new
 
 
-def sphere_partial(coll, center_x, center_y, center_z, row_f, lane_f):
+def sphere_partial(coll, partial, at, center_x, center_y, center_z, row_f, lane_f):
     first = jnp.maximum(lax.shift_right_arithmetic(center_y - (RADIUS + 1), 3), 0)
     last = jnp.minimum(lax.shift_right_arithmetic(center_y + (RADIUS + 1), 3), ROWS // 8 - 1)
     x_f = center_x.astype(jnp.float32)
@@ -270,10 +270,15 @@
         )
 
     sums = lax.fori_loop(first, last + 1, row_tile, (zero,) * 6)
-    packed = zero
     for j in range(6):
-        packed = jnp.where(row_f == float(j), jnp.sum(sums[j], axis=0, keepdims=True), packed)
-    return packed
+        partial[at, j] = sums[j]
+
+
+def summed(partial, at, row_f):
+    packed = jnp.zeros((8, COLS), jnp.float32)
+    for j in range(6):
+        packed = jnp.where(row_f == float(j), jnp.sum(partial[at, j], axis=0, keepdims=True), packed)
+    return 2.0 * jnp.sum(packed, axis=1, keepdims=True)
 
 
 def collide_kernel(
@@ -391,20 +396,33 @@
         outer[20 + t : 21 + t, :] = jnp.where(first, down, up)
 
     def own(s, _):
-        partial[s] = sphere_partial(
-            coll, centers[0, s], centers[1, s] & (ROWS - 1), centers[2, s] & (COLS - 1), row_f, lane_f
+        sphere_partial(
+            coll,
+            partial,
+            s,
+            centers[0, s],
+            centers[1, s] & (ROWS - 1),
+            centers[2, s] & (COLS - 1),
+            row_f,
+            lane_f,
         )
         return 0
 
+    partial[SLOTS:] = jnp.zeros((16, 6, 8, COLS), jnp.float32)
     lax.fori_loop(0, SLOTS, own, 0)
 
     def listed(r, _):
-        partial[SLOTS + r] = jnp.zeros((8, COLS), jnp.float32)
-
         @pl.when(lists[0, r] >= 0)
         def _():
-            partial[SLOTS + r] = sphere_partial(
-                coll, lists[3, r], lists[1, r] + TILE // 2, lists[2, r] + TILE // 2, row_f, lane_f
+            sphere_partial(
+                coll,
+                partial,
+                SLOTS + r,
+                lists[3, r],
+                lists[1, r] + TILE // 2,
+                lists[2, r] + TILE // 2,
+                row_f,
+                lane_f,
             )
 
         return 0
@@ -414,7 +432,7 @@
     base = core * HALF
     tile = jnp.zeros((8, COLS), jnp.float32)
     for s in range(SLOTS):
-        total = 2.0 * jnp.sum(partial[s], axis=1, keepdims=True)
+        total = summed(partial, s, row_f)
         tile = jnp.where(lane == base + 4 * SLOTS + s, total, tile)
         column = jnp.zeros((8, COLS), jnp.float32)
         for r in range(8):
@@ -424,19 +442,61 @@
     for r in range(16):
         offset = DIRECTIONS[r // 2]
         block = (offset[0] + 1) * 3 + offset[1] + 1
-        total = 2.0 * jnp.sum(partial[SLOTS + r], axis=1, keepdims=True)
+        total = summed(partial, SLOTS + r, row_f)
         slot = lists[0, r]
         at = jnp.where(slot >= 0, base + block * SLOTS + slot, -1)
         tile = jnp.where(lane == at, total, tile)
     info[...] = tile
 
 
-Z_ALL = (5, 6, 11, 12, 13, 14, 15, 16, 17, 18)
-Y_ONLY = (3, 4, 7, 8, 9, 10)
-
-
-def stream_kernel(held, walls, out_hbm, z_part, y_part, ext, out, sems):
+Y_ALL = (3, 4, 7, 8, 9, 10, 15, 16, 17, 18)
+
+
+def select_by(meta):
+    second = jnp.broadcast_to(meta[1:2, :], (8, COLS)) > 0.5
+
+    def swap_if(a, b):
+        return jnp.where(second, b, a), jnp.where(second, a, b)
+
+    return second, swap_if
+
+
+def walled(values):
+    return jnp.where(values[5:6, :] > 0.5, jnp.inf, values)
+
+
+def stream_kernel(
+    held, walls, border, meta, near_in, far_in, out_hbm, y_part, ext, turn, out, sems
+):
     wall = jnp.inf
+    _, swap_if = select_by(meta)
+    lane = lax.broadcasted_iota(jnp.int32, (8, COLS), 1)
+    sub = lax.broadcasted_iota(jnp.int32, (8, COLS), 0)
+    row = lane & (ROWS - 1)
+    plane = lax.shift_right_logical(lane, 5)
+
+    def side(here, order):
+        total = here
+        for k, i in enumerate(order):
+            c_x, c_y, _ = VELOCITIES[i]
+            moved = here
+            if c_y == 1:
+                moved = jnp.where(row == 0, wall, pltpu.roll(here, 1, 1))
+            if c_y == -1:
+                moved = jnp.where(row == ROWS - 1, wall, pltpu.roll(here, COLS - 1, 1))
+            if c_x == 1:
+                moved = jnp.where(plane == 0, wall, pltpu.roll(here, 32, 1))
+            if c_x == -1:
+                moved = jnp.where(plane == PLANES - 1, wall, pltpu.roll(here, COLS - 32, 1))
+            total = jnp.where(sub == k, moved, total)
+        return total
+
+    west, east = swap_if(walled(near_in[0:8, :]), walled(far_in[8:16, :]))
+    turn[...] = jnp.zeros((COLS, COLS), jnp.float32)
+    turn[0:8, :] = side(west, Z_UP)
+    turn[8:16, :] = side(east, Z_DOWN)
+    turned = turn[...].T
+    turn[...] = turned
     column = lax.broadcasted_iota(jnp.int32, (ROWS, COLS), 1)
     for t in range(PLANES):
         solid = walls[t] > 0.5
@@ -447,6 +507,7 @@
                 ext[i, t, 7:8, :] = jnp.full((1, COLS), wall, jnp.float32)
             if c_y == -1:
                 ext[i, t, 8 + ROWS : 9 + ROWS, :] = jnp.full((1, COLS), wall, jnp.float32)
+    copies = []
     for t in range(PLANES):
         solid = walls[t] > 0.5
         for i in range(19):
@@ -454,36 +515,30 @@
             source = t - c_x
             if 0 <= source < PLANES:
                 pulled = ext[i, source, 8 - c_y : 8 - c_y + ROWS, :]
-                if c_z == 1:
-                    pulled = jnp.where(column == 0, wall, pltpu.roll(pulled, 1, 1))
-                if c_z == -1:
-                    pulled = jnp.where(column == COLS - 1, wall, pltpu.roll(pulled, COLS - 1, 1))
+                if c_z != 0:
+                    k = Z_UP.index(i) if c_z == 1 else 8 + Z_DOWN.index(i)
+                    pulled = jnp.where(
+                        column == (0 if c_z == 1 else COLS - 1),
+                        turn[t * ROWS : (t + 1) * ROWS, k : k + 1],
+                        pltpu.roll(pulled, 1 if c_z == 1 else COLS - 1, 1),
+                    )
                 fluid = jnp.where(pulled == wall, held[OPPOSITE[i], t], pulled)
             else:
                 fluid = held[OPPOSITE[i], t]
             result = jnp.where(solid, held[i, t], fluid)
-            if c_z == 0:
-                out[i, t] = result
-            else:
-                z_part[Z_ALL.index(i), t] = result
-            if i in Y_ONLY:
-                y_part[Y_ONLY.index(i), t] = result[0:8] if c_y == 1 else result[ROWS - 8 : ROWS]
-    copies = [
-        pltpu.make_async_copy(out.at[lo:hi], out_hbm.at[lo:hi], sems.at[k])
-        for k, (lo, hi) in enumerate(((0, 5), (7, 11)))
-    ]
-    for copy in copies:
-        copy.start()
+            out[i, t] = result
+            if i in Y_ALL:
+                y_part[Y_ALL.index(i), t] = result[0:8] if c_y == 1 else result[ROWS - 8 : ROWS]
+        copies.append(pltpu.make_async_copy(out.at[:, t], out_hbm.at[:, t], sems.at[t]))
+        copies[t].start()
     for copy in copies:
         copy.wait()
 
 
 def update_kernel(
     streamed,
-    z_part,
     y_part,
     walls,
-    border,
     meta,
     chip,
     partner_edge,
@@ -493,62 +548,25 @@
     outer_in,
     inner_in,
     out_hbm,
+    forces_hbm,
+    state_hbm,
+    turn,
+    y_new,
     forces,
     state_next,
-    turn,
-    z_new,
-    y_new,
     sems,
 ):
     del streamed
     lane = lax.broadcasted_iota(jnp.int32, (8, COLS), 1)
     sub = lax.broadcasted_iota(jnp.int32, (8, COLS), 0)
-    row = lane & (ROWS - 1)
-    plane = lax.shift_right_logical(lane, 5)
     wall = jnp.inf
-    second = jnp.broadcast_to(meta[1:2, :], (8, COLS)) > 0.5
-
-    def swap_if(a, b):
-        return jnp.where(second, b, a), jnp.where(second, a, b)
-
-    def walled(values):
-        return jnp.where(values[5:6, :] > 0.5, wall, values)
-
-    def side(here, below, above, shifts):
-        total = here
-        for k, (c_x, c_y) in enumerate(shifts):
-            moved = here
-            if c_y == 1:
-                moved = jnp.where(row == 0, pltpu.roll(below, COLS - 31, 1), pltpu.roll(here, 1, 1))
-            if c_y == -1:
-                moved = jnp.where(
-                    row == ROWS - 1, pltpu.roll(above, 31, 1), pltpu.roll(here, COLS - 1, 1)
-                )
-            if c_x == 1:
-                moved = jnp.where(plane == 0, wall, pltpu.roll(here, 32, 1))
-            if c_x == -1:
-                moved = jnp.where(plane == PLANES - 1, wall, pltpu.roll(here, COLS - 32, 1))
-            total = jnp.where(sub == k, moved, total)
-        return total
-
-    west, east = swap_if(walled(near_in[0:8, :]), walled(far_in[8:16, :]))
+    second, swap_if = select_by(meta)
     west_partner, east_partner = swap_if(walled(near_in[8:16, :]), walled(far_in[0:8, :]))
     west_outer, east_outer = swap_if(
         walled(outer_in[EDGE_ROWS + 8 : EDGE_ROWS + 16, :]), walled(outer_in[EDGE_ROWS : EDGE_ROWS + 8, :])
     )
     west_south, west_north = swap_if(west_outer, west_partner)
     east_south, east_north = swap_if(east_outer, east_partner)
-    low_solid = border[13:14, :] > 0.5
-    high_solid = border[5:6, :] > 0.5
-    turn[...] = jnp.zeros((COLS, COLS), jnp.float32)
-    turn[0:8, :] = jnp.where(
-        low_solid, wall, side(west, west_south, west_north, [VELOCITIES[i][:2] for i in Z_UP])
-    )
-    turn[8:16, :] = jnp.where(
-        high_solid, wall, side(east, east_south, east_north, [VELOCITIES[i][:2] for i in Z_DOWN])
-    )
-    turned = turn[...].T
-    turn[...] = turned
     pairs = [
         swap_if(outer_in[k : k + 8, :], partner_edge[k : k + 8, :]) for k in range(0, EDGE_ROWS, 8)
     ]
@@ -558,19 +576,6 @@
     def edge_row(edge, r):
         return edge[r // 8][r % 8 : r % 8 + 1, :]
 
-    def border_row(i, t):
-        c_x, c_y, _ = VELOCITIES[i]
-        edge, order, cells = (
-            (south, Y_UP, walls[t, 0:1, :]) if c_y == 1 else (north, Y_DOWN, walls[t, ROWS - 1 : ROWS, :])
-        )
-        values = edge_row(edge, order.index(i) * 4 + t - c_x)
-        return jnp.where(edge_row(edge, 20 + t - c_x) > 0.5, wall, values), cells > 0.5
-
-    def mended(tile, i, values):
-        changed = (sub == (0 if VELOCITIES[i][1] == 1 else 7)) & (values != wall)
-        return jnp.where(changed, values, tile)
-
-    column = lax.broadcasted_iota(jnp.int32, (ROWS, COLS), 1)
     first_lane = lax.broadcasted_iota(jnp.int32, (1, COLS), 1)
     copies = []
 
@@ -578,34 +583,32 @@
         copies.append(pltpu.make_async_copy(source, target, sems.at[len(copies)]))
         copies[-1].start()
 
-    for z, i in enumerate(Z_ALL):
-        _, c_y, c_z = VELOCITIES[i]
-        k = Z_UP.index(i) if c_z == 1 else 8 + Z_DOWN.index(i)
-        edge = 0 if c_z == 1 else COLS - 1
+    for y, i in enumerate(Y_ALL):
+        c_x, c_y, c_z = VELOCITIES[i]
+        edge, order = (south, Y_UP) if c_y == 1 else (north, Y_DOWN)
         for t in range(PLANES):
-            entering = turn[t * ROWS : (t + 1) * ROWS, k : k + 1]
-            values = jnp.where((column == edge) & (entering != wall), entering, z_part[z, t])
-            z_new[z, t] = values
-            if c_y != 0:
-                values_in, solid = border_row(i, t)
-                values_in = pltpu.roll(values_in, 1 if c_z == 1 else COLS - 1, 1)
-                values_in = jnp.where(solid | (first_lane == edge), wall, values_in)
-                at = 0 if c_y == 1 else ROWS - 8
-                z_new[z, t, at : at + 8, :] = mended(values[at : at + 8], i, values_in)
-        if z == 1:
-            send(z_new.at[0:2], out_hbm.at[5:7])
-        if z == 5:
-            send(z_new.at[2:6], out_hbm.at[11:15])
-        if z == 9:
-            send(z_new.at[6:10], out_hbm.at[15:19])
-    for y, i in enumerate(Y_ONLY):
-        c_x, c_y, _ = VELOCITIES[i]
-        for t in range(PLANES):
-            tile = y_part[y, t]
-            if 0 <= t - c_x < PLANES:
-                values_in, solid = border_row(i, t)
-                tile = mended(tile, i, jnp.where(solid, wall, values_in))
-            y_new[y, t] = tile
+            source = t - c_x
+            if not 0 <= source < PLANES:
+                y_new[y, t] = y_part[y, t]
+                continue
+            values = edge_row(edge, order.index(i) * 4 + source)
+            values = jnp.where(edge_row(edge, 20 + source) > 0.5, wall, values)
+            if c_z != 0:
+                if c_z == 1:
+                    corner, k = (west_south if c_y == 1 else west_north), Z_UP.index(i)
+                else:
+                    corner, k = (east_south if c_y == 1 else east_north), Z_DOWN.index(i)
+                at = t * ROWS + (ROWS - 1 if c_y == 1 else 0)
+                to = 0 if c_z == 1 else COLS - 1
+                values = jnp.where(
+                    first_lane == to,
+                    pltpu.roll(corner, (to - at) % COLS, 1)[k : k + 1, :],
+                    pltpu.roll(values, 1 if c_z == 1 else COLS - 1, 1),
+                )
+            cells = walls[t, 0:1, :] if c_y == 1 else walls[t, ROWS - 1 : ROWS, :]
+            values = jnp.where(cells > 0.5, wall, values)
+            changed = (sub == (0 if c_y == 1 else 7)) & (values != wall)
+            y_new[y, t] = jnp.where(changed, values, y_part[y, t])
         at = 0 if c_y == 1 else ROWS - 8
         send(y_new.at[y], out_hbm.at[i, :, at : at + 8])
 
@@ -663,6 +666,8 @@
     turned = turn[...].T
     state_next[...] = turned[0:SLOTS, 0:8]
     forces[...] = turned[0:SLOTS, 8:14]
+    send(state_next, state_hbm)
+    send(forces, forces_hbm)
     for copy in copies:
         copy.wait()
 
@@ -721,7 +726,7 @@
             pltpu.VMEM((19, GROUPS, 8, COLS), jnp.float32),
             pltpu.VMEM((N_COEF, 8, COLS), jnp.float32),
             pltpu.VMEM((COLS, COLS), jnp.float32),
-            pltpu.VMEM((20, 8, COLS), jnp.float32),
+            pltpu.VMEM((20, 6, 8, COLS), jnp.float32),
             pltpu.SemaphoreType.DMA((10,)),
         ],
         compiler_params=pltpu.CompilerParams(vmem_limit_bytes=32 * 1024 * 1024),
@@ -744,44 +749,40 @@
     from_outer = swapped(jnp.concatenate([outer, near[0:8], far[8:16]] + spheres), -1)
     from_inner = swapped(jnp.concatenate(spheres), 3)
     walls = walls.reshape(PLANES, ROWS, COLS)
-    streamed, z_part, y_part = pl.pallas_call(
+    streamed, y_part = pl.pallas_call(
         stream_kernel,
-        out_shape=(
-            f32(19, PLANES, ROWS, COLS),
-            f32(10, PLANES, ROWS, COLS),
-            f32(6, PLANES, 8, COLS),
-        ),
-        in_specs=[VMEM] * 2,
-        out_specs=(HBM, VMEM, VMEM),
+        out_shape=(f32(19, PLANES, ROWS, COLS), f32(10, PLANES, 8, COLS)),
+        in_specs=[VMEM] * 6,
+        out_specs=(HBM, VMEM),
         scratch_shapes=[
             pltpu.VMEM((19, PLANES, ROWS + 16, COLS), jnp.float32),
-            pltpu.VMEM((11, PLANES, ROWS, COLS), jnp.float32),
-            pltpu.SemaphoreType.DMA((2,)),
+            pltpu.VMEM((COLS, COLS), jnp.float32),
+            pltpu.VMEM((19, PLANES, ROWS, COLS), jnp.float32),
+            pltpu.SemaphoreType.DMA((PLANES,)),
         ],
         compiler_params=pltpu.CompilerParams(vmem_limit_bytes=32 * 1024 * 1024),
         cost_estimate=pl.CostEstimate(flops=4_000_000, bytes_accessed=4_000_000, transcendentals=0),
         name="stream",
-    )(held.reshape(19, PLANES, ROWS, COLS), walls)
+    )(held.reshape(19, PLANES, ROWS, COLS), walls, border, meta, near, far)
     populations_next, forces, state_next = pl.pallas_call(
         update_kernel,
         out_shape=(f32(19, PLANES, ROWS, COLS), f32(SLOTS, 6), f32(SLOTS, 8)),
-        in_specs=[HBM] + [VMEM] * 12,
-        out_specs=(HBM, VMEM, VMEM),
+        in_specs=[HBM] + [VMEM] * 10,
+        out_specs=(HBM, HBM, HBM),
         scratch_shapes=[
             pltpu.VMEM((COLS, COLS), jnp.float32),
-            pltpu.VMEM((10, PLANES, ROWS, COLS), jnp.float32),
-            pltpu.VMEM((6, PLANES, 8, COLS), jnp.float32),
-            pltpu.SemaphoreType.DMA((9,)),
+            pltpu.VMEM((10, PLANES, 8, COLS), jnp.float32),
+            pltpu.VMEM((SLOTS, 6), jnp.float32),
+            pltpu.VMEM((SLOTS, 8), jnp.float32),
+            pltpu.SemaphoreType.DMA((12,)),
         ],
         input_output_aliases={0: 0},
         compiler_params=pltpu.CompilerParams(vmem_limit_bytes=32 * 1024 * 1024),
         name="update",
     )(
         in_hbm(streamed),
-        z_part,
         y_part,
         walls,
-        border,
         meta,
         chip,
         partner[16:40],

time: 27 us -> 25.9 us (0.959)
  Pallas kernels: 7.18 us -> 6.33 us
  waiting for transfers between devices: 4.61 us -> 3.85 us
  starting transfers between devices: 14.5 us -> 15 us
    pallas_call x1, Pallas kernels: 2.32 us -> 1.15 us  [on_device(): pl.pallas_call(update_kernel, out_shape=(f32(19, PLANES, ROWS, COLS), f32...]
    ppermute x4, waiting for transfers between devices: 3.01 us -> 2.37 us  [swapped(): return lax.ppermute(block, 'gy', route)]
    pallas_call x1, Pallas kernels: 1.03 us -> 1.55 us  [on_device(): pl.pallas_call(stream_kernel, out_shape=(f32(19, PLANES, ROWS, COLS), f32...]
    ppermute x4, starting transfers between devices: 8.56 us -> 8.86 us  [swapped(): return lax.ppermute(block, 'gy', route)]
  transfers between devices with their start and end apart: 6 -> 6, of which waited for: 4 -> 4; matrix products, arithmetic and copies ran while one was open for 0% -> 0% of each run, Pallas kernels for 4% -> 6%
where the time goes in v4:
time: 25.9 us
  starting transfers between devices  15 us (58%)
  Pallas kernels  6.33 us (24%)
  waiting for transfers between devices  3.85 us (15%)
  between operations  0.67 us (3%)
    ppermute x4, starting transfers between devices, swapped(): return lax.ppermute(block, 'gy', route)  8.86 us
    ppermute x2, starting transfers between devices, spread(): return lax.ppermute(block, ('gy', 'gz'), route)  6.14 us
    pallas_call x1, Pallas kernels, on_device(): pl.pallas_call(collide_kernel, out_shape=(f32(19, GROUPS, 8, COLS), f32(G...  3.63 us
    ppermute x4, waiting for transfers between devices, swapped(): return lax.ppermute(block, 'gy', route)  2.37 us
    pallas_call x1, Pallas kernels, on_device(): pl.pallas_call(stream_kernel, out_shape=(f32(19, PLANES, ROWS, COLS), f32...  1.55 us
    ppermute x2, waiting for transfers between devices, spread(): return lax.ppermute(block, ('gy', 'gz'), route)  1.48 us
    pallas_call x1, Pallas kernels, on_device(): pl.pallas_call(update_kernel, out_shape=(f32(19, PLANES, ROWS, COLS), f32...  1.15 us
  transfers between devices with their start and end apart: 6, of which 4 were waited for; matrix products, arithmetic and copies ran while one was open for 0% of the time, Pallas kernels for 6%

profile of v4, /device:TPU:1, one launch (start us, length us, event | category | flops | bytes accessed | tf_op | source)
XLA Modules:
  0.0 25.9 jit_solution(13111427618648543711)
XLA Ops:
  0.6 3.6 %collide.1 = (f32[19,16,8,128]{3,2,1,0:T(8,128)S(1)}, f32[16,8,128]{2,1,0:T(8,128)S(1)}, f32[8,128]{1,0:T(8,128)S(1)}, f32[8,128]{1,0:T(8,128)S(1)}, f32[8,128]{...) custom-call(f32[19,16,8,128]{3,2,1,0:T(8,128)} %bitcast.11, ...), custom_call_target="tpu_custom_call" | custom-call | tf_op jit(solution)/shard_map/collide/pallas_call | solution.py:703
  4.3 1.7 %collective-permute-start = (f32[40,128]{1,0:T(8,128)S(1)}, f32[40,128]{1,0:T(8,128)S(1)}, u32[]{:S(2)}, u32[]{:S(2)}) collective-permute-start(f32[40,128]{1,0:T(8,128)S(1)} %pad_maximum_fusion), channel_id=1, source_target_pairs={{0,16},{16,0},{32,48},{48,32},{64,80},{80,64},{96,112},{112,96},{1... | collective-permute-start | bytes 61448 | tf_op jit(solution)/shard_map/ppermute | solution.py:690
  6.0 0.8 %collective-permute-done = f32[40,128]{1,0:T(8,128)S(1)} collective-permute-done((f32[40,128]{1,0:T(8,128)S(1)}, f32[40,128]{1,0:T(8,128)S(1)}, u32[]{:S(2)}, u32[]{:S(2)}) %collective-permute-start) | collective-permute-done | bytes 20512 | tf_op jit(solution)/shard_map/ppermute | solution.py:690
  6.8 5.1 %collective-permute-start.2 = (f32[8,128]{1,0:T(8,128)S(1)}, f32[8,128]{1,0:T(8,128)S(1)}, u32[]{:S(2)}, u32[]{:S(2)}) collective-permute-start(f32[8,128]{1,0:T(8,128)S(1)} %get-tuple-element.32.chip), channel_id=1, source_target_pairs={{0,2},{1,3},{2,4},{3,5},{4,6},{5,7},{6,8},{7,9},{8,10},{9,11},{10,... | collective-permute-start | bytes 12296 | tf_op jit(solution)/shard_map/ppermute | solution.py:699
  11.9 1.1 %collective-permute-start.1 = (f32[24,128]{1,0:T(8,128)S(1)}, f32[24,128]{1,0:T(8,128)S(1)}, u32[]{:S(2)}, u32[]{:S(2)}) collective-permute-start(f32[24,128]{1,0:T(8,128)S(1)} %pad_maximum_fusion.3), channel_id=1, source_target_pairs={{0,1},{1,2},{2,3},{3,4},{4,5},{5,6},{6,7},{7,8},{8,9},{9,10},{10,1... | collective-permute-start | bytes 36872 | tf_op jit(solution)/shard_map/ppermute | solution.py:699
  12.9 0.0 collective-permute-done.2.near_2
  12.9 1.5 %collective-permute-done.1.near_in = f32[24,128]{1,0:T(8,128)S(1)} collective-permute-done((f32[24,128]{1,0:T(8,128)S(1)}, f32[24,128]{1,0:T(8,128)S(1)}, u32[]{:S(2)}, u32[]{:S(2)}) %collective-permute-start.1) | collective-permute-done | bytes 12320 | tf_op jit(solution)/shard_map/ppermute | solution.py:699
  14.4 2.6 %collective-permute-start.3 = (f32[32,128]{1,0:T(8,128)S(1)}, f32[32,128]{1,0:T(8,128)S(1)}, u32[]{:S(2)}, u32[]{:S(2)}) collective-permute-start(f32[32,128]{1,0:T(8,128)S(1)} %pad_maximum_fusion.2), channel_id=1, source_target_pairs={{0,16},{16,0},{32,48},{48,32},{64,80},{80,64},{96,112},{112,96},{1... | collective-permute-start | bytes 49160 | tf_op jit(solution)/shard_map/ppermute | solution.py:690
  17.0 0.8 %collective-permute-done.3.far_in = f32[32,128]{1,0:T(8,128)S(1)} collective-permute-done((f32[32,128]{1,0:T(8,128)S(1)}, f32[32,128]{1,0:T(8,128)S(1)}, u32[]{:S(2)}, u32[]{:S(2)}) %collective-permute-start.3) | collective-permute-done | bytes 16416 | tf_op jit(solution)/shard_map/ppermute | solution.py:690
  17.9 2.4 %collective-permute-start.4 = (f32[80,128]{1,0:T(8,128)S(1)}, f32[80,128]{1,0:T(8,128)S(1)}, u32[]{:S(2)}, u32[]{:S(2)}) collective-permute-start(f32[80,128]{1,0:T(8,128)S(1)} %get-tuple-element.34), channel_id=1, source_target_pairs={{0,112},{16,32},{32,16},{48,64},{64,48},{80,96},{96,80},{112,0},{1... | collective-permute-start | bytes 122888 | tf_op jit(solution)/shard_map/ppermute | solution.py:690
  20.3 2.2 %collective-permute-start.5 = (f32[40,128]{1,0:T(8,128)S(1)}, f32[40,128]{1,0:T(8,128)S(1)}, u32[]{:S(2)}, u32[]{:S(2)}) collective-permute-start(f32[40,128]{1,0:T(8,128)S(1)} %pad_maximum_fusion.1), channel_id=1, source_target_pairs={{0,48},{16,96},{32,80},{48,0},{64,112},{80,32},{96,16},{112,64},{1... | collective-permute-start | bytes 61448 | tf_op jit(solution)/shard_map/ppermute | solution.py:690
  22.5 1.5 %stream.1 = (f32[19,4,32,128]{3,2,1,0:T(8,128)}, f32[10,4,8,128]{3,2,1,0:T(8,128)S(1)}) custom-call(f32[19,4,32,128]{3,2,1,0:T(8,128)S(1)} %bitcast.8, f32[4,32,128]{2,1,0:T(8,128)S(1)} %bitcast.9, f32[16,128]{1,0:T(8,128)S(1)} %get-tuple-element.19.border, f32[8,128]{1,0:T(8,128)S(1)} %get-tuple-element.20.meta, ...), custom_call_target="tpu_custom_call" | custom-call | flops 4000000 | bytes 4000000 | tf_op jit(solution)/shard_map/stream/pallas_call | solution.py:752
  24.0 0.7 %collective-permute-done.5.inner_in = f32[40,128]{1,0:T(8,128)S(1)} collective-permute-done((f32[40,128]{1,0:T(8,128)S(1)}, f32[40,128]{1,0:T(8,128)S(1)}, u32[]{:S(2)}, u32[]{:S(2)}) %collective-permute-start.5) | collective-permute-done | bytes 20512 | tf_op jit(solution)/shard_map/ppermute | solution.py:690
  24.7 0.0 collective-permute-done.4.outer_in
  24.7 1.2 %update.1 = (f32[19,4,32,128]{3,2,1,0:T(8,128)}, f32[4,6]{1,0:T(4,128)}, f32[4,8]{1,0:T(4,128)}) custom-call(f32[19,4,32,128]{3,2,1,0:T(8,128)} %get-tuple-element.25.streamed, f32[10,4,8,128]{3,2,1,0:T(8,128)S(1)} %get-tuple-element.26.y_part, f32[4,32,128]{2,1,0:T(8,128)S(1)} %bitcast.10, ...), custom_call_target="tpu_custom_call", output_to_operand_aliasing={{0}: (0, {})} | custom-call | tf_op jit(solution)/shard_map/update/pallas_call | solution.py:767
  (13 shorter events, 0.0 us)
Async XLA Ops:
  4.3 2.5 %collective-permute-start = (f32[40,128]{1,0:T(8,128)S(1)}, f32[40,128]{1,0:T(8,128)S(1)}, u32[]{:S(2)}, u32[]{:S(2)}) collective-permute-start(f32[40,128]{1,0:T(8,128)S(1)} %pad_maximum_fusion), channel_id=1, source_target_pairs={{0,16},{16,0},{32,48},{48,32},{64,80},{80,64},{96,112},{112,96},{1... | collective-permute-start | bytes 61448 | tf_op jit(solution)/shard_map/ppermute | solution.py:690
  6.8 6.1 %collective-permute-start.2 = (f32[8,128]{1,0:T(8,128)S(1)}, f32[8,128]{1,0:T(8,128)S(1)}, u32[]{:S(2)}, u32[]{:S(2)}) collective-permute-start(f32[8,128]{1,0:T(8,128)S(1)} %get-tuple-element.32.chip), channel_id=1, source_target_pairs={{0,2},{1,3},{2,4},{3,5},{4,6},{5,7},{6,8},{7,9},{8,10},{9,11},{10,... | collective-permute-start | bytes 12296 | tf_op jit(solution)/shard_map/ppermute | solution.py:699
  11.9 2.5 %collective-permute-start.1 = (f32[24,128]{1,0:T(8,128)S(1)}, f32[24,128]{1,0:T(8,128)S(1)}, u32[]{:S(2)}, u32[]{:S(2)}) collective-permute-start(f32[24,128]{1,0:T(8,128)S(1)} %pad_maximum_fusion.3), channel_id=1, source_target_pairs={{0,1},{1,2},{2,3},{3,4},{4,5},{5,6},{6,7},{7,8},{8,9},{9,10},{10,1... | collective-permute-start | bytes 36872 | tf_op jit(solution)/shard_map/ppermute | solution.py:699
  14.4 3.4 %collective-permute-start.3 = (f32[32,128]{1,0:T(8,128)S(1)}, f32[32,128]{1,0:T(8,128)S(1)}, u32[]{:S(2)}, u32[]{:S(2)}) collective-permute-start(f32[32,128]{1,0:T(8,128)S(1)} %pad_maximum_fusion.2), channel_id=1, source_target_pairs={{0,16},{16,0},{32,48},{48,32},{64,80},{80,64},{96,112},{112,96},{1... | collective-permute-start | bytes 49160 | tf_op jit(solution)/shard_map/ppermute | solution.py:690
  17.9 6.9 %collective-permute-start.4 = (f32[80,128]{1,0:T(8,128)S(1)}, f32[80,128]{1,0:T(8,128)S(1)}, u32[]{:S(2)}, u32[]{:S(2)}) collective-permute-start(f32[80,128]{1,0:T(8,128)S(1)} %get-tuple-element.34), channel_id=1, source_target_pairs={{0,112},{16,32},{32,16},{48,64},{64,48},{80,96},{96,80},{112,0},{1... | collective-permute-start | bytes 122888 | tf_op jit(solution)/shard_map/ppermute | solution.py:690
  20.3 4.4 %collective-permute-start.5 = (f32[40,128]{1,0:T(8,128)S(1)}, f32[40,128]{1,0:T(8,128)S(1)}, u32[]{:S(2)}, u32[]{:S(2)}) collective-permute-start(f32[40,128]{1,0:T(8,128)S(1)} %pad_maximum_fusion.1), channel_id=1, source_target_pairs={{0,48},{16,96},{32,80},{48,0},{64,112},{80,32},{96,16},{112,64},{1... | collective-permute-start | bytes 61448 | tf_op jit(solution)/shard_map/ppermute | solution.py:690

commit v5 on v4

--- a/solution.py
+++ b/solution.py
@@ -270,15 +270,10 @@
         )
 
     sums = lax.fori_loop(first, last + 1, row_tile, (zero,) * 6)
+    packed = zero
     for j in range(6):
-        partial[at, j] = sums[j]
-
-
-def summed(partial, at, row_f):
-    packed = jnp.zeros((8, COLS), jnp.float32)
-    for j in range(6):
-        packed = jnp.where(row_f == float(j), jnp.sum(partial[at, j], axis=0, keepdims=True), packed)
-    return 2.0 * jnp.sum(packed, axis=1, keepdims=True)
+        packed = jnp.where(row_f == float(j), jnp.sum(sums[j], axis=0, keepdims=True), packed)
+    partial[at] = packed
 
 
 def collide_kernel(
@@ -356,7 +351,7 @@
 
     for t in range(PLANES):
         large[t].wait()
-        lax.fori_loop(t * 4, t * 4 + 4, group, 0)
+        lax.fori_loop(t * 4, t * 4 + 4, group, 0, unroll=4)
     for copy in small[2:]:
         copy.wait()
 
@@ -373,15 +368,17 @@
     for g in range(GROUPS):
         edge = jnp.zeros((8, COLS), jnp.float32)
         for k in range(6):
-            values = coll[Z_UP[k], g] if k < 5 else walls[g]
-            edge = jnp.where(lane == k, pltpu.roll(values, k + 1, 1), edge)
-        for k in range(6):
-            values = coll[Z_DOWN[k], g] if k < 5 else walls[g]
-            edge = jnp.where(lane == 8 + k, pltpu.roll(values, 8 + k, 1), edge)
+            values = walls[g]
+            if k < 5:
+                values = jnp.where(lane == 0, coll[Z_DOWN[k], g], coll[Z_UP[k], g])
+            pair = lax.shift_right_logical(lane, 1) == k
+            edge = jnp.where(pair, pltpu.roll(values, 2 * k + 1, 1), edge)
         turn[g * 8 : g * 8 + 8, :] = edge
-    turned = turn[...].T
-    up_z, down_z = turned[0:8, :], turned[8:16, :]
-    border[...] = turned[0:16, :]
+    turn[...] = turn[...].T
+    up_z = turn[pl.ds(0, 8, stride=2), :]
+    down_z = turn[pl.ds(1, 8, stride=2), :]
+    border[0:8, :] = up_z
+    border[8:16, :] = down_z
     keep[...] = jnp.where(first, up_z, down_z)
     give[...] = jnp.where(first, down_z, up_z)
     for t in range(PLANES):
@@ -408,7 +405,7 @@
         )
         return 0
 
-    partial[SLOTS:] = jnp.zeros((16, 6, 8, COLS), jnp.float32)
+    partial[SLOTS:] = jnp.zeros((16, 8, COLS), jnp.float32)
     lax.fori_loop(0, SLOTS, own, 0)
 
     def listed(r, _):
@@ -432,7 +429,7 @@
     base = core * HALF
     tile = jnp.zeros((8, COLS), jnp.float32)
     for s in range(SLOTS):
-        total = summed(partial, s, row_f)
+        total = 2.0 * jnp.sum(partial[s], axis=1, keepdims=True)
         tile = jnp.where(lane == base + 4 * SLOTS + s, total, tile)
         column = jnp.zeros((8, COLS), jnp.float32)
         for r in range(8):
@@ -442,7 +439,7 @@
     for r in range(16):
         offset = DIRECTIONS[r // 2]
         block = (offset[0] + 1) * 3 + offset[1] + 1
-        total = summed(partial, SLOTS + r, row_f)
+        total = 2.0 * jnp.sum(partial[SLOTS + r], axis=1, keepdims=True)
         slot = lists[0, r]
         at = jnp.where(slot >= 0, base + block * SLOTS + slot, -1)
         tile = jnp.where(lane == at, total, tile)
@@ -633,39 +630,46 @@
         tiles[1, b] = jnp.where(second, jnp.where(low, turned_own, turned_after), middle[b])
         tiles[2, b] = jnp.where(second, turned_after, after)
 
-    def device_lanes(a, b, at):
-        shift = (COLS - (at + HALF * (a % 2))) % COLS
+    number = lax.shift_right_logical(lane, 2)
+    number_a = sum((number >= 3 * k).astype(jnp.int32) for k in (1, 2, 3)) - 1
+    number_b = number - 3 * (number_a + 1) - 1
+    listed = lane < 9 * SLOTS
+    near_a = {a: listed & (number_a >= a - 1) & (number_a <= a + 1) for a in range(-2, 3)}
+    near_b = {b: (number_b >= b - 1) & (number_b <= b + 1) for b in range(-2, 3)}
+
+    def device_lanes(a, b, shift):
+        shift = (shift - HALF * (a % 2)) % COLS
         part = tiles[(a + 2) // 2, b]
         return pltpu.roll(part, shift, 1) if shift else part
 
-    own_lanes = lane < SLOTS
-    picked = [jnp.zeros((8, COLS), jnp.float32) for _ in range(SLOTS)]
+    force = jnp.zeros((8, COLS), jnp.float32)
+    for a in range(-2, 3):
+        for b in range(-2, 3):
+            part = device_lanes(a, b, SLOTS * (3 * a + b))
+            force = force + jnp.where(near_a[a] & near_b[b], part, 0.0)
+    record = jnp.zeros((8, COLS), jnp.float32)
+    target = jnp.full((8, COLS), -1.0, jnp.float32)
     for a in (-1, 0, 1):
         for b in (-1, 0, 1):
-            force = jnp.zeros((8, COLS), jnp.float32)
-            for e in (-1, 0, 1):
-                for g in (-1, 0, 1):
-                    block = (1 - e) * 3 + 1 - g
-                    force = force + device_lanes(a + e, b + g, block * SLOTS)
-            if a == 0 and b == 0:
-                own_force = force
-            record = device_lanes(a, b, STATE_LANE)
-            target = device_lanes(a, b, DEST_LANE)[0:1, :]
-            mass = record[6:7, :] * (3.0 / (4.0 * math.pi * RADIUS * RADIUS * RADIUS))
-            spin = mass * record[7:8, :] * (1.0 / (RADIUS * RADIUS))
-            gain = jnp.where(sub < 3, force * mass, jnp.where(sub < 6, force * spin, 0.0))
-            updated = record + gain
-            for j in range(SLOTS):
-                wanted = meta[0:1, :] + float(j)
-                picked[j] = picked[j] + jnp.where(own_lanes & (target == wanted), updated, 0.0)
+            n = 3 * (a + 1) + b + 1
+            record = jnp.where(number == n, device_lanes(a, b, SLOTS * n - STATE_LANE), record)
+            target = jnp.where(number == n, device_lanes(a, b, SLOTS * n - DEST_LANE), target)
+    mass = record[6:7, :] * (3.0 / (4.0 * math.pi * RADIUS * RADIUS * RADIUS))
+    spin = mass * record[7:8, :] * (1.0 / (RADIUS * RADIUS))
+    gain = jnp.where(sub < 3, force * mass, jnp.where(sub < 6, force * spin, 0.0))
+    updated = record + gain
+    picked = [
+        jnp.where(listed & (target[0:1, :] == meta[0:1, :] + float(j)), updated, 0.0)
+        for j in range(SLOTS)
+    ]
     result = jnp.zeros((8, COLS), jnp.float32)
     for j in range(SLOTS):
         result = jnp.where(lane == j, jnp.sum(picked[j], axis=1, keepdims=True), result)
     turn[0:8, :] = result
-    turn[8:16, :] = own_force
+    turn[8:16, :] = force
     turned = turn[...].T
     state_next[...] = turned[0:SLOTS, 0:8]
-    forces[...] = turned[0:SLOTS, 8:14]
+    forces[...] = turned[4 * SLOTS : 5 * SLOTS, 8:14]
     send(state_next, state_hbm)
     send(forces, forces_hbm)
     for copy in copies:
@@ -726,7 +730,7 @@
             pltpu.VMEM((19, GROUPS, 8, COLS), jnp.float32),
             pltpu.VMEM((N_COEF, 8, COLS), jnp.float32),
             pltpu.VMEM((COLS, COLS), jnp.float32),
-            pltpu.VMEM((20, 6, 8, COLS), jnp.float32),
+            pltpu.VMEM((20, 8, COLS), jnp.float32),
             pltpu.SemaphoreType.DMA((10,)),
         ],
         compiler_params=pltpu.CompilerParams(vmem_limit_bytes=32 * 1024 * 1024),

time: 25.9 us -> 25.6 us (0.988)
  waiting for transfers between devices: 3.85 us -> 4.73 us
  starting transfers between devices: 15 us -> 14.3 us
  Pallas kernels: 6.33 us -> 5.96 us
    ppermute x4, starting transfers between devices: 8.86 us -> 7.51 us  [swapped(): return lax.ppermute(block, 'gy', route)]
    ppermute x2, waiting for transfers between devices: 1.48 us -> 2.25 us  [spread(): return lax.ppermute(block, ('gy', 'gz'), route)]
    ppermute x2, starting transfers between devices: 6.14 us -> 6.76 us  [spread(): return lax.ppermute(block, ('gy', 'gz'), route)]
    pallas_call x1, Pallas kernels: 3.63 us -> 3.28 us  [on_device(): pl.pallas_call(collide_kernel, out_shape=(f32(19, GROUPS, 8, COLS), f32(G...]
  transfers between devices with their start and end apart: 6 -> 6, of which waited for: 4 -> 5; matrix products, arithmetic and copies ran while one was open for 0% -> 0% of each run, Pallas kernels for 6% -> 6%
where the time goes in v5:
time: 25.6 us; the launch traced here: 25.7 us
  starting transfers between devices  14.3 us (56%)
  Pallas kernels  5.96 us (23%)
  waiting for transfers between devices  4.73 us (18%)
  between operations  0.67 us (3%)
    ppermute x4, starting transfers between devices, swapped(): return lax.ppermute(block, 'gy', route)  7.51 us
    ppermute x2, starting transfers between devices, spread(): return lax.ppermute(block, ('gy', 'gz'), route)  6.76 us
    pallas_call x1, Pallas kernels, on_device(): pl.pallas_call(collide_kernel, out_shape=(f32(19, GROUPS, 8, COLS), f32(G...  3.28 us
    ppermute x4, waiting for transfers between devices, swapped(): return lax.ppermute(block, 'gy', route)  2.48 us
    ppermute x2, waiting for transfers between devices, spread(): return lax.ppermute(block, ('gy', 'gz'), route)  2.25 us
    pallas_call x1, Pallas kernels, on_device(): pl.pallas_call(stream_kernel, out_shape=(f32(19, PLANES, ROWS, COLS), f32...  1.55 us
    pallas_call x1, Pallas kernels, on_device(): pl.pallas_call(update_kernel, out_shape=(f32(19, PLANES, ROWS, COLS), f32...  1.13 us
  transfers between devices with their start and end apart: 6, of which 5 were waited for; matrix products, arithmetic and copies ran while one was open for 0% of the time, Pallas kernels for 6%

profile of v5, /device:TPU:1, one launch (start us, length us, event | category | flops | bytes accessed | tf_op | source)
XLA Modules:
  0.0 25.7 jit_solution(14707408081513502852)
XLA Ops:
  0.6 3.3 %collide.1 = (f32[19,16,8,128]{3,2,1,0:T(8,128)S(1)}, f32[16,8,128]{2,1,0:T(8,128)S(1)}, f32[8,128]{1,0:T(8,128)S(1)}, f32[8,128]{1,0:T(8,128)S(1)}, f32[8,128]{...) custom-call(f32[19,16,8,128]{3,2,1,0:T(8,128)} %bitcast.11, ...), custom_call_target="tpu_custom_call" | custom-call | tf_op jit(solution)/shard_map/collide/pallas_call | solution.py:707
  3.9 1.3 %collective-permute-start = (f32[40,128]{1,0:T(8,128)S(1)}, f32[40,128]{1,0:T(8,128)S(1)}, u32[]{:S(2)}, u32[]{:S(2)}) collective-permute-start(f32[40,128]{1,0:T(8,128)S(1)} %pad_maximum_fusion), channel_id=1, source_target_pairs={{0,16},{16,0},{32,48},{48,32},{64,80},{80,64},{96,112},{112,96},{1... | collective-permute-start | bytes 61448 | tf_op jit(solution)/shard_map/ppermute | solution.py:694
  5.2 0.8 %collective-permute-done = f32[40,128]{1,0:T(8,128)S(1)} collective-permute-done((f32[40,128]{1,0:T(8,128)S(1)}, f32[40,128]{1,0:T(8,128)S(1)}, u32[]{:S(2)}, u32[]{:S(2)}) %collective-permute-start) | collective-permute-done | bytes 20512 | tf_op jit(solution)/shard_map/ppermute | solution.py:694
  6.1 6.2 %collective-permute-start.2 = (f32[8,128]{1,0:T(8,128)S(1)}, f32[8,128]{1,0:T(8,128)S(1)}, u32[]{:S(2)}, u32[]{:S(2)}) collective-permute-start(f32[8,128]{1,0:T(8,128)S(1)} %get-tuple-element.32.chip), channel_id=1, source_target_pairs={{0,2},{1,3},{2,4},{3,5},{4,6},{5,7},{6,8},{7,9},{8,10},{9,11},{10,... | collective-permute-start | bytes 12296 | tf_op jit(solution)/shard_map/ppermute | solution.py:703
  12.3 0.6 %collective-permute-start.1 = (f32[24,128]{1,0:T(8,128)S(1)}, f32[24,128]{1,0:T(8,128)S(1)}, u32[]{:S(2)}, u32[]{:S(2)}) collective-permute-start(f32[24,128]{1,0:T(8,128)S(1)} %pad_maximum_fusion.3), channel_id=1, source_target_pairs={{0,1},{1,2},{2,3},{3,4},{4,5},{5,6},{6,7},{7,8},{8,9},{9,10},{10,1... | collective-permute-start | bytes 36872 | tf_op jit(solution)/shard_map/ppermute | solution.py:703
  12.8 0.2 collective-permute-done.2.near_2
  13.0 2.1 %collective-permute-done.1.near_in = f32[24,128]{1,0:T(8,128)S(1)} collective-permute-done((f32[24,128]{1,0:T(8,128)S(1)}, f32[24,128]{1,0:T(8,128)S(1)}, u32[]{:S(2)}, u32[]{:S(2)}) %collective-permute-start.1) | collective-permute-done | bytes 12320 | tf_op jit(solution)/shard_map/ppermute | solution.py:703
  15.1 1.8 %collective-permute-start.3 = (f32[32,128]{1,0:T(8,128)S(1)}, f32[32,128]{1,0:T(8,128)S(1)}, u32[]{:S(2)}, u32[]{:S(2)}) collective-permute-start(f32[32,128]{1,0:T(8,128)S(1)} %pad_maximum_fusion.2), channel_id=1, source_target_pairs={{0,16},{16,0},{32,48},{48,32},{64,80},{80,64},{96,112},{112,96},{1... | collective-permute-start | bytes 49160 | tf_op jit(solution)/shard_map/ppermute | solution.py:694
  16.9 0.8 %collective-permute-done.3.far_in = f32[32,128]{1,0:T(8,128)S(1)} collective-permute-done((f32[32,128]{1,0:T(8,128)S(1)}, f32[32,128]{1,0:T(8,128)S(1)}, u32[]{:S(2)}, u32[]{:S(2)}) %collective-permute-start.3) | collective-permute-done | bytes 16416 | tf_op jit(solution)/shard_map/ppermute | solution.py:694
  17.8 2.3 %collective-permute-start.4 = (f32[80,128]{1,0:T(8,128)S(1)}, f32[80,128]{1,0:T(8,128)S(1)}, u32[]{:S(2)}, u32[]{:S(2)}) collective-permute-start(f32[80,128]{1,0:T(8,128)S(1)} %get-tuple-element.34), channel_id=1, source_target_pairs={{0,112},{16,32},{32,16},{48,64},{64,48},{80,96},{96,80},{112,0},{1... | collective-permute-start | bytes 122888 | tf_op jit(solution)/shard_map/ppermute | solution.py:694
  20.1 2.1 %collective-permute-start.5 = (f32[40,128]{1,0:T(8,128)S(1)}, f32[40,128]{1,0:T(8,128)S(1)}, u32[]{:S(2)}, u32[]{:S(2)}) collective-permute-start(f32[40,128]{1,0:T(8,128)S(1)} %pad_maximum_fusion.1), channel_id=1, source_target_pairs={{0,48},{16,96},{32,80},{48,0},{64,112},{80,32},{96,16},{112,64},{1... | collective-permute-start | bytes 61448 | tf_op jit(solution)/shard_map/ppermute | solution.py:694
  22.2 1.5 %stream.1 = (f32[19,4,32,128]{3,2,1,0:T(8,128)}, f32[10,4,8,128]{3,2,1,0:T(8,128)S(1)}) custom-call(f32[19,4,32,128]{3,2,1,0:T(8,128)S(1)} %bitcast.8, f32[4,32,128]{2,1,0:T(8,128)S(1)} %bitcast.9, f32[16,128]{1,0:T(8,128)S(1)} %get-tuple-element.19.border, f32[8,128]{1,0:T(8,128)S(1)} %get-tuple-element.20.meta, ...), custom_call_target="tpu_custom_call" | custom-call | flops 4000000 | bytes 4000000 | tf_op jit(solution)/shard_map/stream/pallas_call | solution.py:756
  23.7 0.8 %collective-permute-done.5.inner_in = f32[40,128]{1,0:T(8,128)S(1)} collective-permute-done((f32[40,128]{1,0:T(8,128)S(1)}, f32[40,128]{1,0:T(8,128)S(1)}, u32[]{:S(2)}, u32[]{:S(2)}) %collective-permute-start.5) | collective-permute-done | bytes 20512 | tf_op jit(solution)/shard_map/ppermute | solution.py:694
  24.5 0.0 collective-permute-done.4.outer_in
  24.5 1.1 %update.1 = (f32[19,4,32,128]{3,2,1,0:T(8,128)}, f32[4,6]{1,0:T(4,128)}, f32[4,8]{1,0:T(4,128)}) custom-call(f32[19,4,32,128]{3,2,1,0:T(8,128)} %get-tuple-element.25.streamed, f32[10,4,8,128]{3,2,1,0:T(8,128)S(1)} %get-tuple-element.26.y_part, f32[4,32,128]{2,1,0:T(8,128)S(1)} %bitcast.10, ...), custom_call_target="tpu_custom_call", output_to_operand_aliasing={{0}: (0, {})} | custom-call | tf_op jit(solution)/shard_map/update/pallas_call | solution.py:771
  (13 shorter events, 0.0 us)
Async XLA Ops:
  3.9 2.1 %collective-permute-start = (f32[40,128]{1,0:T(8,128)S(1)}, f32[40,128]{1,0:T(8,128)S(1)}, u32[]{:S(2)}, u32[]{:S(2)}) collective-permute-start(f32[40,128]{1,0:T(8,128)S(1)} %pad_maximum_fusion), channel_id=1, source_target_pairs={{0,16},{16,0},{32,48},{48,32},{64,80},{80,64},{96,112},{112,96},{1... | collective-permute-start | bytes 61448 | tf_op jit(solution)/shard_map/ppermute | solution.py:694
  6.1 6.9 %collective-permute-start.2 = (f32[8,128]{1,0:T(8,128)S(1)}, f32[8,128]{1,0:T(8,128)S(1)}, u32[]{:S(2)}, u32[]{:S(2)}) collective-permute-start(f32[8,128]{1,0:T(8,128)S(1)} %get-tuple-element.32.chip), channel_id=1, source_target_pairs={{0,2},{1,3},{2,4},{3,5},{4,6},{5,7},{6,8},{7,9},{8,10},{9,11},{10,... | collective-permute-start | bytes 12296 | tf_op jit(solution)/shard_map/ppermute | solution.py:703
  12.3 2.8 %collective-permute-start.1 = (f32[24,128]{1,0:T(8,128)S(1)}, f32[24,128]{1,0:T(8,128)S(1)}, u32[]{:S(2)}, u32[]{:S(2)}) collective-permute-start(f32[24,128]{1,0:T(8,128)S(1)} %pad_maximum_fusion.3), channel_id=1, source_target_pairs={{0,1},{1,2},{2,3},{3,4},{4,5},{5,6},{6,7},{7,8},{8,9},{9,10},{10,1... | collective-permute-start | bytes 36872 | tf_op jit(solution)/shard_map/ppermute | solution.py:703
  15.1 2.7 %collective-permute-start.3 = (f32[32,128]{1,0:T(8,128)S(1)}, f32[32,128]{1,0:T(8,128)S(1)}, u32[]{:S(2)}, u32[]{:S(2)}) collective-permute-start(f32[32,128]{1,0:T(8,128)S(1)} %pad_maximum_fusion.2), channel_id=1, source_target_pairs={{0,16},{16,0},{32,48},{48,32},{64,80},{80,64},{96,112},{112,96},{1... | collective-permute-start | bytes 49160 | tf_op jit(solution)/shard_map/ppermute | solution.py:694
  17.8 6.8 %collective-permute-start.4 = (f32[80,128]{1,0:T(8,128)S(1)}, f32[80,128]{1,0:T(8,128)S(1)}, u32[]{:S(2)}, u32[]{:S(2)}) collective-permute-start(f32[80,128]{1,0:T(8,128)S(1)} %get-tuple-element.34), channel_id=1, source_target_pairs={{0,112},{16,32},{32,16},{48,64},{64,48},{80,96},{96,80},{112,0},{1... | collective-permute-start | bytes 122888 | tf_op jit(solution)/shard_map/ppermute | solution.py:694
  20.1 4.4 %collective-permute-start.5 = (f32[40,128]{1,0:T(8,128)S(1)}, f32[40,128]{1,0:T(8,128)S(1)}, u32[]{:S(2)}, u32[]{:S(2)}) collective-permute-start(f32[40,128]{1,0:T(8,128)S(1)} %pad_maximum_fusion.1), channel_id=1, source_target_pairs={{0,48},{16,96},{32,80},{48,0},{64,112},{80,32},{96,16},{112,64},{1... | collective-permute-start | bytes 61448 | tf_op jit(solution)/shard_map/ppermute | solution.py:694

commit v6 on v5

--- a/solution.py
+++ b/solution.py
@@ -746,8 +746,9 @@
     )
     partner = swapped(jnp.concatenate([give, info, inner]), 1)
     chip = info + partner[8:16]
-    near_2 = spread(chip, 2)
-    near = spread(jnp.concatenate([keep, partner[0:8], chip]), 1)
+    load = jnp.concatenate([keep, partner[0:8], chip])
+    near = spread(load, 1)
+    near_2 = spread(load, 2)[16:24]
     far = swapped(jnp.concatenate([near, near_2]), 1)
     spheres = [chip, near[16:24], near_2, far[16:32]]
     from_outer = swapped(jnp.concatenate([outer, near[0:8], far[8:16]] + spheres), -1)

time: 25.6 us -> 24.6 us (0.961); the launches traced: 25.7 us -> 24.3 us
  starting transfers between devices: 14.3 us -> 11.6 us
  waiting for transfers between devices: 4.73 us -> 6.09 us
    ppermute x4, starting transfers between devices: 7.51 us -> 5.74 us  [swapped(): return lax.ppermute(block, 'gy', route)]
    ppermute x2, waiting for transfers between devices: 2.25 us -> 3.51 us  [spread(): return lax.ppermute(block, ('gy', 'gz'), route)]
    ppermute x2, starting transfers between devices: 6.76 us -> 5.82 us  [spread(): return lax.ppermute(block, ('gy', 'gz'), route)]
  transfers between devices with their start and end apart: 6 -> 6, of which waited for: 5 -> 4; matrix products, arithmetic and copies ran while one was open for 0% -> 0% of each run, Pallas kernels for 6% -> 6%
where the time goes in v6:
time: 24.6 us; the launch traced here: 24.3 us
  starting transfers between devices  11.6 us (47%)
  waiting for transfers between devices  6.09 us (25%)
  Pallas kernels  5.88 us (24%)
  between operations  0.7 us (3%)
    ppermute x2, starting transfers between devices, spread(): return lax.ppermute(block, ('gy', 'gz'), route)  5.82 us
    ppermute x4, starting transfers between devices, swapped(): return lax.ppermute(block, 'gy', route)  5.74 us
    ppermute x2, waiting for transfers between devices, spread(): return lax.ppermute(block, ('gy', 'gz'), route)  3.51 us
    pallas_call x1, Pallas kernels, on_device(): pl.pallas_call(collide_kernel, out_shape=(f32(19, GROUPS, 8, COLS), f32(G...  3.19 us
    ppermute x4, waiting for transfers between devices, swapped(): return lax.ppermute(block, 'gy', route)  2.58 us
    pallas_call x1, Pallas kernels, on_device(): pl.pallas_call(stream_kernel, out_shape=(f32(19, PLANES, ROWS, COLS), f32...  1.55 us
    pallas_call x1, Pallas kernels, on_device(): pl.pallas_call(update_kernel, out_shape=(f32(19, PLANES, ROWS, COLS), f32...  1.13 us
  transfers between devices with their start and end apart: 6, of which 4 were waited for; matrix products, arithmetic and copies ran while one was open for 0% of the time, Pallas kernels for 6%

profile of v6, /device:TPU:1, one launch (start us, length us, event | category | flops | bytes accessed | tf_op | source)
XLA Modules:
  0.0 24.3 jit_solution(2637734466958920031)
XLA Ops:
  0.6 3.2 %collide.1 = (f32[19,16,8,128]{3,2,1,0:T(8,128)S(1)}, f32[16,8,128]{2,1,0:T(8,128)S(1)}, f32[8,128]{1,0:T(8,128)S(1)}, f32[8,128]{1,0:T(8,128)S(1)}, f32[8,128]{...) custom-call(f32[19,16,8,128]{3,2,1,0:T(8,128)} %bitcast.11, ...), custom_call_target="tpu_custom_call" | custom-call | tf_op jit(solution)/shard_map/collide/pallas_call | solution.py:707
  3.8 1.6 %collective-permute-start = (f32[40,128]{1,0:T(8,128)S(1)}, f32[40,128]{1,0:T(8,128)S(1)}, u32[]{:S(2)}, u32[]{:S(2)}) collective-permute-start(f32[40,128]{1,0:T(8,128)S(1)} %pad_maximum_fusion), channel_id=1, source_target_pairs={{0,16},{16,0},{32,48},{48,32},{64,80},{80,64},{96,112},{112,96},{1... | collective-permute-start | bytes 61448 | tf_op jit(solution)/shard_map/ppermute | solution.py:694
  5.4 0.8 %collective-permute-done = f32[40,128]{1,0:T(8,128)S(1)} collective-permute-done((f32[40,128]{1,0:T(8,128)S(1)}, f32[40,128]{1,0:T(8,128)S(1)}, u32[]{:S(2)}, u32[]{:S(2)}) %collective-permute-start) | collective-permute-done | bytes 20512 | tf_op jit(solution)/shard_map/ppermute | solution.py:694
  6.3 5.3 %collective-permute-start.1 = (f32[24,128]{1,0:T(8,128)S(1)}, f32[24,128]{1,0:T(8,128)S(1)}, u32[]{:S(2)}, u32[]{:S(2)}) collective-permute-start(f32[24,128]{1,0:T(8,128)S(1)} %pad_maximum_fusion.3), channel_id=1, source_target_pairs={{0,1},{1,2},{2,3},{3,4},{4,5},{5,6},{6,7},{7,8},{8,9},{9,10},{10,1... | collective-permute-start | bytes 36872 | tf_op jit(solution)/shard_map/ppermute | solution.py:703
  11.6 0.5 %collective-permute-start.2 = (f32[24,128]{1,0:T(8,128)S(1)}, f32[24,128]{1,0:T(8,128)S(1)}, u32[]{:S(2)}, u32[]{:S(2)}) collective-permute-start(f32[24,128]{1,0:T(8,128)S(1)} %pad_maximum_fusion.3), channel_id=1, source_target_pairs={{0,2},{1,3},{2,4},{3,5},{4,6},{5,7},{6,8},{7,9},{8,10},{9,11},{10,... | collective-permute-start | bytes 36872 | tf_op jit(solution)/shard_map/ppermute | solution.py:703
  12.1 3.5 %collective-permute-done.2 = f32[24,128]{1,0:T(8,128)S(1)} collective-permute-done((f32[24,128]{1,0:T(8,128)S(1)}, f32[24,128]{1,0:T(8,128)S(1)}, u32[]{:S(2)}, u32[]{:S(2)}) %collective-permute-start.2) | collective-permute-done | bytes 12320 | tf_op jit(solution)/shard_map/ppermute | solution.py:703
  15.6 0.0 collective-permute-done.1.near_in
  15.6 0.1 collective-permute-start.3
  15.7 1.2 %collective-permute-done.3.far_in = f32[32,128]{1,0:T(8,128)S(1)} collective-permute-done((f32[32,128]{1,0:T(8,128)S(1)}, f32[32,128]{1,0:T(8,128)S(1)}, u32[]{:S(2)}, u32[]{:S(2)}) %collective-permute-start.3) | collective-permute-done | bytes 16416 | tf_op jit(solution)/shard_map/ppermute | solution.py:694
  16.9 1.8 %collective-permute-start.4 = (f32[80,128]{1,0:T(8,128)S(1)}, f32[80,128]{1,0:T(8,128)S(1)}, u32[]{:S(2)}, u32[]{:S(2)}) collective-permute-start(f32[80,128]{1,0:T(8,128)S(1)} %get-tuple-element.34), channel_id=1, source_target_pairs={{0,112},{16,32},{32,16},{48,64},{64,48},{80,96},{96,80},{112,0},{1... | collective-permute-start | bytes 122888 | tf_op jit(solution)/shard_map/ppermute | solution.py:694
  18.7 2.3 %collective-permute-start.5 = (f32[40,128]{1,0:T(8,128)S(1)}, f32[40,128]{1,0:T(8,128)S(1)}, u32[]{:S(2)}, u32[]{:S(2)}) collective-permute-start(f32[40,128]{1,0:T(8,128)S(1)} %pad_maximum_fusion.1), channel_id=1, source_target_pairs={{0,48},{16,96},{32,80},{48,0},{64,112},{80,32},{96,16},{112,64},{1... | collective-permute-start | bytes 61448 | tf_op jit(solution)/shard_map/ppermute | solution.py:694
  21.0 1.5 %stream.1 = (f32[19,4,32,128]{3,2,1,0:T(8,128)}, f32[10,4,8,128]{3,2,1,0:T(8,128)S(1)}) custom-call(f32[19,4,32,128]{3,2,1,0:T(8,128)S(1)} %bitcast.8, f32[4,32,128]{2,1,0:T(8,128)S(1)} %bitcast.9, f32[16,128]{1,0:T(8,128)S(1)} %get-tuple-element.19.border, f32[8,128]{1,0:T(8,128)S(1)} %get-tuple-element.20.meta, ...), custom_call_target="tpu_custom_call" | custom-call | flops 4000000 | bytes 4000000 | tf_op jit(solution)/shard_map/stream/pallas_call | solution.py:757
  22.5 0.6 %collective-permute-done.5.inner_in = f32[40,128]{1,0:T(8,128)S(1)} collective-permute-done((f32[40,128]{1,0:T(8,128)S(1)}, f32[40,128]{1,0:T(8,128)S(1)}, u32[]{:S(2)}, u32[]{:S(2)}) %collective-permute-start.5) | collective-permute-done | bytes 20512 | tf_op jit(solution)/shard_map/ppermute | solution.py:694
  23.1 0.0 collective-permute-done.4.outer_in
  23.1 1.1 %update.1 = (f32[19,4,32,128]{3,2,1,0:T(8,128)}, f32[4,6]{1,0:T(4,128)}, f32[4,8]{1,0:T(4,128)}) custom-call(f32[19,4,32,128]{3,2,1,0:T(8,128)} %get-tuple-element.25.streamed, f32[10,4,8,128]{3,2,1,0:T(8,128)S(1)} %get-tuple-element.26.y_part, f32[4,32,128]{2,1,0:T(8,128)S(1)} %bitcast.10, ...), custom_call_target="tpu_custom_call", output_to_operand_aliasing={{0}: (0, {})} | custom-call | tf_op jit(solution)/shard_map/update/pallas_call | solution.py:772
  (14 shorter events, 0.0 us)
Async XLA Ops:
  3.8 2.4 %collective-permute-start = (f32[40,128]{1,0:T(8,128)S(1)}, f32[40,128]{1,0:T(8,128)S(1)}, u32[]{:S(2)}, u32[]{:S(2)}) collective-permute-start(f32[40,128]{1,0:T(8,128)S(1)} %pad_maximum_fusion), channel_id=1, source_target_pairs={{0,16},{16,0},{32,48},{48,32},{64,80},{80,64},{96,112},{112,96},{1... | collective-permute-start | bytes 61448 | tf_op jit(solution)/shard_map/ppermute | solution.py:694
  6.3 9.3 %collective-permute-start.1 = (f32[24,128]{1,0:T(8,128)S(1)}, f32[24,128]{1,0:T(8,128)S(1)}, u32[]{:S(2)}, u32[]{:S(2)}) collective-permute-start(f32[24,128]{1,0:T(8,128)S(1)} %pad_maximum_fusion.3), channel_id=1, source_target_pairs={{0,1},{1,2},{2,3},{3,4},{4,5},{5,6},{6,7},{7,8},{8,9},{9,10},{10,1... | collective-permute-start | bytes 36872 | tf_op jit(solution)/shard_map/ppermute | solution.py:703
  11.6 4.0 %collective-permute-start.2 = (f32[24,128]{1,0:T(8,128)S(1)}, f32[24,128]{1,0:T(8,128)S(1)}, u32[]{:S(2)}, u32[]{:S(2)}) collective-permute-start(f32[24,128]{1,0:T(8,128)S(1)} %pad_maximum_fusion.3), channel_id=1, source_target_pairs={{0,2},{1,3},{2,4},{3,5},{4,6},{5,7},{6,8},{7,9},{8,10},{9,11},{10,... | collective-permute-start | bytes 36872 | tf_op jit(solution)/shard_map/ppermute | solution.py:703
  15.6 1.3 %collective-permute-start.3 = (f32[32,128]{1,0:T(8,128)S(1)}, f32[32,128]{1,0:T(8,128)S(1)}, u32[]{:S(2)}, u32[]{:S(2)}) collective-permute-start(f32[32,128]{1,0:T(8,128)S(1)} %pad_maximum_fusion.2), channel_id=1, source_target_pairs={{0,16},{16,0},{32,48},{48,32},{64,80},{80,64},{96,112},{112,96},{1... | collective-permute-start | bytes 49160 | tf_op jit(solution)/shard_map/ppermute | solution.py:694
  16.9 6.2 %collective-permute-start.4 = (f32[80,128]{1,0:T(8,128)S(1)}, f32[80,128]{1,0:T(8,128)S(1)}, u32[]{:S(2)}, u32[]{:S(2)}) collective-permute-start(f32[80,128]{1,0:T(8,128)S(1)} %get-tuple-element.34), channel_id=1, source_target_pairs={{0,112},{16,32},{32,16},{48,64},{64,48},{80,96},{96,80},{112,0},{1... | collective-permute-start | bytes 122888 | tf_op jit(solution)/shard_map/ppermute | solution.py:694
  18.7 4.4 %collective-permute-start.5 = (f32[40,128]{1,0:T(8,128)S(1)}, f32[40,128]{1,0:T(8,128)S(1)}, u32[]{:S(2)}, u32[]{:S(2)}) collective-permute-start(f32[40,128]{1,0:T(8,128)S(1)} %pad_maximum_fusion.1), channel_id=1, source_target_pairs={{0,48},{16,96},{32,80},{48,0},{64,112},{80,32},{96,16},{112,64},{1... | collective-permute-start | bytes 61448 | tf_op jit(solution)/shard_map/ppermute | solution.py:694

commit v7 on v6

--- a/solution.py
+++ b/solution.py
@@ -406,7 +406,7 @@
         return 0
 
     partial[SLOTS:] = jnp.zeros((16, 8, COLS), jnp.float32)
-    lax.fori_loop(0, SLOTS, own, 0)
+    lax.fori_loop(0, SLOTS, own, 0, unroll=True)
 
     def listed(r, _):
         @pl.when(lists[0, r] >= 0)
@@ -748,7 +748,7 @@
     chip = info + partner[8:16]
     load = jnp.concatenate([keep, partner[0:8], chip])
     near = spread(load, 1)
-    near_2 = spread(load, 2)[16:24]
+    near_2 = spread(load[8:24], 2)[8:16]
     far = swapped(jnp.concatenate([near, near_2]), 1)
     spheres = [chip, near[16:24], near_2, far[16:32]]
     from_outer = swapped(jnp.concatenate([outer, near[0:8], far[8:16]] + spheres), -1)

time: 24.6 us -> 24.5 us (level)
  waiting for transfers between devices: 6.09 us -> 5.44 us
  starting transfers between devices: 11.6 us -> 12.2 us
    ppermute x4, starting transfers between devices: 5.74 us -> 6.5 us  [swapped(): return lax.ppermute(block, 'gy', route)]
    ppermute x4, waiting for transfers between devices: 2.58 us -> 2.01 us  [swapped(): return lax.ppermute(block, 'gy', route)]
where the time goes in v7:
time: 24.5 us; the launch traced here: 24.2 us
  starting transfers between devices  12.2 us (50%)
  Pallas kernels  5.85 us (24%)
  waiting for transfers between devices  5.44 us (22%)
  between operations  0.68 us (3%)
    ppermute x4, starting transfers between devices, swapped(): return lax.ppermute(block, 'gy', route)  6.5 us
    ppermute x2, starting transfers between devices, spread(): return lax.ppermute(block, ('gy', 'gz'), route)  5.71 us
    ppermute x2, waiting for transfers between devices, spread(): return lax.ppermute(block, ('gy', 'gz'), route)  3.44 us
    pallas_call x1, Pallas kernels, on_device(): pl.pallas_call(collide_kernel, out_shape=(f32(19, GROUPS, 8, COLS), f32(G...  3.17 us
    ppermute x4, waiting for transfers between devices, swapped(): return lax.ppermute(block, 'gy', route)  2.01 us
    pallas_call x1, Pallas kernels, on_device(): pl.pallas_call(stream_kernel, out_shape=(f32(19, PLANES, ROWS, COLS), f32...  1.55 us
    pallas_call x1, Pallas kernels, on_device(): pl.pallas_call(update_kernel, out_shape=(f32(19, PLANES, ROWS, COLS), f32...  1.13 us
  transfers between devices with their start and end apart: 6, of which 4 were waited for; matrix products, arithmetic and copies ran while one was open for 0% of the time, Pallas kernels for 6%

profile of v7, /device:TPU:1, one launch (start us, length us, event | category | flops | bytes accessed | tf_op | source)
XLA Modules:
  0.0 24.2 jit_solution(17968311276742877353)
XLA Ops:
  0.6 3.2 %collide.1 = (f32[19,16,8,128]{3,2,1,0:T(8,128)S(1)}, f32[16,8,128]{2,1,0:T(8,128)S(1)}, f32[8,128]{1,0:T(8,128)S(1)}, f32[8,128]{1,0:T(8,128)S(1)}, f32[8,128]{...) custom-call(f32[19,16,8,128]{3,2,1,0:T(8,128)} %bitcast.11, ...), custom_call_target="tpu_custom_call" | custom-call | tf_op jit(solution)/shard_map/collide/pallas_call | solution.py:707
  3.8 1.5 %collective-permute-start = (f32[40,128]{1,0:T(8,128)S(1)}, f32[40,128]{1,0:T(8,128)S(1)}, u32[]{:S(2)}, u32[]{:S(2)}) collective-permute-start(f32[40,128]{1,0:T(8,128)S(1)} %pad_maximum_fusion), channel_id=1, source_target_pairs={{0,16},{16,0},{32,48},{48,32},{64,80},{80,64},{96,112},{112,96},{1... | collective-permute-start | bytes 61448 | tf_op jit(solution)/shard_map/ppermute | solution.py:694
  5.3 0.8 %collective-permute-done = f32[40,128]{1,0:T(8,128)S(1)} collective-permute-done((f32[40,128]{1,0:T(8,128)S(1)}, f32[40,128]{1,0:T(8,128)S(1)}, u32[]{:S(2)}, u32[]{:S(2)}) %collective-permute-start) | collective-permute-done | bytes 20512 | tf_op jit(solution)/shard_map/ppermute | solution.py:694
  6.1 5.1 %collective-permute-start.1 = (f32[24,128]{1,0:T(8,128)S(1)}, f32[24,128]{1,0:T(8,128)S(1)}, u32[]{:S(2)}, u32[]{:S(2)}) collective-permute-start(f32[24,128]{1,0:T(8,128)S(1)} %pad_maximum_fusion.3), channel_id=1, source_target_pairs={{0,1},{1,2},{2,3},{3,4},{4,5},{5,6},{6,7},{7,8},{8,9},{9,10},{10,1... | collective-permute-start | bytes 36872 | tf_op jit(solution)/shard_map/ppermute | solution.py:703
  11.3 0.6 %collective-permute-start.2 = (f32[16,128]{1,0:T(8,128)S(1)}, f32[16,128]{1,0:T(8,128)S(1)}, u32[]{:S(2)}, u32[]{:S(2)}) collective-permute-start(f32[16,128]{1,0:T(8,128)S(1)} %pad_maximum_fusion.4), channel_id=1, source_target_pairs={{0,2},{1,3},{2,4},{3,5},{4,6},{5,7},{6,8},{7,9},{8,10},{9,11},{10,... | collective-permute-start | bytes 24584 | tf_op jit(solution)/shard_map/ppermute | solution.py:703
  11.9 3.4 %collective-permute-done.2 = f32[16,128]{1,0:T(8,128)S(1)} collective-permute-done((f32[16,128]{1,0:T(8,128)S(1)}, f32[16,128]{1,0:T(8,128)S(1)}, u32[]{:S(2)}, u32[]{:S(2)}) %collective-permute-start.2) | collective-permute-done | bytes 8224 | tf_op jit(solution)/shard_map/ppermute | solution.py:703
  15.3 0.0 collective-permute-done.1.near_in
  15.3 0.5 %collective-permute-start.3 = (f32[32,128]{1,0:T(8,128)S(1)}, f32[32,128]{1,0:T(8,128)S(1)}, u32[]{:S(2)}, u32[]{:S(2)}) collective-permute-start(f32[32,128]{1,0:T(8,128)S(1)} %pad_maximum_fusion.2), channel_id=1, source_target_pairs={{0,16},{16,0},{32,48},{48,32},{64,80},{80,64},{96,112},{112,96},{1... | collective-permute-start | bytes 49160 | tf_op jit(solution)/shard_map/ppermute | solution.py:694
  15.8 0.8 %collective-permute-done.3.far_in = f32[32,128]{1,0:T(8,128)S(1)} collective-permute-done((f32[32,128]{1,0:T(8,128)S(1)}, f32[32,128]{1,0:T(8,128)S(1)}, u32[]{:S(2)}, u32[]{:S(2)}) %collective-permute-start.3) | collective-permute-done | bytes 16416 | tf_op jit(solution)/shard_map/ppermute | solution.py:694
  16.6 2.0 %collective-permute-start.4 = (f32[80,128]{1,0:T(8,128)S(1)}, f32[80,128]{1,0:T(8,128)S(1)}, u32[]{:S(2)}, u32[]{:S(2)}) collective-permute-start(f32[80,128]{1,0:T(8,128)S(1)} %get-tuple-element.34), channel_id=1, source_target_pairs={{0,112},{16,32},{32,16},{48,64},{64,48},{80,96},{96,80},{112,0},{1... | collective-permute-start | bytes 122888 | tf_op jit(solution)/shard_map/ppermute | solution.py:694
  18.7 2.5 %collective-permute-start.5 = (f32[40,128]{1,0:T(8,128)S(1)}, f32[40,128]{1,0:T(8,128)S(1)}, u32[]{:S(2)}, u32[]{:S(2)}) collective-permute-start(f32[40,128]{1,0:T(8,128)S(1)} %pad_maximum_fusion.1), channel_id=1, source_target_pairs={{0,48},{16,96},{32,80},{48,0},{64,112},{80,32},{96,16},{112,64},{1... | collective-permute-start | bytes 61448 | tf_op jit(solution)/shard_map/ppermute | solution.py:694
  21.2 1.5 %stream.1 = (f32[19,4,32,128]{3,2,1,0:T(8,128)}, f32[10,4,8,128]{3,2,1,0:T(8,128)S(1)}) custom-call(f32[19,4,32,128]{3,2,1,0:T(8,128)S(1)} %bitcast.8, f32[4,32,128]{2,1,0:T(8,128)S(1)} %bitcast.9, f32[16,128]{1,0:T(8,128)S(1)} %get-tuple-element.19.border, f32[8,128]{1,0:T(8,128)S(1)} %get-tuple-element.20.meta, ...), custom_call_target="tpu_custom_call" | custom-call | flops 4000000 | bytes 4000000 | tf_op jit(solution)/shard_map/stream/pallas_call | solution.py:757
  22.8 0.3 %collective-permute-done.5.inner_in = f32[40,128]{1,0:T(8,128)S(1)} collective-permute-done((f32[40,128]{1,0:T(8,128)S(1)}, f32[40,128]{1,0:T(8,128)S(1)}, u32[]{:S(2)}, u32[]{:S(2)}) %collective-permute-start.5) | collective-permute-done | bytes 20512 | tf_op jit(solution)/shard_map/ppermute | solution.py:694
  23.1 0.0 collective-permute-done.4.outer_in
  23.1 1.1 %update.1 = (f32[19,4,32,128]{3,2,1,0:T(8,128)}, f32[4,6]{1,0:T(4,128)}, f32[4,8]{1,0:T(4,128)}) custom-call(f32[19,4,32,128]{3,2,1,0:T(8,128)} %get-tuple-element.25.streamed, f32[10,4,8,128]{3,2,1,0:T(8,128)S(1)} %get-tuple-element.26.y_part, f32[4,32,128]{2,1,0:T(8,128)S(1)} %bitcast.10, ...), custom_call_target="tpu_custom_call", output_to_operand_aliasing={{0}: (0, {})} | custom-call | tf_op jit(solution)/shard_map/update/pallas_call | solution.py:772
  (15 shorter events, 0.0 us)
Async XLA Ops:
  3.8 2.3 %collective-permute-start = (f32[40,128]{1,0:T(8,128)S(1)}, f32[40,128]{1,0:T(8,128)S(1)}, u32[]{:S(2)}, u32[]{:S(2)}) collective-permute-start(f32[40,128]{1,0:T(8,128)S(1)} %pad_maximum_fusion), channel_id=1, source_target_pairs={{0,16},{16,0},{32,48},{48,32},{64,80},{80,64},{96,112},{112,96},{1... | collective-permute-start | bytes 61448 | tf_op jit(solution)/shard_map/ppermute | solution.py:694
  6.1 9.2 %collective-permute-start.1 = (f32[24,128]{1,0:T(8,128)S(1)}, f32[24,128]{1,0:T(8,128)S(1)}, u32[]{:S(2)}, u32[]{:S(2)}) collective-permute-start(f32[24,128]{1,0:T(8,128)S(1)} %pad_maximum_fusion.3), channel_id=1, source_target_pairs={{0,1},{1,2},{2,3},{3,4},{4,5},{5,6},{6,7},{7,8},{8,9},{9,10},{10,1... | collective-permute-start | bytes 36872 | tf_op jit(solution)/shard_map/ppermute | solution.py:703
  11.3 4.0 %collective-permute-start.2 = (f32[16,128]{1,0:T(8,128)S(1)}, f32[16,128]{1,0:T(8,128)S(1)}, u32[]{:S(2)}, u32[]{:S(2)}) collective-permute-start(f32[16,128]{1,0:T(8,128)S(1)} %pad_maximum_fusion.4), channel_id=1, source_target_pairs={{0,2},{1,3},{2,4},{3,5},{4,6},{5,7},{6,8},{7,9},{8,10},{9,11},{10,... | collective-permute-start | bytes 24584 | tf_op jit(solution)/shard_map/ppermute | solution.py:703
  15.3 1.3 %collective-permute-start.3 = (f32[32,128]{1,0:T(8,128)S(1)}, f32[32,128]{1,0:T(8,128)S(1)}, u32[]{:S(2)}, u32[]{:S(2)}) collective-permute-start(f32[32,128]{1,0:T(8,128)S(1)} %pad_maximum_fusion.2), channel_id=1, source_target_pairs={{0,16},{16,0},{32,48},{48,32},{64,80},{80,64},{96,112},{112,96},{1... | collective-permute-start | bytes 49160 | tf_op jit(solution)/shard_map/ppermute | solution.py:694
  16.6 6.5 %collective-permute-start.4 = (f32[80,128]{1,0:T(8,128)S(1)}, f32[80,128]{1,0:T(8,128)S(1)}, u32[]{:S(2)}, u32[]{:S(2)}) collective-permute-start(f32[80,128]{1,0:T(8,128)S(1)} %get-tuple-element.34), channel_id=1, source_target_pairs={{0,112},{16,32},{32,16},{48,64},{64,48},{80,96},{96,80},{112,0},{1... | collective-permute-start | bytes 122888 | tf_op jit(solution)/shard_map/ppermute | solution.py:694
  18.7 4.4 %collective-permute-start.5 = (f32[40,128]{1,0:T(8,128)S(1)}, f32[40,128]{1,0:T(8,128)S(1)}, u32[]{:S(2)}, u32[]{:S(2)}) collective-permute-start(f32[40,128]{1,0:T(8,128)S(1)} %pad_maximum_fusion.1), channel_id=1, source_target_pairs={{0,48},{16,96},{32,80},{48,0},{64,112},{80,32},{96,16},{112,64},{1... | collective-permute-start | bytes 61448 | tf_op jit(solution)/shard_map/ppermute | solution.py:694
